TPU v7x, 32 devices: a whole 2x2x4 slice. The times are simulated.
32 devices in a mesh: dp: 4 (over x, core), tm: 4 (over z), rows: 2 (over y).
Axes of the slice: x: 2, y: 2, z: 4, core: 2. Of those that a mesh axis runs over, the one named last changes fastest.
Arguments:
- latents: bfloat16 [4, 8, 2, 30, 512], P('dp', 'tm', 'rows'), may hold values from -6 to 6
- grad_out: bfloat16 [4, 8, 4, 60, 256], P('dp', 'tm', 'rows'), may hold values from -6 to 6
- kernel: bfloat16 [3, 3, 3, 512, 256], replicated, may hold values from -0.0546875 to 0.0546875
Outputs:
- grad_latents: bfloat16 [4, 8, 2, 30, 512], P('dp', 'tm', 'rows')
- weight_grad: float32 [512, 3, 3, 3, 256], P(('dp', 'tm', 'rows'))
All inputs are finite; a program needn't handle non-finite values.
Results may differ from a plain program's by a relative error of at most 0.001.
Values may be sent and summed in bfloat16 or wider, within the bound.
No kernel may reach another device: no remote copies, remote signals or barrier semaphores. Data moves between devices by JAX's collectives and lax.ppermute only.
A program may use at most 128 MiB of HBM per device.

v0:
```python
import jax
import jax.numpy as jnp
from jax import lax
from jax.sharding import PartitionSpec as P


def from_behind(shard, axis, by):
    peers = lax.axis_size(axis)
    pairs = [(i, i + by) for i in range(peers) if 0 <= i + by < peers]
    return lax.ppermute(shard, axis, pairs)


def with_halo(block, sides, width):
    for axis, dim in sides:
        count = lax.axis_size(axis)
        forward = [(i, i + 1) for i in range(count - 1)]
        backward = [(target, source) for source, target in forward]
        low = lax.ppermute(
            lax.slice_in_dim(block, block.shape[dim] - width, None, axis=dim), axis, forward
        )
        high = lax.ppermute(lax.slice_in_dim(block, 0, width, axis=dim), axis, backward)
        block = jnp.concatenate([low, block, high], axis=dim)
    return block


def tap_terms(source, grad_flat, frames, height, width):
    taps = []
    for a in range(3):
        for i in range(3):
            for j in range(3):
                window = source[a : a + frames, i : i + height, j : j + width]
                flat = window.reshape(frames * height * width, window.shape[3])
                taps.append(
                    lax.dot_general(
                        flat,
                        grad_flat,
                        (((0,), (0,)), ((), ())),
                        preferred_element_type=jnp.float32,
                    )
                )
    return jnp.stack(taps, axis=1)


def body(latents, grad_out, kernel):
    frames = grad_out.shape[1]
    height = grad_out.shape[2]
    width = grad_out.shape[3]
    channels = latents.shape[4]
    outputs = grad_out.shape[4]
    devices = lax.axis_size("dp") * lax.axis_size("tm") * lax.axis_size("rows")
    factor = float(devices * frames * height * width) ** (-0.5)
    earlier = from_behind(latents, "tm", 1)
    with_earlier = jnp.concatenate([earlier, latents], axis=1)
    grad_ext = with_halo(grad_out, (("rows", 2),), 1)
    later = from_behind(grad_ext, "tm", -1)
    grad_all = jnp.concatenate([grad_ext, later], axis=1)[0]
    grad_all = jnp.pad(grad_all, ((0, 0), (0, 0), (1, 1), (0, 0)))
    grad_up = jnp.zeros((frames, height, width, channels), jnp.float32)
    for a in range(3):
        for i in range(3):
            for j in range(3):
                window = grad_all[
                    2 - a : 2 - a + frames, 2 - i : 2 - i + height, 2 - j : 2 - j + width
                ]
                grad_up = grad_up + lax.dot_general(
                    window,
                    kernel[a, i, j],
                    (((3,), (1,)), ((), ())),
                    preferred_element_type=jnp.float32,
                )
    pooled = grad_up.reshape(frames, height // 2, 2, width // 2, 2, channels).sum(axis=(2, 4))
    grad_latents = pooled.astype(jnp.bfloat16)[None]
    slab_count = lax.axis_size("rows")
    groups = lax.axis_size("dp") * lax.axis_size("tm")
    share = channels // devices
    lead = with_earlier.shape[:4]
    regrouped = with_earlier.reshape(lead + (groups, slab_count, share))
    regrouped = jnp.swapaxes(regrouped, 4, 5).reshape(lead + (channels,))
    owned = lax.all_to_all(regrouped, "rows", split_axis=4, concat_axis=2, tiled=True)[0]
    source = jnp.repeat(jnp.repeat(owned, 2, axis=1), 2, axis=2)
    source = jnp.pad(source, ((0, 0), (1, 1), (1, 1), (0, 0)))
    grad_whole = lax.all_gather(grad_out, "rows", axis=2, tiled=True)[0]
    whole_height = grad_whole.shape[1]
    grad_flat = grad_whole.reshape(frames * whole_height * width, outputs)
    term = tap_terms(source, grad_flat, frames, whole_height, width) * factor
    term = term.reshape(source.shape[3], 3, 3, 3, outputs)
    weight_grad = lax.psum_scatter(term, ("dp", "tm"), scatter_dimension=0, tiled=True)
    return (grad_latents, weight_grad)


def solution(mesh):
    in_specs = (P("dp", "tm", "rows", None, None), P("dp", "tm", "rows", None, None), P())
    out_specs = (P("dp", "tm", "rows", None, None), P(("dp", "tm", "rows"), None, None, None, None))
    return jax.shard_map(body, mesh=mesh, in_specs=in_specs, out_specs=out_specs, check_vma=False)
```

profile of v0, /device:TPU:0, one launch (start us, length us, event | category | flops | bytes accessed | tf_op | source)
XLA Modules:
  0.0 179.5 jit_solution(13845496387164521734)
XLA Ops:
  7.2 4.9 %collective-permute-start.3 = (bf16[1,2,1,30,512]{4,1,3,2,0:T(2,128)(2,1)}, bf16[1,2,1,30,512]{4,1,3,2,0:T(2,128)(2,1)S(1)}, u32[]{:S(2)}, u32[]{:S(2)}) collective-permute-start(bf16[1,2,1,30,512]{4,1,3,2,0:T(2,128)(2,1)} %param.3), channel_id=1, source_target_pairs={{0,2},{2,4},{4,6},{1,3},{3,5},{5,7},{8,10},{10,12},{12,14},{9,11},... | collective-permute-start | bytes 184328 | tf_op jit(solution)/shard_map/ppermute | solution.py:10
  12.1 1.0 copy.58
  13.1 1.2 collective-permute-done.3
  14.3 1.0 pad_maximum_fusion
  16.0 1.6 reshape.186
  17.6 3.4 %all-to-all-start = ((bf16[2,2,15360]{2,1,0:T(2,128)(2,1)}), bf16[2,2,15360]{2,1,0:T(2,128)(2,1)S(1)}, u32[]{:S(2)}, u32[]{:S(2)}) async-start(bf16[2,2,15360]{2,1,0:T(2,128)(2,1)} %reshape.186), calls=%async_computation | async-start | bytes 245760 | tf_op jit(solution)/shard_map/all_to_all | solution.py:79
  21.1 5.7 %all_gather.3 = bf16[1,2,4,60,256]{4,1,3,0,2:T(2,128)(2,1)S(1)} all-gather(bf16[1,2,2,60,256]{4,1,3,0,2:T(2,128)(2,1)S(1)} %copy.58), channel_id=1, replica_groups=mesh['dp'=4,'tm'=4,'rows'=2] {'rows'}, dimensions={2}, use_global_device_ids=true | all-gather | bytes 368640 | tf_op jit(solution)/shard_map/all_gather | solution.py:82
  26.8 1.4 reshape.187
  29.0 1.1 pad_slice_fusion.1
  30.1 4.0 %pad_slice_fusion = (bf16[2,4,60,256]{3,1,2,0:T(4,128)(2,1)S(1)}, bf16[2,4,60,256]{3,1,2,0:T(4,128)(2,1)}, bf16[2,4,60,256]{3,1,2,0:T(4,128)(2,1)S(1)}, bf16[2,4...) fusion(bf16[4,4,60,256]{3,1,2,0:T(4,128)(2,1)S(1)} %bitcast.397), kind=kLoop, calls=%fused_computation | loop fusion | bytes 5160960 | tf_op jit(solution)/shard_map/slice | solution.py:31
  34.5 1.0 copy.57
  35.6 1.0 copy.60
  36.7 1.0 copy.62
  38.8 1.0 copy.65
  39.9 1.0 copy.66
  41.6 1.0 copy.67
  43.3 1.0 copy.68
  45.0 1.0 copy.69
  46.0 0.8 reshape.142
  46.8 1.0 copy.70
  48.5 1.0 copy.71
  50.2 0.8 copy.72
  51.2 0.8 reshape.145
  52.0 1.0 copy.73
  52.9 0.8 reshape.146
  53.7 1.0 copy.74
  54.7 0.7 reshape.147
  55.4 1.0 copy.75
  57.1 1.0 copy.76
  58.9 1.0 copy.77
  60.6 1.0 copy.78
  62.3 1.0 copy.79
  65.0 0.8 reshape.154
  67.4 0.8 reshape.157
  68.2 0.8 reshape.158
  76.9 3.5 %broadcast_multiply_fusion = f32[256,27,256]{2,0,1:T(8,128)} fusion(f32[256,27,256]{2,0,1:T(8,128)S(1)} %fusion.18), kind=kLoop, calls=%fused_computation.24 | loop fusion | flops 1769472 | bytes 14155776 | tf_op jit(solution)/shard_map/mul | solution.py:85
  80.4 0.9 copy-done
  81.4 4.0 %collective-permute-start = (bf16[1,2,1,60,256]{4,3,2,1,0:T(8,128)(2,1)S(1)}, bf16[1,2,1,60,256]{4,3,2,1,0:T(8,128)(2,1)S(1)}, u32[]{:S(2)}, u32[]{:S(2)}) collective-permute-start(bf16[1,2,1,60,256]{4,3,2,1,0:T(8,128)(2,1)S(1)} %copy.116), channel_id=1, source_target_pairs={{0,1},{2,3},{4,5},{6,7},{8,9},{10,11},{12,13},{14,15},{16,17},{18,... | collective-permute-start | bytes 184328 | tf_op jit(solution)/shard_map/ppermute | solution.py:18
  85.4 1.3 collective-permute-start.1
  87.3 4.3 %collective-permute-done.1 = bf16[1,2,1,60,256]{4,3,2,1,0:T(8,128)(2,1)S(1)} collective-permute-done((bf16[1,2,1,60,256]{4,3,2,1,0:T(8,128)(2,1)S(1)}, bf16[1,2,1,60,256]{4,3,2,1,0:T(8,128)(2,1)S(1)}, u32[]{:S(2)}, u32[]{:S(2)}) %collective-permute-start.1) | collective-permute-done | bytes 61472 | tf_op jit(solution)/shard_map/ppermute | solution.py:21
  91.6 1.5 collective-permute-start.2
  93.1 7.0 %collective-permute-done.2 = bf16[1,2,4,60,256]{4,3,2,1,0:T(8,128)(2,1)S(1)} collective-permute-done((bf16[1,2,4,60,256]{4,3,2,1,0:T(8,128)(2,1)S(1)}, bf16[1,2,4,60,256]{4,3,2,1,0:T(8,128)(2,1)S(1)}, u32[]{:S(2)}, u32[]{:S(2)}) %collective-permute-start.2) | collective-permute-done | bytes 245792 | tf_op jit(solution)/shard_map/ppermute | solution.py:10
  100.2 1.2 fusion.83
  101.4 1.3 fusion.85
  102.7 1.2 fusion.88
  103.9 1.2 fusion.78
  111.5 0.8 reduce_sum.18
  112.3 60.4 %reduce-scatter.2.cloned.1.call-done = f32[16,3,3,3,256]{4,0,3,2,1:T(8,128)} async-done(((f32[256,3,3,3,256]{4,0,3,2,1:T(8,128)}), f32[16,3,3,3,256]{4,0,3,2,1:T(8,128)}) %reduce-scatter.2.cloned.1.call-update) | async-done | bytes 442384 | tf_op jit(solution)/shard_map/reduce_scatter | solution.py:87
  (154 shorter events, 27.9 us)
Async XLA Ops:
  7.2 7.1 %collective-permute-start.3 = (bf16[1,2,1,30,512]{4,1,3,2,0:T(2,128)(2,1)}, bf16[1,2,1,30,512]{4,1,3,2,0:T(2,128)(2,1)S(1)}, u32[]{:S(2)}, u32[]{:S(2)}) collective-permute-start(bf16[1,2,1,30,512]{4,1,3,2,0:T(2,128)(2,1)} %param.3), channel_id=1, source_target_pairs={{0,2},{2,4},{4,6},{1,3},{3,5},{5,7},{8,10},{10,12},{12,14},{9,11},... | collective-permute-start | bytes 184328 | tf_op jit(solution)/shard_map/ppermute | solution.py:10
  17.6 9.2 %all-to-all-start = ((bf16[2,2,15360]{2,1,0:T(2,128)(2,1)}), bf16[2,2,15360]{2,1,0:T(2,128)(2,1)S(1)}, u32[]{:S(2)}, u32[]{:S(2)}) async-start(bf16[2,2,15360]{2,1,0:T(2,128)(2,1)} %reshape.186), calls=%async_computation | async-start | bytes 245760 | tf_op jit(solution)/shard_map/all_to_all | solution.py:79
  21.0 151.7 %reduce-scatter.2.cloned.1.call-start = ((), (), s32[]{:S(2)}) async-start(), calls=%async_computation.2 | async-start | bytes 7520256 | tf_op jit(solution)/shard_map/reduce_scatter | solution.py:87
  64.0 6.9 %copy-start.1 = (bf16[480,256]{1,0:T(8,128)(2,1)S(1)}, bf16[480,256]{1,0:T(8,128)(2,1)}, u32[]{:S(2)}) copy-start(bf16[480,256]{1,0:T(8,128)(2,1)} %reshape.139) | copy-start | bytes 737284
  65.8 5.5 %copy-start.2 = (bf16[480,256]{1,0:T(8,128)(2,1)S(1)}, bf16[480,256]{1,0:T(8,128)(2,1)}, u32[]{:S(2)}) copy-start(bf16[480,256]{1,0:T(8,128)(2,1)} %reshape.140) | copy-start | bytes 737284
  66.6 5.0 %copy-start.3 = (bf16[480,256]{1,0:T(8,128)(2,1)S(1)}, bf16[480,256]{1,0:T(8,128)(2,1)}, u32[]{:S(2)}) copy-start(bf16[480,256]{1,0:T(8,128)(2,1)} %reshape.141) | copy-start | bytes 737284
  67.3 4.5 %copy-start.4 = (bf16[480,256]{1,0:T(8,128)(2,1)S(1)}, bf16[480,256]{1,0:T(8,128)(2,1)}, u32[]{:S(2)}) copy-start(bf16[480,256]{1,0:T(8,128)(2,1)} %reshape.142) | copy-start | bytes 737284
  68.1 4.0 %copy-start.5 = (bf16[480,256]{1,0:T(8,128)(2,1)S(1)}, bf16[480,256]{1,0:T(8,128)(2,1)}, u32[]{:S(2)}) copy-start(bf16[480,256]{1,0:T(8,128)(2,1)} %reshape.143) | copy-start | bytes 737284
  68.9 3.5 %copy-start.6 = (bf16[480,256]{1,0:T(8,128)(2,1)S(1)}, bf16[480,256]{1,0:T(8,128)(2,1)}, u32[]{:S(2)}) copy-start(bf16[480,256]{1,0:T(8,128)(2,1)} %reshape.144) | copy-start | bytes 737284
  68.9 3.8 %copy-start.7 = (bf16[480,256]{1,0:T(8,128)(2,1)S(1)}, bf16[480,256]{1,0:T(8,128)(2,1)}, u32[]{:S(2)}) copy-start(bf16[480,256]{1,0:T(8,128)(2,1)} %reshape.145) | copy-start | bytes 737284
  68.9 4.1 %copy-start.8 = (bf16[480,256]{1,0:T(8,128)(2,1)S(1)}, bf16[480,256]{1,0:T(8,128)(2,1)}, u32[]{:S(2)}) copy-start(bf16[480,256]{1,0:T(8,128)(2,1)} %reshape.146) | copy-start | bytes 737284
  68.9 4.4 %copy-start.9 = (bf16[480,256]{1,0:T(8,128)(2,1)S(1)}, bf16[480,256]{1,0:T(8,128)(2,1)}, u32[]{:S(2)}) copy-start(bf16[480,256]{1,0:T(8,128)(2,1)} %reshape.147) | copy-start | bytes 737284
  68.9 4.7 %copy-start.10 = (bf16[480,256]{1,0:T(8,128)(2,1)S(1)}, bf16[480,256]{1,0:T(8,128)(2,1)}, u32[]{:S(2)}) copy-start(bf16[480,256]{1,0:T(8,128)(2,1)} %reshape.148) | copy-start | bytes 737284
  68.9 5.0 %copy-start.11 = (bf16[480,256]{1,0:T(8,128)(2,1)S(1)}, bf16[480,256]{1,0:T(8,128)(2,1)}, u32[]{:S(2)}) copy-start(bf16[480,256]{1,0:T(8,128)(2,1)} %reshape.149) | copy-start | bytes 737284
  68.9 5.3 %copy-start.12 = (bf16[480,256]{1,0:T(8,128)(2,1)S(1)}, bf16[480,256]{1,0:T(8,128)(2,1)}, u32[]{:S(2)}) copy-start(bf16[480,256]{1,0:T(8,128)(2,1)} %reshape.150) | copy-start | bytes 737284
  69.0 5.6 %copy-start.13 = (bf16[480,256]{1,0:T(8,128)(2,1)S(1)}, bf16[480,256]{1,0:T(8,128)(2,1)}, u32[]{:S(2)}) copy-start(bf16[480,256]{1,0:T(8,128)(2,1)} %reshape.151) | copy-start | bytes 737284
  69.2 5.6 %copy-start.14 = (bf16[480,256]{1,0:T(8,128)(2,1)S(1)}, bf16[480,256]{1,0:T(8,128)(2,1)}, u32[]{:S(2)}) copy-start(bf16[480,256]{1,0:T(8,128)(2,1)} %reshape.152) | copy-start | bytes 737284
  69.5 5.6 %copy-start.15 = (bf16[480,256]{1,0:T(8,128)(2,1)S(1)}, bf16[480,256]{1,0:T(8,128)(2,1)}, u32[]{:S(2)}) copy-start(bf16[480,256]{1,0:T(8,128)(2,1)} %reshape.153) | copy-start | bytes 737284
  69.8 5.6 %copy-start.16 = (bf16[480,256]{1,0:T(8,128)(2,1)S(1)}, bf16[480,256]{1,0:T(8,128)(2,1)}, u32[]{:S(2)}) copy-start(bf16[480,256]{1,0:T(8,128)(2,1)} %reshape.154) | copy-start | bytes 737284
  70.1 5.6 %copy-start.17 = (bf16[480,256]{1,0:T(8,128)(2,1)S(1)}, bf16[480,256]{1,0:T(8,128)(2,1)}, u32[]{:S(2)}) copy-start(bf16[480,256]{1,0:T(8,128)(2,1)} %reshape.155) | copy-start | bytes 737284
  70.4 5.6 %copy-start.18 = (bf16[480,256]{1,0:T(8,128)(2,1)S(1)}, bf16[480,256]{1,0:T(8,128)(2,1)}, u32[]{:S(2)}) copy-start(bf16[480,256]{1,0:T(8,128)(2,1)} %reshape.156) | copy-start | bytes 737284
  70.7 5.6 %copy-start.19 = (bf16[480,256]{1,0:T(8,128)(2,1)S(1)}, bf16[480,256]{1,0:T(8,128)(2,1)}, u32[]{:S(2)}) copy-start(bf16[480,256]{1,0:T(8,128)(2,1)} %reshape.157) | copy-start | bytes 737284
  71.0 5.6 %copy-start.20 = (bf16[480,256]{1,0:T(8,128)(2,1)S(1)}, bf16[480,256]{1,0:T(8,128)(2,1)}, u32[]{:S(2)}) copy-start(bf16[480,256]{1,0:T(8,128)(2,1)} %reshape.158) | copy-start | bytes 737284
  80.3 0.9 copy-start
  80.3 24.8 %slice-start = ((s8[7077888]{0:T(1024)(128)(4,1)}), s8[2883584]{0:T(1024)(128)(4,1)S(1)}, s32[]{:S(2)}) async-start(s8[7077888]{0:T(1024)(128)(4,1)} %bitcast.392), calls=%async_computation.3 | async-start | bytes 5767168
  81.2 23.9 %slice-start.1 = ((s8[7077888]{0:T(1024)(128)(4,1)}), s8[4194304]{0:T(1024)(128)(4,1)S(1)}, s32[]{:S(2)}) async-start(s8[7077888]{0:T(1024)(128)(4,1)} %bitcast.392), calls=%async_computation.4 | async-start | bytes 8388608
  81.4 5.9 %collective-permute-start = (bf16[1,2,1,60,256]{4,3,2,1,0:T(8,128)(2,1)S(1)}, bf16[1,2,1,60,256]{4,3,2,1,0:T(8,128)(2,1)S(1)}, u32[]{:S(2)}, u32[]{:S(2)}) collective-permute-start(bf16[1,2,1,60,256]{4,3,2,1,0:T(8,128)(2,1)S(1)} %copy.116), channel_id=1, source_target_pairs={{0,1},{2,3},{4,5},{6,7},{8,9},{10,11},{12,13},{14,15},{16,17},{18,... | collective-permute-start | bytes 184328 | tf_op jit(solution)/shard_map/ppermute | solution.py:18
  85.4 6.2 %collective-permute-start.1 = (bf16[1,2,1,60,256]{4,3,2,1,0:T(8,128)(2,1)S(1)}, bf16[1,2,1,60,256]{4,3,2,1,0:T(8,128)(2,1)S(1)}, u32[]{:S(2)}, u32[]{:S(2)}) collective-permute-start(bf16[1,2,1,60,256]{4,3,2,1,0:T(8,128)(2,1)S(1)} %copy.117), channel_id=1, source_target_pairs={{1,0},{3,2},{5,4},{7,6},{9,8},{11,10},{13,12},{15,14},{17,16},{19,... | collective-permute-start | bytes 184328 | tf_op jit(solution)/shard_map/ppermute | solution.py:21
  91.6 8.5 %collective-permute-start.2 = (bf16[1,2,4,60,256]{4,3,2,1,0:T(8,128)(2,1)S(1)}, bf16[1,2,4,60,256]{4,3,2,1,0:T(8,128)(2,1)S(1)}, u32[]{:S(2)}, u32[]{:S(2)}) collective-permute-start(bf16[1,2,4,60,256]{4,3,2,1,0:T(8,128)(2,1)S(1)} %constant_dynamic-update-slice_fusion), channel_id=1, source_target_pairs={{2,0},{4,2},{6,4},{3,1},{5,3},{7,5},{10,8},{12,10},{14,12},{11,9},... | collective-permute-start | bytes 737288 | tf_op jit(solution)/shard_map/ppermute | solution.py:10
Sparse Core Ops, SparseCore 0:
  80.5 92.1 reduce-scatter.1
where the time goes:
time: 181 us; the launch traced here: 180 us
  waiting for transfers between devices  73.4 us (41%)
  local copies, waits for them, and re-layouts  46.6 us (26%)
  matrix products  18.3 us (10%)
  starting transfers between devices  15.1 us (8%)
  between operations  15.1 us (8%)
  blocking collectives  5.68 us (3%)
  other arithmetic  5.28 us (3%)
    reduce_scatter x1, waiting for transfers between devices, body(): lax.psum_scatter(term, ('dp', 'tm'), scatter_dimension=0, tiled=True)  60.4 us
    slice x30, local copies, waits for them, and re-layouts, tap_terms(): window = source[a:a + frames, i:i + height, j:j + width]  23.5 us
    reshape x27, local copies, waits for them, and re-layouts, tap_terms(): flat = window.reshape(frames * height * width, window.shape[3])  15.3 us
    dot_general x27, matrix products, body(): lax.dot_general(window, kernel[a, i, j], (((3,), (1,)), ((), ())), prefer...  10.9 us
    ppermute x2, waiting for transfers between devices, from_behind(): return lax.ppermute(shard, axis, pairs)  8.14 us
    dot_general x27, matrix products, tap_terms(): lax.dot_general(flat, grad_flat, (((0,), (0,)), ((), ())), preferred_elem...  7.43 us
    ppermute x2, starting transfers between devices, from_behind(): return lax.ppermute(shard, axis, pairs)  6.43 us
    all_gather x1, blocking collectives, body(): grad_whole = lax.all_gather(grad_out, 'rows', axis=2, tiled=True)[0]  5.68 us
  transfers between devices with their start and end apart: 6, of which 5 were waited for; matrix products, arithmetic and copies ran while one was open for 7% of the time, Pallas kernels for 0%

commit v1 on v0

--- a/solution.py
+++ b/solution.py
@@ -1,7 +1,252 @@
+import functools
+
 import jax
 import jax.numpy as jnp
 from jax import lax
+from jax.experimental import pallas as pl
+from jax.experimental.pallas import tpu as pltpu
 from jax.sharding import PartitionSpec as P
+
+VMEM_LIMIT = 40 * 1024 * 1024
+SLOTS = (1, 3, 0, 2)
+
+
+def cycle(size, by):
+    return [(i, (i + by) % size) for i in range(size)]
+
+
+def whole(count):
+    return [pl.BlockSpec(memory_space=pltpu.VMEM)] * count
+
+
+def params():
+    return pltpu.CompilerParams(vmem_limit_bytes=VMEM_LIMIT)
+
+
+def select_kernel(tm, share, lat_ref, own_ref, other_ref):
+    channels = lat_ref.shape[1]
+    width = channels // 2
+    me_dp, me_tm, me_rows = lax.axis_index("dp"), lax.axis_index("tm"), lax.axis_index("rows")
+    col = lax.broadcasted_iota(jnp.int32, (1, width), 1)
+    inner = col % share
+    place = (col // share) % 4
+    shift = col // (4 * share)
+    slot = jnp.where(place == 0, SLOTS[0], jnp.where(place == 1, SLOTS[1], jnp.where(place == 2, SLOTS[2], SLOTS[3])))
+    dp = jnp.bitwise_xor(slot, me_dp)
+    frame = (shift + me_tm) % tm
+    row = lax.broadcasted_iota(jnp.int32, (channels, width), 0)
+    for ref, rows in ((own_ref, me_rows), (other_ref, 1 - me_rows)):
+        wanted = ((dp * tm + frame) * 2 + rows) * share + inner
+        pick = jnp.where(row == wanted, 1.0, 0.0).astype(jnp.bfloat16)
+        ref[...] = jnp.dot(lat_ref[...], pick, preferred_element_type=jnp.float32).astype(jnp.bfloat16)
+
+
+def pair_kernel(tm, own_ref, other_ref, *outs):
+    width = own_ref.shape[1] // tm
+    for k in range(tm):
+        cols = slice(k * width, (k + 1) * width)
+        outs[k][...] = jnp.concatenate([own_ref[:, cols], other_ref[:, cols]], axis=1)
+
+
+def windows_kernel(tm, share, *refs):
+    pieces, out_ref, lat_ref, pick_ref = refs[:tm], refs[tm], refs[tm + 1], refs[tm + 2]
+    group = 4 * share
+    me_tm, me_rows = lax.axis_index("tm"), lax.axis_index("rows")
+    lat_ref[...] = jnp.zeros_like(lat_ref)
+    for k in range(tm):
+        t = lax.rem(me_tm + tm - k, tm)
+        block = pieces[k][...].astype(jnp.float32)
+        lat_ref[t, me_rows, 0:60, :] = block[:, :group]
+        lat_ref[t, 1 - me_rows, 0:60, :] = block[:, group:]
+    kappa = lax.broadcasted_iota(jnp.int32, (128, 128), 0)
+    rho = lax.broadcasted_iota(jnp.int32, (1, 128), 1)
+    w, h = rho // 2, rho % 2
+    for f in range(2):
+        for ij in range(9):
+            i, j = ij // 3, ij % 3
+            for s in range(2):
+                r = (2 * s + h + 1 + i) // 2 - 1
+                q = (w + 1 + j) // 2 - 1
+                ok = (r >= 0) & (r < 2) & (q >= 0) & (q < 30) & (rho < 120)
+                target = jnp.where(ok, r * 64 + q * 2 + f, -1)
+                pick = jnp.where(kappa == target, 1.0, 0.0).astype(jnp.bfloat16)
+                base = (f * 9 + ij) * 256 + s * 128
+                pick_ref[:, base : base + 128] = pick
+    stacked = jnp.concatenate(
+        [jnp.transpose(lat_ref[t].reshape(128, group)) for t in range(tm)], axis=0
+    ).astype(jnp.bfloat16)
+    out_ref[0:2] = jnp.zeros((2,) + out_ref.shape[1:], jnp.bfloat16)
+    for f in range(2):
+        for ij in range(9):
+            base = (f * 9 + ij) * 256
+            wide = jnp.dot(stacked, pick_ref[:, base : base + 256], preferred_element_type=jnp.float32)
+            wide = wide.astype(jnp.bfloat16)
+            for t in range(tm):
+                for p in range(4):
+                    src = t * group + p * share
+                    dst = p * 9 * share + ij * share
+                    out_ref[2 * t + f + 2, dst : dst + share, :] = wide[src : src + share]
+
+
+def gather_kernel(tm, *refs):
+    blocks, out_ref = refs[: 2 * tm], refs[2 * tm]
+    me_tm, me_rows = lax.axis_index("tm"), lax.axis_index("rows")
+    out_ref[:, :, 112:128, :] = jnp.zeros(out_ref.shape[:2] + (16, out_ref.shape[3]), jnp.bfloat16)
+    for k in range(tm):
+        t = lax.rem(me_tm + tm - k, tm)
+        for f in range(2):
+            out_ref[2 * t + f, me_rows, 0:120, :] = blocks[2 * k][f]
+            out_ref[2 * t + f, 1 - me_rows, 0:120, :] = blocks[2 * k + 1][f]
+
+
+def terms_kernel(a, frames, win_ref, grad_ref, send_ref, keep_ref):
+    half = send_ref.shape[0]
+    for ref, start in ((send_ref, 0), (keep_ref, half)):
+        total = None
+        for f in range(frames):
+            g = grad_ref[f].reshape(256, grad_ref.shape[3])
+            term = jnp.dot(win_ref[f + a, start : start + half, :], g, preferred_element_type=jnp.float32)
+            total = term if total is None else total + term
+        ref[...] = total
+
+
+def latents_kernel(tm, own_ref, other_ref, next_ref, next_other_ref, kernel_ref, out_ref, wide_ref, pool_ref, total_ref):
+    step = pl.program_id(0)
+    outputs = own_ref.shape[2]
+
+    @pl.when(step == 0)
+    def _():
+        me_tm, me_rows = lax.axis_index("tm"), lax.axis_index("rows")
+        later = jnp.where(me_tm < tm - 1, 1.0, 0.0)
+        above = jnp.where(me_rows > 0, 1.0, 0.0)
+        lanes = outputs // 128
+        wide_ref[:, :, 120:128, :] = jnp.zeros((2, lanes, 8, 128), jnp.float32)
+
+        def every_fourth(source, first):
+            parts = [wide_ref[source, n, pl.ds(first, 32, stride=4), :] for n in range(lanes)]
+            return jnp.concatenate(parts, axis=1)
+
+        for f in range(4):
+            mine, theirs = (own_ref, other_ref) if f < 2 else (next_ref, next_other_ref)
+            for n in range(lanes):
+                wide_ref[0, n, 0:120, :] = mine[f % 2, :, 128 * n : 128 * n + 128].astype(jnp.float32)
+                wide_ref[1, n, 0:120, :] = theirs[f % 2, :, 128 * n : 128 * n + 128].astype(jnp.float32)
+            x = [[every_fourth(0, 2 * t + h) for t in range(2)] for h in range(2)]
+            up = [every_fourth(1, 2 * t + 1) * above for t in range(2)]
+            down = [every_fourth(1, 2 * t) * (1.0 - above) for t in range(2)]
+            sums = (
+                [x[1][t] + down[t] for t in range(2)],
+                [x[0][t] + x[1][t] for t in range(2)],
+                [up[t] + x[0][t] for t in range(2)],
+            )
+            for i in range(3):
+                even, odd = sums[i]
+                after = pltpu.roll(even, 31, 0)
+                before = pltpu.roll(odd, 1, 0)
+                for j, pooled in enumerate((odd + after, even + odd, before + even)):
+                    if f >= 2:
+                        pooled = pooled * later
+                    high = pooled.astype(jnp.bfloat16)
+                    low = (pooled - high.astype(jnp.float32)).astype(jnp.bfloat16)
+                    pool_ref[3 * i + j, 0, f] = high
+                    pool_ref[3 * i + j, 1, f] = low
+        total_ref[...] = jnp.zeros_like(total_ref)
+
+    total = total_ref[...]
+    for ij in range(9):
+        lhs = pool_ref[ij, :, pl.ds(2 - step, 2)].reshape(128, outputs)
+        total = total + lax.dot_general(
+            lhs, kernel_ref[ij], (((1,), (1,)), ((), ())), preferred_element_type=jnp.float32
+        )
+    total_ref[...] = total
+
+    @pl.when(step == 2)
+    def _():
+        for f in range(2):
+            sum_f = total[32 * f : 32 * f + 32] + total[64 + 32 * f : 96 + 32 * f]
+            out_ref[f] = sum_f[0:30].astype(jnp.bfloat16)
+
+
+def narrow_body(latents, grad_out, kernel):
+    tm = lax.axis_size("tm")
+    devices = lax.axis_size("dp") * tm * 2
+    channels = latents.shape[4]
+    outputs = grad_out.shape[4]
+    share = channels // devices
+    frames = 2 * tm
+    factor = float(devices * 240) ** (-0.5)
+    swap = [(0, 1), (1, 0)]
+
+    mine = jnp.transpose(grad_out[0], (0, 2, 1, 3)).reshape(2, 120, outputs)
+    shifted = [mine] + [lax.ppermute(mine, "tm", cycle(tm, k)) for k in range(1, tm)]
+    across = [lax.ppermute(block, "rows", swap) for block in shifted]
+
+    lat = jnp.transpose(latents[0, :, 0], (1, 0, 2)).reshape(60, channels)
+    half = jax.ShapeDtypeStruct((60, channels // 2), jnp.bfloat16)
+    own, other = pl.pallas_call(
+        functools.partial(select_kernel, tm, share),
+        out_shape=(half, half),
+        in_specs=whole(1),
+        out_specs=tuple(whole(2)),
+        compiler_params=params(),
+    )(lat)
+    other = lax.ppermute(other, "rows", swap)
+    pieces = pl.pallas_call(
+        functools.partial(pair_kernel, tm),
+        out_shape=tuple([jax.ShapeDtypeStruct((60, 8 * share), jnp.bfloat16)] * tm),
+        in_specs=whole(2),
+        out_specs=tuple(whole(tm)),
+        compiler_params=params(),
+    )(own, other)
+    pieces = [pieces[0]] + [lax.ppermute(pieces[k], "tm", cycle(tm, k)) for k in range(1, tm)]
+    windows = pl.pallas_call(
+        functools.partial(windows_kernel, tm, share),
+        out_shape=jax.ShapeDtypeStruct((frames + 2, 36 * share, 256), jnp.bfloat16),
+        in_specs=whole(tm),
+        out_specs=whole(1)[0],
+        scratch_shapes=[pltpu.VMEM((tm, 2, 64, 4 * share), jnp.float32), pltpu.VMEM((128, 18 * 256), jnp.bfloat16)],
+        compiler_params=params(),
+    )(*pieces)
+    grads = pl.pallas_call(
+        functools.partial(gather_kernel, tm),
+        out_shape=jax.ShapeDtypeStruct((frames, 2, 128, outputs), jnp.bfloat16),
+        in_specs=whole(2 * tm),
+        out_specs=whole(1)[0],
+        compiler_params=params(),
+    )(*[block for pair in zip(shifted, across) for block in pair])
+
+    rows = 18 * share
+    parts = []
+    for a in range(3):
+        send, keep = pl.pallas_call(
+            functools.partial(terms_kernel, a, frames),
+            out_shape=tuple([jax.ShapeDtypeStruct((rows, outputs), jnp.float32)] * 2),
+            in_specs=whole(2),
+            out_specs=tuple(whole(2)),
+            compiler_params=params(),
+        )(windows, grads)
+        both = keep + lax.ppermute(send, "dp", [(i, i ^ 1) for i in range(4)])
+        kept, sent = both[: rows // 2], both[rows // 2 :]
+        parts.append((kept + lax.ppermute(sent, "dp", [(i, i ^ 2) for i in range(4)])) * factor)
+    weight_grad = jnp.stack(parts).reshape(3, 3, 3, share, outputs)
+    weight_grad = jnp.transpose(weight_grad, (3, 0, 1, 2, 4))
+
+    taps = kernel.reshape(27, channels, outputs)
+    grad_latents = pl.pallas_call(
+        functools.partial(latents_kernel, tm),
+        grid=(3,),
+        out_shape=jax.ShapeDtypeStruct((2, 30, channels), jnp.bfloat16),
+        in_specs=[pl.BlockSpec((2, 120, outputs), lambda a: (0, 0, 0))] * 4
+        + [pl.BlockSpec((9, channels, outputs), lambda a: (a, 0, 0))],
+        out_specs=pl.BlockSpec((2, 30, channels), lambda a: (0, 0, 0)),
+        scratch_shapes=[
+            pltpu.VMEM((2, outputs // 128, 128, 128), jnp.float32),
+            pltpu.VMEM((9, 2, 4, 32, outputs), jnp.bfloat16),
+            pltpu.VMEM((128, channels), jnp.float32),
+        ],
+        compiler_params=params(),
+    )(shifted[0], across[0], shifted[tm - 1], across[tm - 1], taps)
+    return (grad_latents.reshape(latents.shape), weight_grad)
 
 
 def from_behind(shard, axis, by):
@@ -41,7 +286,7 @@
     return jnp.stack(taps, axis=1)
 
 
-def body(latents, grad_out, kernel):
+def wide_body(latents, grad_out, kernel):
     frames = grad_out.shape[1]
     height = grad_out.shape[2]
     width = grad_out.shape[3]
@@ -88,6 +333,12 @@
     return (grad_latents, weight_grad)
 
 
+def body(latents, grad_out, kernel):
+    share = latents.shape[4] // (lax.axis_size("dp") * lax.axis_size("tm") * lax.axis_size("rows"))
+    narrow = lax.axis_size("rows") == 2 and lax.axis_size("dp") == 4 and share % 16 == 0
+    return (narrow_body if narrow else wide_body)(latents, grad_out, kernel)
+
+
 def solution(mesh):
     in_specs = (P("dp", "tm", "rows", None, None), P("dp", "tm", "rows", None, None), P())
     out_specs = (P("dp", "tm", "rows", None, None), P(("dp", "tm", "rows"), None, None, None, None))

time: 181 us -> 58.2 us (0.32)
  waiting for transfers between devices: 73.4 us -> 29.3 us
  local copies, waits for them, and re-layouts: 46.6 us -> 2.55 us
  matrix products: 18.3 us -> 0 us
  between operations: 15.1 us -> 0.83 us
  Pallas kernels: 0 us -> 6.78 us
  blocking collectives: 5.68 us -> 0 us
  other arithmetic: 5.28 us -> 0.97 us
  starting transfers between devices: 15.1 us -> 17.6 us
    reduce_scatter x1 -> x0, waiting for transfers between devices: 60.4 us -> none  [body(): lax.psum_scatter(term, ('dp', 'tm'), scatter_dimension=0, tiled=True)]
    slice x31 -> x3, local copies, waits for them, and re-layouts: 23.7 us -> 0.03 us  [narrow_body(): kept, sent = (both[:rows // 2], both[rows // 2:])]
    dot_general x54 -> x0, matrix products: 18.3 us -> none  [the longest x27 10.9 us: body(): lax.dot_general(window, kernel[a, i, j], (((3,), (1,)), ((), ())), prefer...]
    ppermute x4 -> x17, waiting for transfers between devices: 13 us -> 29.3 us  [the longest x3 13.5 us: narrow_body(): lax.ppermute(pieces[k], 'tm', cycle(tm, k))]
    reshape x29 -> x2, local copies, waits for them, and re-layouts: 15.9 us -> 1.81 us  [the longest x1 0.95 us: narrow_body(): mine = jnp.transpose(grad_out[0], (0, 2, 1, 3)).reshape(2, 120, outputs)]
    pallas_call x0 -> x8, Pallas kernels: none -> 6.78 us  [the longest x1 3.1 us: narrow_body(): pl.pallas_call(functools.partial(latents_kernel, tm), grid=(3,), out_shap...]
    ppermute x4 -> x17, starting transfers between devices: 11.7 us -> 17.6 us  [the longest x3 6.11 us: narrow_body(): lax.ppermute(mine, 'tm', cycle(tm, k))]
    all_gather x1 -> x0, blocking collectives: 5.68 us -> none  [body(): grad_whole = lax.all_gather(grad_out, 'rows', axis=2, tiled=True)[0]]
  transfers between devices with their start and end apart: 6 -> 17, of which waited for: 5 -> 9; matrix products, arithmetic and copies ran while one was open for 7% -> 3% of each run, Pallas kernels for 0% -> 10%
where the time goes in v1:
time: 58.2 us; the launch traced here: 58 us
  waiting for transfers between devices  29.3 us (50%)
  starting transfers between devices  17.6 us (30%)
  Pallas kernels  6.78 us (12%)
  local copies, waits for them, and re-layouts  2.55 us (4%)
  other arithmetic  0.97 us (2%)
  between operations  0.83 us (1%)
    ppermute x3, waiting for transfers between devices, narrow_body(): lax.ppermute(pieces[k], 'tm', cycle(tm, k))  13.5 us
    ppermute x3, waiting for transfers between devices, narrow_body(): lax.ppermute(sent, 'dp', [(i, i ^ 2) for i in range(4)])  6.92 us
    ppermute x3, starting transfers between devices, narrow_body(): lax.ppermute(mine, 'tm', cycle(tm, k))  6.11 us
    ppermute x4, starting transfers between devices, narrow_body(): across = [lax.ppermute(block, 'rows', swap) for block in shifted]  6.08 us
    ppermute x3, waiting for transfers between devices, narrow_body(): lax.ppermute(mine, 'tm', cycle(tm, k))  5.37 us
    ppermute x3, starting transfers between devices, narrow_body(): lax.ppermute(sent, 'dp', [(i, i ^ 2) for i in range(4)])  3.71 us
    ppermute x1, waiting for transfers between devices, narrow_body(): other = lax.ppermute(other, 'rows', swap)  3.41 us
    pallas_call x1, Pallas kernels, narrow_body(): pl.pallas_call(functools.partial(latents_kernel, tm), grid=(3,), out_shap...  3.1 us
  transfers between devices with their start and end apart: 17, of which 9 were waited for; matrix products, arithmetic and copies ran while one was open for 3% of the time, Pallas kernels for 10%

profile of v1, /device:TPU:0, one launch (start us, length us, event | category | flops | bytes accessed | tf_op | source)
XLA Modules:
  0.0 58.0 jit_solution(12498920817231398307)
XLA Ops:
  0.6 1.0 %reshape.23.own_ref.refs_0_ = bf16[2,120,256]{2,1,0:T(8,128)(2,1)S(1)} reshape(bf16[2,60,2,256]{3,2,1,0:T(2,128)(2,1)} %bitcast.20) | data formatting | bytes 245760 | tf_op jit(solution)/shard_map/reshape | solution.py:180
  1.6 5.1 %collective-permute-start.1 = (bf16[2,120,256]{2,1,0:T(8,128)(2,1)S(1)}, bf16[2,120,256]{2,1,0:T(8,128)(2,1)S(1)}, u32[]{:S(2)}, u32[]{:S(2)}) collective-permute-start(bf16[2,120,256]{2,1,0:T(8,128)(2,1)S(1)} %reshape.23.own_ref.refs_0_), channel_id=1, source_target_pairs={{0,6},{2,0},{4,2},{6,4},{1,7},{3,1},{5,3},{7,5},{8,14},{10,8},{12,... | collective-permute-start | bytes 368648 | tf_op jit(solution)/shard_map/ppermute | solution.py:181
  6.7 0.0 collective-permute-start.7
  6.7 1.0 %collective-permute-start.9 = (bf16[2,120,256]{2,1,0:T(8,128)(2,1)S(1)}, bf16[2,120,256]{2,1,0:T(8,128)(2,1)S(1)}, u32[]{:S(2)}, u32[]{:S(2)}) collective-permute-start(bf16[2,120,256]{2,1,0:T(8,128)(2,1)S(1)} %reshape.23.own_ref.refs_0_), channel_id=1, source_target_pairs={{0,4},{2,6},{4,0},{6,2},{1,5},{3,7},{5,1},{7,3},{8,12},{10,14},{12... | collective-permute-start | bytes 368648 | tf_op jit(solution)/shard_map/ppermute | solution.py:181
  7.7 1.5 %collective-permute-start = (bf16[2,120,256]{2,1,0:T(8,128)(2,1)S(1)}, bf16[2,120,256]{2,1,0:T(8,128)(2,1)S(1)}, u32[]{:S(2)}, u32[]{:S(2)}) collective-permute-start(bf16[2,120,256]{2,1,0:T(8,128)(2,1)S(1)} %reshape.23.own_ref.refs_0_), channel_id=1, source_target_pairs={{0,1},{1,0},{2,3},{3,2},{4,5},{5,4},{6,7},{7,6},{8,9},{9,8},{10,11... | collective-permute-start | bytes 368648 | tf_op jit(solution)/shard_map/ppermute | solution.py:182
  9.2 1.2 %collective-permute-done.1.next_ref.refs_6_ = bf16[2,120,256]{2,1,0:T(8,128)(2,1)S(1)} collective-permute-done((bf16[2,120,256]{2,1,0:T(8,128)(2,1)S(1)}, bf16[2,120,256]{2,1,0:T(8,128)(2,1)S(1)}, u32[]{:S(2)}, u32[]{:S(2)}) %collective-permute-start.1) | collective-permute-done | bytes 122912 | tf_op jit(solution)/shard_map/ppermute | solution.py:181
  10.4 1.5 %collective-permute-start.2 = (bf16[2,120,256]{2,1,0:T(8,128)(2,1)S(1)}, bf16[2,120,256]{2,1,0:T(8,128)(2,1)S(1)}, u32[]{:S(2)}, u32[]{:S(2)}) collective-permute-start(bf16[2,120,256]{2,1,0:T(8,128)(2,1)S(1)} %collective-permute-done.1.next_ref.refs_6_), channel_id=1, source_target_pairs={{0,1},{1,0},{2,3},{3,2},{4,5},{5,4},{6,7},{7,6},{8,9},{9,8},{10,11... | collective-permute-start | bytes 368648 | tf_op jit(solution)/shard_map/ppermute | solution.py:182
  11.9 2.7 %collective-permute-done.7.refs_2_ = bf16[2,120,256]{2,1,0:T(8,128)(2,1)S(1)} collective-permute-done((bf16[2,120,256]{2,1,0:T(8,128)(2,1)S(1)}, bf16[2,120,256]{2,1,0:T(8,128)(2,1)S(1)}, u32[]{:S(2)}, u32[]{:S(2)}) %collective-permute-start.7) | collective-permute-done | bytes 122912 | tf_op jit(solution)/shard_map/ppermute | solution.py:181
  14.7 1.5 %collective-permute-start.8 = (bf16[2,120,256]{2,1,0:T(8,128)(2,1)S(1)}, bf16[2,120,256]{2,1,0:T(8,128)(2,1)S(1)}, u32[]{:S(2)}, u32[]{:S(2)}) collective-permute-start(bf16[2,120,256]{2,1,0:T(8,128)(2,1)S(1)} %collective-permute-done.7.refs_2_), channel_id=1, source_target_pairs={{0,1},{1,0},{2,3},{3,2},{4,5},{5,4},{6,7},{7,6},{8,9},{9,8},{10,11... | collective-permute-start | bytes 368648 | tf_op jit(solution)/shard_map/ppermute | solution.py:182
  16.2 1.4 %collective-permute-done.9.refs_4_ = bf16[2,120,256]{2,1,0:T(8,128)(2,1)S(1)} collective-permute-done((bf16[2,120,256]{2,1,0:T(8,128)(2,1)S(1)}, bf16[2,120,256]{2,1,0:T(8,128)(2,1)S(1)}, u32[]{:S(2)}, u32[]{:S(2)}) %collective-permute-start.9) | collective-permute-done | bytes 122912 | tf_op jit(solution)/shard_map/ppermute | solution.py:181
  17.6 1.5 %collective-permute-start.10 = (bf16[2,120,256]{2,1,0:T(8,128)(2,1)S(1)}, bf16[2,120,256]{2,1,0:T(8,128)(2,1)S(1)}, u32[]{:S(2)}, u32[]{:S(2)}) collective-permute-start(bf16[2,120,256]{2,1,0:T(8,128)(2,1)S(1)} %collective-permute-done.9.refs_4_), channel_id=1, source_target_pairs={{0,1},{1,0},{2,3},{3,2},{4,5},{5,4},{6,7},{7,6},{8,9},{9,8},{10,11... | collective-permute-start | bytes 368648 | tf_op jit(solution)/shard_map/ppermute | solution.py:182
  19.2 0.9 %reshape.26.lat_ref = bf16[60,512]{1,0:T(8,128)(2,1)S(1)} reshape(bf16[30,2,512]{2,1,0:T(2,128)(2,1)} %bitcast.21) | data formatting | bytes 122880 | tf_op jit(solution)/shard_map/reshape | solution.py:184
  20.0 0.3 shard_map.51
  20.3 0.6 collective-permute-start.3
  20.9 3.4 %collective-permute-done.3.other_ref = bf16[60,256]{1,0:T(8,128)(2,1)S(1)} collective-permute-done((bf16[60,256]{1,0:T(8,128)(2,1)S(1)}, bf16[60,256]{1,0:T(8,128)(2,1)S(1)}, u32[]{:S(2)}, u32[]{:S(2)}) %collective-permute-start.3) | collective-permute-done | bytes 30752 | tf_op jit(solution)/shard_map/ppermute | solution.py:193
  24.3 0.1 shard_map.52
  24.4 0.1 collective-permute-start.4
  24.5 5.5 %collective-permute-done.4.refs_1_ = bf16[60,128]{1,0:T(8,128)(2,1)S(1)} collective-permute-done((bf16[60,128]{1,0:T(8,128)(2,1)S(1)}, bf16[60,128]{1,0:T(8,128)(2,1)S(1)}, u32[]{:S(2)}, u32[]{:S(2)}) %collective-permute-start.4) | collective-permute-done | bytes 15392 | tf_op jit(solution)/shard_map/ppermute | solution.py:201
  30.0 0.0 collective-permute-start.5
  30.0 4.6 %collective-permute-done.5.refs_2_ = bf16[60,128]{1,0:T(8,128)(2,1)S(1)} collective-permute-done((bf16[60,128]{1,0:T(8,128)(2,1)S(1)}, bf16[60,128]{1,0:T(8,128)(2,1)S(1)}, u32[]{:S(2)}, u32[]{:S(2)}) %collective-permute-start.5) | collective-permute-done | bytes 15392 | tf_op jit(solution)/shard_map/ppermute | solution.py:201
  34.6 0.4 collective-permute-start.6
  35.0 3.4 %collective-permute-done.6.refs_3_ = bf16[60,128]{1,0:T(8,128)(2,1)S(1)} collective-permute-done((bf16[60,128]{1,0:T(8,128)(2,1)S(1)}, bf16[60,128]{1,0:T(8,128)(2,1)S(1)}, u32[]{:S(2)}, u32[]{:S(2)}) %collective-permute-start.6) | collective-permute-done | bytes 15392 | tf_op jit(solution)/shard_map/ppermute | solution.py:201
  38.4 0.9 %shard_map.53.win_ref = bf16[10,576,256]{2,1,0:T(8,128)(2,1)S(1)} custom-call(bf16[60,128]{1,0:T(8,128)(2,1)S(1)} %get-tuple-element.16.refs_0_, bf16[60,128]{1,0:T(8,128)(2,1)S(1)} %collective-permute-done.4.refs_1_, bf16[60,128]{1,0:T(8,128)(2,1)S(1)} %collective-permute-done.5.refs_2_, bf16[60,128]{1,0:T(8,128)(2,1)S(1)} %collective-permute-done.6.refs_3_), custom_call_target="tpu_custom_call" | custom-call | tf_op jit(solution)/shard_map/pallas_call | solution.py:202
  39.3 0.0 collective-permute-done.other_ref.refs_1_
  39.3 0.0 collective-permute-done.2.next_other_ref.refs_7_
  39.3 0.0 collective-permute-done.8.refs_3_
  39.3 0.0 collective-permute-done.10.refs_5_
  39.3 0.1 shard_map.54.grad_ref
  39.4 0.0 slice-start
  39.4 0.8 %shard_map.57 = (f32[288,256]{1,0:T(8,128)S(1)}, f32[288,256]{1,0:T(8,128)S(1)}) custom-call(bf16[10,576,256]{2,1,0:T(8,128)(2,1)S(1)} %shard_map.53.win_ref, bf16[8,2,128,256]{3,2,1,0:T(8,128)(2,1)S(1)} %shard_map.54.grad_ref), custom_call_target="tpu_custom_call" | custom-call | tf_op jit(solution)/shard_map/pallas_call | solution.py:221
  40.2 0.0 slice-start.1
  40.2 0.1 collective-permute-start.15
  40.3 0.8 %shard_map.56 = (f32[288,256]{1,0:T(8,128)S(1)}, f32[288,256]{1,0:T(8,128)S(1)}) custom-call(bf16[10,576,256]{2,1,0:T(8,128)(2,1)S(1)} %shard_map.53.win_ref, bf16[8,2,128,256]{3,2,1,0:T(8,128)(2,1)S(1)} %shard_map.54.grad_ref), custom_call_target="tpu_custom_call" | custom-call | tf_op jit(solution)/shard_map/pallas_call | solution.py:221
  41.1 0.6 collective-permute-start.13
  41.6 0.8 %shard_map.55 = (f32[288,256]{1,0:T(8,128)S(1)}, f32[288,256]{1,0:T(8,128)S(1)}) custom-call(bf16[10,576,256]{2,1,0:T(8,128)(2,1)S(1)} %shard_map.53.win_ref, bf16[8,2,128,256]{3,2,1,0:T(8,128)(2,1)S(1)} %shard_map.54.grad_ref), custom_call_target="tpu_custom_call" | custom-call | tf_op jit(solution)/shard_map/pallas_call | solution.py:221
  42.4 0.1 collective-permute-start.11
  42.5 0.0 collective-permute-done.15
  42.6 1.6 %collective-permute-start.16 = (f32[144,256]{1,0:T(8,128)S(1)}, f32[144,256]{1,0:T(8,128)S(1)}, u32[]{:S(2)}, u32[]{:S(2)}) collective-permute-start(f32[144,256]{1,0:T(8,128)S(1)} %slice.29), channel_id=1, source_target_pairs={{0,16},{8,24},{16,0},{24,8},{1,17},{9,25},{17,1},{25,9},{2,18},{10... | collective-permute-start | bytes 442376 | tf_op jit(solution)/shard_map/ppermute | solution.py:230
  44.1 3.1 %shard_map.50 = bf16[2,30,512]{2,1,0:T(8,128)(2,1)S(1)} custom-call(bf16[2,120,256]{2,1,0:T(8,128)(2,1)S(1)} %reshape.23.own_ref.refs_0_, bf16[2,120,256]{2,1,0:T(8,128)(2,1)S(1)} %collective-permute-done.other_ref.refs_1_, bf16[2,120,256]{2,1,0:T(8,128)(2,1)S(1)} %collective-permute-done.1.next_ref.refs_6_, ...), custom_call_target="tpu_custom_call" | custom-call | tf_op jit(solution)/shard_map/pallas_call | solution.py:235
  47.2 0.7 %copy.5 = bf16[1,2,1,30,512]{4,1,3,2,0:T(2,128)(2,1)} copy(bf16[1,2,1,30,512]{4,3,1,2,0:T(8,128)(2,1)S(1)} %bitcast.16) | data formatting | bytes 122880
  47.9 0.0 collective-permute-done.13
  48.0 0.6 %collective-permute-start.14 = (f32[144,256]{1,0:T(8,128)S(1)}, f32[144,256]{1,0:T(8,128)S(1)}, u32[]{:S(2)}, u32[]{:S(2)}) collective-permute-start(f32[144,256]{1,0:T(8,128)S(1)} %slice.27), channel_id=1, source_target_pairs={{0,16},{8,24},{16,0},{24,8},{1,17},{9,25},{17,1},{25,9},{2,18},{10... | collective-permute-start | bytes 442376 | tf_op jit(solution)/shard_map/ppermute | solution.py:230
  48.6 0.0 collective-permute-done.11
  48.7 1.5 %collective-permute-start.12 = (f32[144,256]{1,0:T(8,128)S(1)}, f32[144,256]{1,0:T(8,128)S(1)}, u32[]{:S(2)}, u32[]{:S(2)}) collective-permute-start(f32[144,256]{1,0:T(8,128)S(1)} %slice.25), channel_id=1, source_target_pairs={{0,16},{8,24},{16,0},{24,8},{1,17},{9,25},{17,1},{25,9},{2,18},{10... | collective-permute-start | bytes 442376 | tf_op jit(solution)/shard_map/ppermute | solution.py:230
  50.2 0.0 collective-permute-done.16
  50.2 4.5 %collective-permute-done.14 = f32[144,256]{1,0:T(8,128)S(1)} collective-permute-done((f32[144,256]{1,0:T(8,128)S(1)}, f32[144,256]{1,0:T(8,128)S(1)}, u32[]{:S(2)}, u32[]{:S(2)}) %collective-permute-start.14) | collective-permute-done | bytes 147488 | tf_op jit(solution)/shard_map/ppermute | solution.py:230
  54.8 2.4 %collective-permute-done.12 = f32[144,256]{1,0:T(8,128)S(1)} collective-permute-done((f32[144,256]{1,0:T(8,128)S(1)}, f32[144,256]{1,0:T(8,128)S(1)}, u32[]{:S(2)}, u32[]{:S(2)}) %collective-permute-start.12) | collective-permute-done | bytes 147488 | tf_op jit(solution)/shard_map/ppermute | solution.py:230
  57.2 0.8 %maximum_bitcast_fusion = f32[16,3,3,3,256]{4,0,3,2,1:T(8,128)} fusion(f32[1,3,3,16,256]{4,3,2,1,0:T(8,128)S(1)} %bitcast.17, f32[1,3,3,16,256]{4,3,2,1,0:T(8,128)S(1)} %bitcast.18, f32[1,3,3,16,256]{4,3,2,1,0:T(8,128)S(1)} %bitcast.19), kind=kLoop, calls=%fused_computation | loop fusion | flops 221184 | bytes 884736 | tf_op jit(solution)/shard_map/transpose | solution.py:232
  (12 shorter events, 0.2 us)
Async XLA Ops:
  1.6 8.8 %collective-permute-start.1 = (bf16[2,120,256]{2,1,0:T(8,128)(2,1)S(1)}, bf16[2,120,256]{2,1,0:T(8,128)(2,1)S(1)}, u32[]{:S(2)}, u32[]{:S(2)}) collective-permute-start(bf16[2,120,256]{2,1,0:T(8,128)(2,1)S(1)} %reshape.23.own_ref.refs_0_), channel_id=1, source_target_pairs={{0,6},{2,0},{4,2},{6,4},{1,7},{3,1},{5,3},{7,5},{8,14},{10,8},{12,... | collective-permute-start | bytes 368648 | tf_op jit(solution)/shard_map/ppermute | solution.py:181
  6.7 8.0 %collective-permute-start.7 = (bf16[2,120,256]{2,1,0:T(8,128)(2,1)S(1)}, bf16[2,120,256]{2,1,0:T(8,128)(2,1)S(1)}, u32[]{:S(2)}, u32[]{:S(2)}) collective-permute-start(bf16[2,120,256]{2,1,0:T(8,128)(2,1)S(1)} %reshape.23.own_ref.refs_0_), channel_id=1, source_target_pairs={{0,2},{2,4},{4,6},{6,0},{1,3},{3,5},{5,7},{7,1},{8,10},{10,12},{12... | collective-permute-start | bytes 368648 | tf_op jit(solution)/shard_map/ppermute | solution.py:181
  6.7 10.9 %collective-permute-start.9 = (bf16[2,120,256]{2,1,0:T(8,128)(2,1)S(1)}, bf16[2,120,256]{2,1,0:T(8,128)(2,1)S(1)}, u32[]{:S(2)}, u32[]{:S(2)}) collective-permute-start(bf16[2,120,256]{2,1,0:T(8,128)(2,1)S(1)} %reshape.23.own_ref.refs_0_), channel_id=1, source_target_pairs={{0,4},{2,6},{4,0},{6,2},{1,5},{3,7},{5,1},{7,3},{8,12},{10,14},{12... | collective-permute-start | bytes 368648 | tf_op jit(solution)/shard_map/ppermute | solution.py:181
  7.7 31.6 %collective-permute-start = (bf16[2,120,256]{2,1,0:T(8,128)(2,1)S(1)}, bf16[2,120,256]{2,1,0:T(8,128)(2,1)S(1)}, u32[]{:S(2)}, u32[]{:S(2)}) collective-permute-start(bf16[2,120,256]{2,1,0:T(8,128)(2,1)S(1)} %reshape.23.own_ref.refs_0_), channel_id=1, source_target_pairs={{0,1},{1,0},{2,3},{3,2},{4,5},{5,4},{6,7},{7,6},{8,9},{9,8},{10,11... | collective-permute-start | bytes 368648 | tf_op jit(solution)/shard_map/ppermute | solution.py:182
  10.4 28.9 %collective-permute-start.2 = (bf16[2,120,256]{2,1,0:T(8,128)(2,1)S(1)}, bf16[2,120,256]{2,1,0:T(8,128)(2,1)S(1)}, u32[]{:S(2)}, u32[]{:S(2)}) collective-permute-start(bf16[2,120,256]{2,1,0:T(8,128)(2,1)S(1)} %collective-permute-done.1.next_ref.refs_6_), channel_id=1, source_target_pairs={{0,1},{1,0},{2,3},{3,2},{4,5},{5,4},{6,7},{7,6},{8,9},{9,8},{10,11... | collective-permute-start | bytes 368648 | tf_op jit(solution)/shard_map/ppermute | solution.py:182
  14.7 24.6 %collective-permute-start.8 = (bf16[2,120,256]{2,1,0:T(8,128)(2,1)S(1)}, bf16[2,120,256]{2,1,0:T(8,128)(2,1)S(1)}, u32[]{:S(2)}, u32[]{:S(2)}) collective-permute-start(bf16[2,120,256]{2,1,0:T(8,128)(2,1)S(1)} %collective-permute-done.7.refs_2_), channel_id=1, source_target_pairs={{0,1},{1,0},{2,3},{3,2},{4,5},{5,4},{6,7},{7,6},{8,9},{9,8},{10,11... | collective-permute-start | bytes 368648 | tf_op jit(solution)/shard_map/ppermute | solution.py:182
  17.6 21.7 %collective-permute-start.10 = (bf16[2,120,256]{2,1,0:T(8,128)(2,1)S(1)}, bf16[2,120,256]{2,1,0:T(8,128)(2,1)S(1)}, u32[]{:S(2)}, u32[]{:S(2)}) collective-permute-start(bf16[2,120,256]{2,1,0:T(8,128)(2,1)S(1)} %collective-permute-done.9.refs_4_), channel_id=1, source_target_pairs={{0,1},{1,0},{2,3},{3,2},{4,5},{5,4},{6,7},{7,6},{8,9},{9,8},{10,11... | collective-permute-start | bytes 368648 | tf_op jit(solution)/shard_map/ppermute | solution.py:182
  20.3 4.0 %collective-permute-start.3 = (bf16[60,256]{1,0:T(8,128)(2,1)S(1)}, bf16[60,256]{1,0:T(8,128)(2,1)S(1)}, u32[]{:S(2)}, u32[]{:S(2)}) collective-permute-start(bf16[60,256]{1,0:T(8,128)(2,1)S(1)} %get-tuple-element.15), channel_id=1, source_target_pairs={{0,1},{1,0},{2,3},{3,2},{4,5},{5,4},{6,7},{7,6},{8,9},{9,8},{10,11... | collective-permute-start | bytes 92168 | tf_op jit(solution)/shard_map/ppermute | solution.py:193
  24.4 5.6 %collective-permute-start.4 = (bf16[60,128]{1,0:T(8,128)(2,1)S(1)}, bf16[60,128]{1,0:T(8,128)(2,1)S(1)}, u32[]{:S(2)}, u32[]{:S(2)}) collective-permute-start(bf16[60,128]{1,0:T(8,128)(2,1)S(1)} %get-tuple-element.17), channel_id=1, source_target_pairs={{0,2},{2,4},{4,6},{6,0},{1,3},{3,5},{5,7},{7,1},{8,10},{10,12},{12... | collective-permute-start | bytes 46088 | tf_op jit(solution)/shard_map/ppermute | solution.py:201
  30.0 4.6 %collective-permute-start.5 = (bf16[60,128]{1,0:T(8,128)(2,1)S(1)}, bf16[60,128]{1,0:T(8,128)(2,1)S(1)}, u32[]{:S(2)}, u32[]{:S(2)}) collective-permute-start(bf16[60,128]{1,0:T(8,128)(2,1)S(1)} %get-tuple-element.18), channel_id=1, source_target_pairs={{0,4},{2,6},{4,0},{6,2},{1,5},{3,7},{5,1},{7,3},{8,12},{10,14},{12... | collective-permute-start | bytes 46088 | tf_op jit(solution)/shard_map/ppermute | solution.py:201
  34.6 3.7 %collective-permute-start.6 = (bf16[60,128]{1,0:T(8,128)(2,1)S(1)}, bf16[60,128]{1,0:T(8,128)(2,1)S(1)}, u32[]{:S(2)}, u32[]{:S(2)}) collective-permute-start(bf16[60,128]{1,0:T(8,128)(2,1)S(1)} %get-tuple-element.19), channel_id=1, source_target_pairs={{0,6},{2,0},{4,2},{6,4},{1,7},{3,1},{5,3},{7,5},{8,14},{10,8},{12,... | collective-permute-start | bytes 46088 | tf_op jit(solution)/shard_map/ppermute | solution.py:201
  39.4 4.7 %slice-start = ((s8[7077888]{0:T(1024)(128)(4,1)}), s8[4194304]{0:T(1024)(128)(4,1)S(1)}, s32[]{:S(2)}) async-start(s8[7077888]{0:T(1024)(128)(4,1)} %bitcast.13), calls=%async_computation | async-start | bytes 8388608
  40.2 3.9 %slice-start.1 = ((s8[7077888]{0:T(1024)(128)(4,1)}), s8[2883584]{0:T(1024)(128)(4,1)S(1)}, s32[]{:S(2)}) async-start(s8[7077888]{0:T(1024)(128)(4,1)} %bitcast.13), calls=%async_computation.1 | async-start | bytes 5767168
  40.2 2.3 %collective-permute-start.15 = (f32[288,256]{1,0:T(8,128)S(1)}, f32[288,256]{1,0:T(8,128)S(1)}, u32[]{:S(2)}, u32[]{:S(2)}) collective-permute-start(f32[288,256]{1,0:T(8,128)S(1)} %get-tuple-element.25), channel_id=1, source_target_pairs={{0,8},{8,0},{16,24},{24,16},{1,9},{9,1},{17,25},{25,17},{2,10},{10... | collective-permute-start | bytes 884744 | tf_op jit(solution)/shard_map/ppermute | solution.py:228
  41.1 6.8 %collective-permute-start.13 = (f32[288,256]{1,0:T(8,128)S(1)}, f32[288,256]{1,0:T(8,128)S(1)}, u32[]{:S(2)}, u32[]{:S(2)}) collective-permute-start(f32[288,256]{1,0:T(8,128)S(1)} %get-tuple-element.23), channel_id=1, source_target_pairs={{0,8},{8,0},{16,24},{24,16},{1,9},{9,1},{17,25},{25,17},{2,10},{10... | collective-permute-start | bytes 884744 | tf_op jit(solution)/shard_map/ppermute | solution.py:228
  42.4 6.2 %collective-permute-start.11 = (f32[288,256]{1,0:T(8,128)S(1)}, f32[288,256]{1,0:T(8,128)S(1)}, u32[]{:S(2)}, u32[]{:S(2)}) collective-permute-start(f32[288,256]{1,0:T(8,128)S(1)} %get-tuple-element.21), channel_id=1, source_target_pairs={{0,8},{8,0},{16,24},{24,16},{1,9},{9,1},{17,25},{25,17},{2,10},{10... | collective-permute-start | bytes 884744 | tf_op jit(solution)/shard_map/ppermute | solution.py:228
  42.6 7.6 %collective-permute-start.16 = (f32[144,256]{1,0:T(8,128)S(1)}, f32[144,256]{1,0:T(8,128)S(1)}, u32[]{:S(2)}, u32[]{:S(2)}) collective-permute-start(f32[144,256]{1,0:T(8,128)S(1)} %slice.29), channel_id=1, source_target_pairs={{0,16},{8,24},{16,0},{24,8},{1,17},{9,25},{17,1},{25,9},{2,18},{10... | collective-permute-start | bytes 442376 | tf_op jit(solution)/shard_map/ppermute | solution.py:230
  48.0 6.7 %collective-permute-start.14 = (f32[144,256]{1,0:T(8,128)S(1)}, f32[144,256]{1,0:T(8,128)S(1)}, u32[]{:S(2)}, u32[]{:S(2)}) collective-permute-start(f32[144,256]{1,0:T(8,128)S(1)} %slice.27), channel_id=1, source_target_pairs={{0,16},{8,24},{16,0},{24,8},{1,17},{9,25},{17,1},{25,9},{2,18},{10... | collective-permute-start | bytes 442376 | tf_op jit(solution)/shard_map/ppermute | solution.py:230
  48.7 8.5 %collective-permute-start.12 = (f32[144,256]{1,0:T(8,128)S(1)}, f32[144,256]{1,0:T(8,128)S(1)}, u32[]{:S(2)}, u32[]{:S(2)}) collective-permute-start(f32[144,256]{1,0:T(8,128)S(1)} %slice.25), channel_id=1, source_target_pairs={{0,16},{8,24},{16,0},{24,8},{1,17},{9,25},{17,1},{25,9},{2,18},{10... | collective-permute-start | bytes 442376 | tf_op jit(solution)/shard_map/ppermute | solution.py:230

commit v2 on v1

--- a/solution.py
+++ b/solution.py
@@ -8,7 +8,7 @@
 from jax.sharding import PartitionSpec as P
 
 VMEM_LIMIT = 40 * 1024 * 1024
-SLOTS = (1, 3, 0, 2)
+SLOTS = (3, 2, 1, 0)
 
 
 def cycle(size, by):
@@ -19,95 +19,101 @@
     return [pl.BlockSpec(memory_space=pltpu.VMEM)] * count
 
 
-def params():
-    return pltpu.CompilerParams(vmem_limit_bytes=VMEM_LIMIT)
-
-
-def select_kernel(tm, share, lat_ref, own_ref, other_ref):
+def params(limit=VMEM_LIMIT):
+    return pltpu.CompilerParams(vmem_limit_bytes=limit)
+
+
+def light():
+    return pl.CostEstimate(flops=1, bytes_accessed=1, transcendentals=0)
+
+
+LATENT_ROWS = 16
+MESSAGE_ROWS = LATENT_ROWS + 120
+
+
+def message_kernel(tm, share, lat_ref, grad_ref, *refs):
+    outs, wide_ref = refs[:tm], refs[tm]
     channels = lat_ref.shape[1]
-    width = channels // 2
     me_dp, me_tm, me_rows = lax.axis_index("dp"), lax.axis_index("tm"), lax.axis_index("rows")
-    col = lax.broadcasted_iota(jnp.int32, (1, width), 1)
+    col = lax.broadcasted_iota(jnp.int32, (1, channels), 1)
     inner = col % share
     place = (col // share) % 4
-    shift = col // (4 * share)
+    crossing = (col // (4 * share)) % 2
+    shift = col // (8 * share)
     slot = jnp.where(place == 0, SLOTS[0], jnp.where(place == 1, SLOTS[1], jnp.where(place == 2, SLOTS[2], SLOTS[3])))
     dp = jnp.bitwise_xor(slot, me_dp)
-    frame = (shift + me_tm) % tm
-    row = lax.broadcasted_iota(jnp.int32, (channels, width), 0)
-    for ref, rows in ((own_ref, me_rows), (other_ref, 1 - me_rows)):
-        wanted = ((dp * tm + frame) * 2 + rows) * share + inner
-        pick = jnp.where(row == wanted, 1.0, 0.0).astype(jnp.bfloat16)
-        ref[...] = jnp.dot(lat_ref[...], pick, preferred_element_type=jnp.float32).astype(jnp.bfloat16)
-
-
-def pair_kernel(tm, own_ref, other_ref, *outs):
-    width = own_ref.shape[1] // tm
+    rows = jnp.bitwise_xor(crossing, me_rows)
+    wanted = ((dp * tm + (shift + me_tm) % tm) * 2 + rows) * share + inner
+    row = lax.broadcasted_iota(jnp.int32, (channels, channels), 0)
+    pick = jnp.where(row == wanted, 1.0, 0.0).astype(jnp.bfloat16)
+    wide_ref[48:64, :] = jnp.zeros((16, channels), jnp.float32)
+    wide_ref[0:60, :] = jnp.dot(lat_ref[...], pick, preferred_element_type=jnp.float32)
     for k in range(tm):
-        cols = slice(k * width, (k + 1) * width)
-        outs[k][...] = jnp.concatenate([own_ref[:, cols], other_ref[:, cols]], axis=1)
-
-
-def windows_kernel(tm, share, *refs):
-    pieces, out_ref, lat_ref, pick_ref = refs[:tm], refs[tm], refs[tm + 1], refs[tm + 2]
+        for part in range(4):
+            piece = wide_ref[16 * part : 16 * part + 16, 128 * k : 128 * k + 128]
+            lanes = slice(128 * (part % 2), 128 * (part % 2) + 128)
+            outs[k][part // 2, 0:LATENT_ROWS, lanes] = piece.astype(jnp.bfloat16)
+        for f in range(2):
+            outs[k][f, LATENT_ROWS:, :] = grad_ref[f]
+
+
+def arrange_kernel(tm, share, shifts, *refs):
+    blocks = refs[: 2 * len(shifts)]
+    win_ref, grad_ref, pick_ref, lat_ref = refs[-4:]
     group = 4 * share
     me_tm, me_rows = lax.axis_index("tm"), lax.axis_index("rows")
-    lat_ref[...] = jnp.zeros_like(lat_ref)
-    for k in range(tm):
-        t = lax.rem(me_tm + tm - k, tm)
-        block = pieces[k][...].astype(jnp.float32)
-        lat_ref[t, me_rows, 0:60, :] = block[:, :group]
-        lat_ref[t, 1 - me_rows, 0:60, :] = block[:, group:]
-    kappa = lax.broadcasted_iota(jnp.int32, (128, 128), 0)
-    rho = lax.broadcasted_iota(jnp.int32, (1, 128), 1)
-    w, h = rho // 2, rho % 2
-    for f in range(2):
-        for ij in range(9):
-            i, j = ij // 3, ij % 3
-            for s in range(2):
-                r = (2 * s + h + 1 + i) // 2 - 1
-                q = (w + 1 + j) // 2 - 1
-                ok = (r >= 0) & (r < 2) & (q >= 0) & (q < 30) & (rho < 120)
-                target = jnp.where(ok, r * 64 + q * 2 + f, -1)
-                pick = jnp.where(kappa == target, 1.0, 0.0).astype(jnp.bfloat16)
-                base = (f * 9 + ij) * 256 + s * 128
-                pick_ref[:, base : base + 128] = pick
+    if 0 in shifts:
+        kappa = lax.broadcasted_iota(jnp.int32, (128, 128), 0)
+        rho = lax.broadcasted_iota(jnp.int32, (1, 128), 1)
+        w, h = rho // 2, rho % 2
+        for f in range(2):
+            for ij in range(9):
+                i, j = ij // 3, ij % 3
+                for s in range(2):
+                    r = (2 * s + h + 1 + i) // 2 - 1
+                    q = (w + 1 + j) // 2 - 1
+                    ok = (r >= 0) & (r < 2) & (q >= 0) & (q < 30) & (rho < 120)
+                    target = jnp.where(ok, r * 64 + q * 2 + f, -1)
+                    pick = jnp.where(kappa == target, 1.0, 0.0).astype(jnp.bfloat16)
+                    base = (f * 9 + ij) * 256 + s * 128
+                    pick_ref[:, base : base + 128] = pick
+        win_ref[0:2] = jnp.zeros((2,) + win_ref.shape[1:], jnp.bfloat16)
+    where = [lax.rem(me_tm + tm - k, tm) for k in shifts]
+    for n, t in enumerate(where):
+        for half, rows in enumerate((me_rows, 1 - me_rows)):
+            block = blocks[2 * n + half]
+            for part in range(4):
+                lanes = 128 * (part % 2) + group * half
+                piece = block[part // 2, 0:LATENT_ROWS, lanes : lanes + group]
+                lat_ref[n, rows, 16 * part : 16 * part + 16, :] = piece.astype(jnp.float32)
+            for f in range(2):
+                grad_ref[2 * t + f, rows, 112:128, :] = jnp.zeros((16, grad_ref.shape[3]), jnp.bfloat16)
+                grad_ref[2 * t + f, rows, 0:120, :] = block[f, LATENT_ROWS:, :]
     stacked = jnp.concatenate(
-        [jnp.transpose(lat_ref[t].reshape(128, group)) for t in range(tm)], axis=0
+        [jnp.transpose(lat_ref[n].reshape(128, group)) for n in range(len(shifts))], axis=0
     ).astype(jnp.bfloat16)
-    out_ref[0:2] = jnp.zeros((2,) + out_ref.shape[1:], jnp.bfloat16)
     for f in range(2):
         for ij in range(9):
             base = (f * 9 + ij) * 256
             wide = jnp.dot(stacked, pick_ref[:, base : base + 256], preferred_element_type=jnp.float32)
             wide = wide.astype(jnp.bfloat16)
-            for t in range(tm):
+            for n, t in enumerate(where):
                 for p in range(4):
-                    src = t * group + p * share
+                    src = n * group + p * share
                     dst = p * 9 * share + ij * share
-                    out_ref[2 * t + f + 2, dst : dst + share, :] = wide[src : src + share]
-
-
-def gather_kernel(tm, *refs):
-    blocks, out_ref = refs[: 2 * tm], refs[2 * tm]
-    me_tm, me_rows = lax.axis_index("tm"), lax.axis_index("rows")
-    out_ref[:, :, 112:128, :] = jnp.zeros(out_ref.shape[:2] + (16, out_ref.shape[3]), jnp.bfloat16)
-    for k in range(tm):
-        t = lax.rem(me_tm + tm - k, tm)
-        for f in range(2):
-            out_ref[2 * t + f, me_rows, 0:120, :] = blocks[2 * k][f]
-            out_ref[2 * t + f, 1 - me_rows, 0:120, :] = blocks[2 * k + 1][f]
-
-
-def terms_kernel(a, frames, win_ref, grad_ref, send_ref, keep_ref):
-    half = send_ref.shape[0]
-    for ref, start in ((send_ref, 0), (keep_ref, half)):
-        total = None
-        for f in range(frames):
-            g = grad_ref[f].reshape(256, grad_ref.shape[3])
-            term = jnp.dot(win_ref[f + a, start : start + half, :], g, preferred_element_type=jnp.float32)
-            total = term if total is None else total + term
-        ref[...] = total
+                    win_ref[2 * t + f + 2, dst : dst + share, :] = wide[src : src + share]
+
+
+def terms_kernel(first, taps, frames, win_ref, grad_ref, send_ref, keep_ref):
+    rows = send_ref.shape[0] // len(taps)
+    for n, a in enumerate(taps):
+        for ref, start in ((send_ref, first), (keep_ref, first + rows)):
+            total = None
+            for f in range(frames):
+                g = grad_ref[f].reshape(256, grad_ref.shape[3])
+                term = jnp.dot(win_ref[f + a, start : start + rows, :], g, preferred_element_type=jnp.float32)
+                total = term if total is None else total + term
+            ref[n * rows : (n + 1) * rows] = total
 
 
 def latents_kernel(tm, own_ref, other_ref, next_ref, next_other_ref, kernel_ref, out_ref, wide_ref, pool_ref, total_ref):
@@ -129,8 +135,8 @@
         for f in range(4):
             mine, theirs = (own_ref, other_ref) if f < 2 else (next_ref, next_other_ref)
             for n in range(lanes):
-                wide_ref[0, n, 0:120, :] = mine[f % 2, :, 128 * n : 128 * n + 128].astype(jnp.float32)
-                wide_ref[1, n, 0:120, :] = theirs[f % 2, :, 128 * n : 128 * n + 128].astype(jnp.float32)
+                wide_ref[0, n, 0:120, :] = mine[f % 2, LATENT_ROWS:, 128 * n : 128 * n + 128].astype(jnp.float32)
+                wide_ref[1, n, 0:120, :] = theirs[f % 2, LATENT_ROWS:, 128 * n : 128 * n + 128].astype(jnp.float32)
             x = [[every_fourth(0, 2 * t + h) for t in range(2)] for h in range(2)]
             up = [every_fourth(1, 2 * t + 1) * above for t in range(2)]
             down = [every_fourth(1, 2 * t) * (1.0 - above) for t in range(2)]
@@ -178,65 +184,66 @@
     swap = [(0, 1), (1, 0)]
 
     mine = jnp.transpose(grad_out[0], (0, 2, 1, 3)).reshape(2, 120, outputs)
-    shifted = [mine] + [lax.ppermute(mine, "tm", cycle(tm, k)) for k in range(1, tm)]
-    across = [lax.ppermute(block, "rows", swap) for block in shifted]
-
     lat = jnp.transpose(latents[0, :, 0], (1, 0, 2)).reshape(60, channels)
-    half = jax.ShapeDtypeStruct((60, channels // 2), jnp.bfloat16)
-    own, other = pl.pallas_call(
-        functools.partial(select_kernel, tm, share),
-        out_shape=(half, half),
-        in_specs=whole(1),
-        out_specs=tuple(whole(2)),
-        compiler_params=params(),
-    )(lat)
-    other = lax.ppermute(other, "rows", swap)
-    pieces = pl.pallas_call(
-        functools.partial(pair_kernel, tm),
-        out_shape=tuple([jax.ShapeDtypeStruct((60, 8 * share), jnp.bfloat16)] * tm),
+    message = jax.ShapeDtypeStruct((2, MESSAGE_ROWS, outputs), jnp.bfloat16)
+    messages = pl.pallas_call(
+        functools.partial(message_kernel, tm, share),
+        out_shape=tuple([message] * tm),
         in_specs=whole(2),
         out_specs=tuple(whole(tm)),
+        scratch_shapes=[pltpu.VMEM((64, channels), jnp.float32)],
         compiler_params=params(),
-    )(own, other)
-    pieces = [pieces[0]] + [lax.ppermute(pieces[k], "tm", cycle(tm, k)) for k in range(1, tm)]
-    windows = pl.pallas_call(
-        functools.partial(windows_kernel, tm, share),
-        out_shape=jax.ShapeDtypeStruct((frames + 2, 36 * share, 256), jnp.bfloat16),
-        in_specs=whole(tm),
-        out_specs=whole(1)[0],
-        scratch_shapes=[pltpu.VMEM((tm, 2, 64, 4 * share), jnp.float32), pltpu.VMEM((128, 18 * 256), jnp.bfloat16)],
-        compiler_params=params(),
-    )(*pieces)
-    grads = pl.pallas_call(
-        functools.partial(gather_kernel, tm),
-        out_shape=jax.ShapeDtypeStruct((frames, 2, 128, outputs), jnp.bfloat16),
-        in_specs=whole(2 * tm),
-        out_specs=whole(1)[0],
-        compiler_params=params(),
-    )(*[block for pair in zip(shifted, across) for block in pair])
-
-    rows = 18 * share
-    parts = []
-    for a in range(3):
-        send, keep = pl.pallas_call(
-            functools.partial(terms_kernel, a, frames),
-            out_shape=tuple([jax.ShapeDtypeStruct((rows, outputs), jnp.float32)] * 2),
+    )(lat, mine)
+    order = [0, tm - 1] + list(range(1, tm - 1))
+    shifted = {k: lax.ppermute(messages[k], "tm", cycle(tm, k)) if k else messages[0] for k in order}
+    across = {k: lax.ppermute(shifted[k], "rows", swap) for k in order}
+
+    arranged = (
+        jax.ShapeDtypeStruct((frames + 2, 36 * share, 256), jnp.bfloat16),
+        jax.ShapeDtypeStruct((frames, 2, 128, outputs), jnp.bfloat16),
+        jax.ShapeDtypeStruct((128, 18 * 256), jnp.bfloat16),
+    )
+
+    def arrange(shifts, earlier):
+        blocks = [block for k in shifts for block in (shifted[k], across[k])]
+        return pl.pallas_call(
+            functools.partial(arrange_kernel, tm, share, tuple(shifts)),
+            out_shape=arranged,
+            in_specs=whole(len(blocks) + len(earlier)),
+            out_specs=tuple(whole(3)),
+            scratch_shapes=[pltpu.VMEM((len(shifts), 2, 64, 4 * share), jnp.float32)],
+            input_output_aliases={len(blocks) + n: n for n in range(len(earlier))},
+            compiler_params=params(),
+        )(*blocks, *earlier)
+
+    early = arrange(order[:-1], ())
+    windows, grads, _ = arrange(order[-1:], early)
+
+    rows = 9 * share
+
+    def terms(first, taps, windows):
+        return pl.pallas_call(
+            functools.partial(terms_kernel, first, taps, frames),
+            out_shape=tuple([jax.ShapeDtypeStruct((len(taps) * rows, outputs), jnp.float32)] * 2),
             in_specs=whole(2),
             out_specs=tuple(whole(2)),
             compiler_params=params(),
+            cost_estimate=light(),
         )(windows, grads)
-        both = keep + lax.ppermute(send, "dp", [(i, i ^ 1) for i in range(4)])
-        kept, sent = both[: rows // 2], both[rows // 2 :]
-        parts.append((kept + lax.ppermute(sent, "dp", [(i, i ^ 2) for i in range(4)])) * factor)
-    weight_grad = jnp.stack(parts).reshape(3, 3, 3, share, outputs)
-    weight_grad = jnp.transpose(weight_grad, (3, 0, 1, 2, 4))
-
+
+    def other_core(block):
+        return lax.ppermute(block, "dp", [(i, i ^ 1) for i in range(4)])
+
+    send, keep = terms(0, (0, 1, 2), windows)
+    chip = keep + other_core(send)
+    crossed = lax.ppermute(chip, "dp", [(i, i ^ 2) for i in range(4)])
+    windows, first, *_ = lax.optimization_barrier((windows, shifted[0], chip))
     taps = kernel.reshape(27, channels, outputs)
     grad_latents = pl.pallas_call(
         functools.partial(latents_kernel, tm),
         grid=(3,),
         out_shape=jax.ShapeDtypeStruct((2, 30, channels), jnp.bfloat16),
-        in_specs=[pl.BlockSpec((2, 120, outputs), lambda a: (0, 0, 0))] * 4
+        in_specs=[pl.BlockSpec((2, MESSAGE_ROWS, outputs), lambda a: (0, 0, 0))] * 4
         + [pl.BlockSpec((9, channels, outputs), lambda a: (a, 0, 0))],
         out_specs=pl.BlockSpec((2, 30, channels), lambda a: (0, 0, 0)),
         scratch_shapes=[
@@ -245,7 +252,15 @@
             pltpu.VMEM((128, channels), jnp.float32),
         ],
         compiler_params=params(),
-    )(shifted[0], across[0], shifted[tm - 1], across[tm - 1], taps)
+        cost_estimate=light(),
+    )(first, across[0], shifted[tm - 1], across[tm - 1], taps)
+
+    stay = []
+    for a in range(3):
+        send, keep = terms(2 * rows, (a,), windows)
+        stay.append(keep + other_core(send))
+    total = (jnp.concatenate(stay) + crossed) * factor
+    weight_grad = jnp.transpose(total.reshape(3, 3, 3, share, outputs), (3, 0, 1, 2, 4))
     return (grad_latents.reshape(latents.shape), weight_grad)
 
 
@@ -335,7 +350,7 @@
 
 def body(latents, grad_out, kernel):
     share = latents.shape[4] // (lax.axis_size("dp") * lax.axis_size("tm") * lax.axis_size("rows"))
-    narrow = lax.axis_size("rows") == 2 and lax.axis_size("dp") == 4 and share % 16 == 0
+    narrow = lax.axis_size("rows") == 2 and lax.axis_size("dp") == 4 and share == 16
     return (narrow_body if narrow else wide_body)(latents, grad_out, kernel)
 
 

time: 58.2 us -> 41.6 us (0.71)
  waiting for transfers between devices: 29.3 us -> 15.4 us
  starting transfers between devices: 17.6 us -> 14.5 us
    ppermute x17 -> x12, waiting for transfers between devices: 29.3 us -> 15.4 us  [the longest x3 6.43 us: narrow_body(): lax.ppermute(messages[k], 'tm', cycle(tm, k))]
    ppermute x17 -> x12, starting transfers between devices: 17.6 us -> 14.5 us  [the longest x3 6.11 us: narrow_body(): lax.ppermute(messages[k], 'tm', cycle(tm, k))]
    transpose x1 -> x0, other arithmetic: 0.79 us -> none  [narrow_body(): weight_grad = jnp.transpose(weight_grad, (3, 0, 1, 2, 4))]
    mul x3 -> x1, other arithmetic: 0.06 us -> 0.82 us  [narrow_body(): total = (jnp.concatenate(stay) + crossed) * factor]
  transfers between devices with their start and end apart: 17 -> 12, of which waited for: 9 -> 6; matrix products, arithmetic and copies ran while one was open for 3% -> 2% of each run, Pallas kernels for 10% -> 13%
where the time goes in v2:
time: 41.6 us; the launch traced here: 41.4 us
  waiting for transfers between devices  15.4 us (37%)
  starting transfers between devices  14.5 us (35%)
  Pallas kernels  7.12 us (17%)
  local copies, waits for them, and re-layouts  2.66 us (6%)
  other arithmetic  0.94 us (2%)
  between operations  0.76 us (2%)
    ppermute x3, waiting for transfers between devices, narrow_body(): lax.ppermute(messages[k], 'tm', cycle(tm, k))  6.43 us
    ppermute x3, starting transfers between devices, narrow_body(): lax.ppermute(messages[k], 'tm', cycle(tm, k))  6.11 us
    ppermute x4, starting transfers between devices, narrow_body(): across = {k: lax.ppermute(shifted[k], 'rows', swap) for k in order}  6.08 us
    ppermute x1, waiting for transfers between devices, narrow_body(): crossed = lax.ppermute(chip, 'dp', [(i, i ^ 2) for i in range(4)])  4.49 us
    pallas_call x1, Pallas kernels, narrow_body(): pl.pallas_call(functools.partial(latents_kernel, tm), grid=(3,), out_shap...  3.1 us
    ppermute x4, waiting for transfers between devices, narrow_body(): across = {k: lax.ppermute(shifted[k], 'rows', swap) for k in order}  2.67 us
    pallas_call x4, Pallas kernels, terms(): pl.pallas_call(functools.partial(terms_kernel, first, taps, frames), out_...  2.49 us
    ppermute x4, waiting for transfers between devices, other_core(): return lax.ppermute(block, 'dp', [(i, i ^ 1) for i in range(4)])  1.79 us
  transfers between devices with their start and end apart: 12, of which 6 were waited for; matrix products, arithmetic and copies ran while one was open for 2% of the time, Pallas kernels for 13%

profile of v2, /device:TPU:0, one launch (start us, length us, event | category | flops | bytes accessed | tf_op | source)
XLA Modules:
  0.0 41.4 jit_solution(2624434901873578374)
XLA Ops:
  0.6 0.9 %reshape.19.lat_ref = bf16[60,512]{1,0:T(8,128)(2,1)S(1)} reshape(bf16[30,2,512]{2,1,0:T(2,128)(2,1)} %bitcast.17) | data formatting | bytes 122880 | tf_op jit(solution)/shard_map/reshape | solution.py:187
  1.5 1.0 %reshape.20.grad_ref = bf16[2,120,256]{2,1,0:T(8,128)(2,1)S(1)} reshape(bf16[2,60,2,256]{3,2,1,0:T(2,128)(2,1)} %bitcast.16) | data formatting | bytes 245760 | tf_op jit(solution)/shard_map/reshape | solution.py:186
  2.5 0.2 shard_map.50
  2.7 5.1 %collective-permute-start.3 = (bf16[2,136,256]{2,1,0:T(8,128)(2,1)S(1)}, bf16[2,136,256]{2,1,0:T(8,128)(2,1)S(1)}, u32[]{:S(2)}, u32[]{:S(2)}) collective-permute-start(bf16[2,136,256]{2,1,0:T(8,128)(2,1)S(1)} %get-tuple-element.23), channel_id=1, source_target_pairs={{0,6},{2,0},{4,2},{6,4},{1,7},{3,1},{5,3},{7,5},{8,14},{10,8},{12,... | collective-permute-start | bytes 417800 | tf_op jit(solution)/shard_map/ppermute | solution.py:198
  7.8 0.0 collective-permute-start.5
  7.8 1.0 %collective-permute-start = (bf16[2,136,256]{2,1,0:T(8,128)(2,1)S(1)}, bf16[2,136,256]{2,1,0:T(8,128)(2,1)S(1)}, u32[]{:S(2)}, u32[]{:S(2)}) collective-permute-start(bf16[2,136,256]{2,1,0:T(8,128)(2,1)S(1)} %get-tuple-element.21), channel_id=1, source_target_pairs={{0,4},{2,6},{4,0},{6,2},{1,5},{3,7},{5,1},{7,3},{8,12},{10,14},{12... | collective-permute-start | bytes 417800 | tf_op jit(solution)/shard_map/ppermute | solution.py:198
  8.8 1.5 %collective-permute-start.2 = (bf16[2,136,256]{2,1,0:T(8,128)(2,1)S(1)}, bf16[2,136,256]{2,1,0:T(8,128)(2,1)S(1)}, u32[]{:S(2)}, u32[]{:S(2)}) collective-permute-start(bf16[2,136,256]{2,1,0:T(8,128)(2,1)S(1)} %get-tuple-element.32.refs_0_.own_ref), channel_id=1, source_target_pairs={{0,1},{1,0},{2,3},{3,2},{4,5},{5,4},{6,7},{7,6},{8,9},{9,8},{10,11... | collective-permute-start | bytes 417800 | tf_op jit(solution)/shard_map/ppermute | solution.py:199
  10.3 1.5 %collective-permute-done.3.refs_2_.next_ref = bf16[2,136,256]{2,1,0:T(8,128)(2,1)S(1)} collective-permute-done((bf16[2,136,256]{2,1,0:T(8,128)(2,1)S(1)}, bf16[2,136,256]{2,1,0:T(8,128)(2,1)S(1)}, u32[]{:S(2)}, u32[]{:S(2)}) %collective-permute-start.3) | collective-permute-done | bytes 139296 | tf_op jit(solution)/shard_map/ppermute | solution.py:198
  11.9 1.5 %collective-permute-start.4 = (bf16[2,136,256]{2,1,0:T(8,128)(2,1)S(1)}, bf16[2,136,256]{2,1,0:T(8,128)(2,1)S(1)}, u32[]{:S(2)}, u32[]{:S(2)}) collective-permute-start(bf16[2,136,256]{2,1,0:T(8,128)(2,1)S(1)} %collective-permute-done.3.refs_2_.next_ref), channel_id=1, source_target_pairs={{0,1},{1,0},{2,3},{3,2},{4,5},{5,4},{6,7},{7,6},{8,9},{9,8},{10,11... | collective-permute-start | bytes 417800 | tf_op jit(solution)/shard_map/ppermute | solution.py:199
  13.4 2.9 %collective-permute-done.5.refs_4_ = bf16[2,136,256]{2,1,0:T(8,128)(2,1)S(1)} collective-permute-done((bf16[2,136,256]{2,1,0:T(8,128)(2,1)S(1)}, bf16[2,136,256]{2,1,0:T(8,128)(2,1)S(1)}, u32[]{:S(2)}, u32[]{:S(2)}) %collective-permute-start.5) | collective-permute-done | bytes 139296 | tf_op jit(solution)/shard_map/ppermute | solution.py:198
  16.3 1.5 %collective-permute-start.6 = (bf16[2,136,256]{2,1,0:T(8,128)(2,1)S(1)}, bf16[2,136,256]{2,1,0:T(8,128)(2,1)S(1)}, u32[]{:S(2)}, u32[]{:S(2)}) collective-permute-start(bf16[2,136,256]{2,1,0:T(8,128)(2,1)S(1)} %collective-permute-done.5.refs_4_), channel_id=1, source_target_pairs={{0,1},{1,0},{2,3},{3,2},{4,5},{5,4},{6,7},{7,6},{8,9},{9,8},{10,11... | collective-permute-start | bytes 417800 | tf_op jit(solution)/shard_map/ppermute | solution.py:199
  17.8 2.0 %collective-permute-done.refs_0_ = bf16[2,136,256]{2,1,0:T(8,128)(2,1)S(1)} collective-permute-done((bf16[2,136,256]{2,1,0:T(8,128)(2,1)S(1)}, bf16[2,136,256]{2,1,0:T(8,128)(2,1)S(1)}, u32[]{:S(2)}, u32[]{:S(2)}) %collective-permute-start) | collective-permute-done | bytes 139296 | tf_op jit(solution)/shard_map/ppermute | solution.py:198
  19.8 1.5 %collective-permute-start.1 = (bf16[2,136,256]{2,1,0:T(8,128)(2,1)S(1)}, bf16[2,136,256]{2,1,0:T(8,128)(2,1)S(1)}, u32[]{:S(2)}, u32[]{:S(2)}) collective-permute-start(bf16[2,136,256]{2,1,0:T(8,128)(2,1)S(1)} %collective-permute-done.refs_0_), channel_id=1, source_target_pairs={{0,1},{1,0},{2,3},{3,2},{4,5},{5,4},{6,7},{7,6},{8,9},{9,8},{10,11... | collective-permute-start | bytes 417800 | tf_op jit(solution)/shard_map/ppermute | solution.py:199
  21.3 0.0 collective-permute-done.2.refs_1_.other_ref
  21.3 0.0 collective-permute-done.4.refs_3_.next_other_ref
  21.3 0.0 collective-permute-done.6.refs_5_
  21.3 0.9 %shard_map.51 = (bf16[10,576,256]{2,1,0:T(8,128)(2,1)S(1)}, bf16[8,2,128,256]{3,2,1,0:T(8,128)(2,1)S(1)}, bf16[128,4608]{1,0:T(8,128)(2,1)S(1)}) custom-call(bf16[2,136,256]{2,1,0:T(8,128)(2,1)S(1)} %get-tuple-element.32.refs_0_.own_ref, bf16[2,136,256]{2,1,0:T(8,128)(2,1)S(1)} %collective-permute-done.2.refs_1_.other_ref, ...), custom_call_target="tpu_custom_call" | custom-call | tf_op jit(solution)/shard_map/pallas_call | solution.py:209
  22.2 2.7 %collective-permute-done.1.refs_1_ = bf16[2,136,256]{2,1,0:T(8,128)(2,1)S(1)} collective-permute-done((bf16[2,136,256]{2,1,0:T(8,128)(2,1)S(1)}, bf16[2,136,256]{2,1,0:T(8,128)(2,1)S(1)}, u32[]{:S(2)}, u32[]{:S(2)}) %collective-permute-start.1) | collective-permute-done | bytes 139296 | tf_op jit(solution)/shard_map/ppermute | solution.py:199
  24.9 0.4 %shard_map.52 = (bf16[10,576,256]{2,1,0:T(8,128)(2,1)S(1)}, bf16[8,2,128,256]{3,2,1,0:T(8,128)(2,1)S(1)}, bf16[128,4608]{1,0:T(8,128)(2,1)S(1)}) custom-call(bf16[2,136,256]{2,1,0:T(8,128)(2,1)S(1)} %collective-permute-done.refs_0_, ...), custom_call_target="tpu_custom_call", output_to_operand_aliasing={{0}: (2, {}), {1}: (3, {}), {2}: (4, {})} | custom-call | tf_op jit(solution)/shard_map/pallas_call | solution.py:209
  25.3 1.1 %shard_map.53 = (f32[432,256]{1,0:T(8,128)S(1)}, f32[432,256]{1,0:T(8,128)S(1)}) custom-call(bf16[10,576,256]{2,1,0:T(8,128)(2,1)S(1)} %get-tuple-element.33.win_ref, bf16[8,2,128,256]{3,2,1,0:T(8,128)(2,1)S(1)} %get-tuple-element.29.grad_ref), custom_call_target="tpu_custom_call" | custom-call | flops 1 | bytes 1 | tf_op jit(solution)/shard_map/pallas_call | solution.py:225
  26.4 0.1 collective-permute-start.7
  26.5 1.8 %collective-permute-done.7 = f32[432,256]{1,0:T(8,128)S(1)} collective-permute-done((f32[432,256]{1,0:T(8,128)S(1)}, f32[432,256]{1,0:T(8,128)S(1)}, u32[]{:S(2)}, u32[]{:S(2)}) %collective-permute-start.7) | collective-permute-done | bytes 442400 | tf_op jit(solution)/shard_map/ppermute | solution.py:235
  28.2 0.0 slice-start
  28.2 0.1 add.15
  28.3 1.6 %collective-permute-start.11 = (f32[432,256]{1,0:T(8,128)S(1)}, f32[432,256]{1,0:T(8,128)S(1)}, u32[]{:S(2)}, u32[]{:S(2)}) collective-permute-start(f32[432,256]{1,0:T(8,128)S(1)} %add.15), channel_id=1, source_target_pairs={{0,16},{8,24},{16,0},{24,8},{1,17},{9,25},{17,1},{25,9},{2,18},{10... | collective-permute-start | bytes 1327112 | tf_op jit(solution)/shard_map/ppermute | solution.py:239
  29.9 0.5 %shard_map.57 = (f32[144,256]{1,0:T(8,128)S(1)}, f32[144,256]{1,0:T(8,128)S(1)}) custom-call(bf16[10,576,256]{2,1,0:T(8,128)(2,1)S(1)} %get-tuple-element.33.win_ref, bf16[8,2,128,256]{3,2,1,0:T(8,128)(2,1)S(1)} %get-tuple-element.29.grad_ref), custom_call_target="tpu_custom_call" | custom-call | flops 1 | bytes 1 | tf_op jit(solution)/shard_map/pallas_call | solution.py:225
  30.4 0.0 slice-start.1
  30.4 0.1 collective-permute-start.10
  30.4 0.5 %shard_map.56 = (f32[144,256]{1,0:T(8,128)S(1)}, f32[144,256]{1,0:T(8,128)S(1)}) custom-call(bf16[10,576,256]{2,1,0:T(8,128)(2,1)S(1)} %get-tuple-element.33.win_ref, bf16[8,2,128,256]{3,2,1,0:T(8,128)(2,1)S(1)} %get-tuple-element.29.grad_ref), custom_call_target="tpu_custom_call" | custom-call | flops 1 | bytes 1 | tf_op jit(solution)/shard_map/pallas_call | solution.py:225
  30.9 0.6 %collective-permute-start.9 = (f32[144,256]{1,0:T(8,128)S(1)}, f32[144,256]{1,0:T(8,128)S(1)}, u32[]{:S(2)}, u32[]{:S(2)}) collective-permute-start(f32[144,256]{1,0:T(8,128)S(1)} %get-tuple-element.37), channel_id=1, source_target_pairs={{0,8},{8,0},{16,24},{24,16},{1,9},{9,1},{17,25},{25,17},{2,10},{10... | collective-permute-start | bytes 442376 | tf_op jit(solution)/shard_map/ppermute | solution.py:235
  31.5 0.5 %shard_map.55 = (f32[144,256]{1,0:T(8,128)S(1)}, f32[144,256]{1,0:T(8,128)S(1)}) custom-call(bf16[10,576,256]{2,1,0:T(8,128)(2,1)S(1)} %get-tuple-element.33.win_ref, bf16[8,2,128,256]{3,2,1,0:T(8,128)(2,1)S(1)} %get-tuple-element.29.grad_ref), custom_call_target="tpu_custom_call" | custom-call | flops 1 | bytes 1 | tf_op jit(solution)/shard_map/pallas_call | solution.py:225
  32.0 0.1 collective-permute-start.8
  32.0 0.0 slice-done
  32.0 0.1 slice-done.1
  32.2 3.1 %shard_map.54 = bf16[2,30,512]{2,1,0:T(8,128)(2,1)S(1)} custom-call(bf16[2,136,256]{2,1,0:T(8,128)(2,1)S(1)} %get-tuple-element.32.refs_0_.own_ref, bf16[2,136,256]{2,1,0:T(8,128)(2,1)S(1)} %collective-permute-done.2.refs_1_.other_ref, bf16[2,136,256]{2,1,0:T(8,128)(2,1)S(1)} %collective-permute-done.3.refs_2_.next_ref, ...), custom_call_target="tpu_custom_call" | custom-call | flops 1 | bytes 1 | tf_op jit(solution)/shard_map/pallas_call | solution.py:242
  35.3 0.7 %copy.8 = bf16[1,2,1,30,512]{4,1,3,2,0:T(2,128)(2,1)} copy(bf16[1,2,1,30,512]{4,3,1,2,0:T(8,128)(2,1)S(1)} %bitcast.14) | data formatting | bytes 122880
  36.0 0.0 collective-permute-done.10
  36.0 0.0 collective-permute-done.9
  36.1 0.0 collective-permute-done.8
  36.1 4.5 %collective-permute-done.11 = f32[432,256]{1,0:T(8,128)S(1)} collective-permute-done((f32[432,256]{1,0:T(8,128)S(1)}, f32[432,256]{1,0:T(8,128)S(1)}, u32[]{:S(2)}, u32[]{:S(2)}) %collective-permute-start.11) | collective-permute-done | bytes 442400 | tf_op jit(solution)/shard_map/ppermute | solution.py:239
  40.6 0.8 %fusion = f32[432,256]{1,0:T(8,128)} fusion(f32[432,256]{1,0:T(8,128)S(1)} %collective-permute-done.11, f32[144,256]{1,0:T(8,128)S(1)} %add.18, f32[144,256]{1,0:T(8,128)S(1)} %add.17, f32[144,256]{1,0:T(8,128)S(1)} %add.16), kind=kLoop, calls=%fused_computation.1 | loop fusion | flops 442368 | bytes 1327104 | tf_op jit(solution)/shard_map/mul | solution.py:262
  (4 shorter events, 0.1 us)
Async XLA Ops:
  2.7 9.2 %collective-permute-start.3 = (bf16[2,136,256]{2,1,0:T(8,128)(2,1)S(1)}, bf16[2,136,256]{2,1,0:T(8,128)(2,1)S(1)}, u32[]{:S(2)}, u32[]{:S(2)}) collective-permute-start(bf16[2,136,256]{2,1,0:T(8,128)(2,1)S(1)} %get-tuple-element.23), channel_id=1, source_target_pairs={{0,6},{2,0},{4,2},{6,4},{1,7},{3,1},{5,3},{7,5},{8,14},{10,8},{12,... | collective-permute-start | bytes 417800 | tf_op jit(solution)/shard_map/ppermute | solution.py:198
  7.8 8.5 %collective-permute-start.5 = (bf16[2,136,256]{2,1,0:T(8,128)(2,1)S(1)}, bf16[2,136,256]{2,1,0:T(8,128)(2,1)S(1)}, u32[]{:S(2)}, u32[]{:S(2)}) collective-permute-start(bf16[2,136,256]{2,1,0:T(8,128)(2,1)S(1)} %get-tuple-element.24), channel_id=1, source_target_pairs={{0,2},{2,4},{4,6},{6,0},{1,3},{3,5},{5,7},{7,1},{8,10},{10,12},{12... | collective-permute-start | bytes 417800 | tf_op jit(solution)/shard_map/ppermute | solution.py:198
  7.8 12.0 %collective-permute-start = (bf16[2,136,256]{2,1,0:T(8,128)(2,1)S(1)}, bf16[2,136,256]{2,1,0:T(8,128)(2,1)S(1)}, u32[]{:S(2)}, u32[]{:S(2)}) collective-permute-start(bf16[2,136,256]{2,1,0:T(8,128)(2,1)S(1)} %get-tuple-element.21), channel_id=1, source_target_pairs={{0,4},{2,6},{4,0},{6,2},{1,5},{3,7},{5,1},{7,3},{8,12},{10,14},{12... | collective-permute-start | bytes 417800 | tf_op jit(solution)/shard_map/ppermute | solution.py:198
  8.8 12.5 %collective-permute-start.2 = (bf16[2,136,256]{2,1,0:T(8,128)(2,1)S(1)}, bf16[2,136,256]{2,1,0:T(8,128)(2,1)S(1)}, u32[]{:S(2)}, u32[]{:S(2)}) collective-permute-start(bf16[2,136,256]{2,1,0:T(8,128)(2,1)S(1)} %get-tuple-element.32.refs_0_.own_ref), channel_id=1, source_target_pairs={{0,1},{1,0},{2,3},{3,2},{4,5},{5,4},{6,7},{7,6},{8,9},{9,8},{10,11... | collective-permute-start | bytes 417800 | tf_op jit(solution)/shard_map/ppermute | solution.py:199
  11.9 9.4 %collective-permute-start.4 = (bf16[2,136,256]{2,1,0:T(8,128)(2,1)S(1)}, bf16[2,136,256]{2,1,0:T(8,128)(2,1)S(1)}, u32[]{:S(2)}, u32[]{:S(2)}) collective-permute-start(bf16[2,136,256]{2,1,0:T(8,128)(2,1)S(1)} %collective-permute-done.3.refs_2_.next_ref), channel_id=1, source_target_pairs={{0,1},{1,0},{2,3},{3,2},{4,5},{5,4},{6,7},{7,6},{8,9},{9,8},{10,11... | collective-permute-start | bytes 417800 | tf_op jit(solution)/shard_map/ppermute | solution.py:199
  16.3 5.1 %collective-permute-start.6 = (bf16[2,136,256]{2,1,0:T(8,128)(2,1)S(1)}, bf16[2,136,256]{2,1,0:T(8,128)(2,1)S(1)}, u32[]{:S(2)}, u32[]{:S(2)}) collective-permute-start(bf16[2,136,256]{2,1,0:T(8,128)(2,1)S(1)} %collective-permute-done.5.refs_4_), channel_id=1, source_target_pairs={{0,1},{1,0},{2,3},{3,2},{4,5},{5,4},{6,7},{7,6},{8,9},{9,8},{10,11... | collective-permute-start | bytes 417800 | tf_op jit(solution)/shard_map/ppermute | solution.py:199
  19.8 5.1 %collective-permute-start.1 = (bf16[2,136,256]{2,1,0:T(8,128)(2,1)S(1)}, bf16[2,136,256]{2,1,0:T(8,128)(2,1)S(1)}, u32[]{:S(2)}, u32[]{:S(2)}) collective-permute-start(bf16[2,136,256]{2,1,0:T(8,128)(2,1)S(1)} %collective-permute-done.refs_0_), channel_id=1, source_target_pairs={{0,1},{1,0},{2,3},{3,2},{4,5},{5,4},{6,7},{7,6},{8,9},{9,8},{10,11... | collective-permute-start | bytes 417800 | tf_op jit(solution)/shard_map/ppermute | solution.py:199
  26.4 1.9 %collective-permute-start.7 = (f32[432,256]{1,0:T(8,128)S(1)}, f32[432,256]{1,0:T(8,128)S(1)}, u32[]{:S(2)}, u32[]{:S(2)}) collective-permute-start(f32[432,256]{1,0:T(8,128)S(1)} %get-tuple-element.31), channel_id=1, source_target_pairs={{0,8},{8,0},{16,24},{24,16},{1,9},{9,1},{17,25},{25,17},{2,10},{10... | collective-permute-start | bytes 1327112 | tf_op jit(solution)/shard_map/ppermute | solution.py:235
  28.2 3.8 %slice-start = ((s8[7077888]{0:T(1024)(128)(4,1)}), s8[4194304]{0:T(1024)(128)(4,1)S(1)}, s32[]{:S(2)}) async-start(s8[7077888]{0:T(1024)(128)(4,1)} %bitcast.11), calls=%async_computation | async-start | bytes 8388608
  28.3 12.3 %collective-permute-start.11 = (f32[432,256]{1,0:T(8,128)S(1)}, f32[432,256]{1,0:T(8,128)S(1)}, u32[]{:S(2)}, u32[]{:S(2)}) collective-permute-start(f32[432,256]{1,0:T(8,128)S(1)} %add.15), channel_id=1, source_target_pairs={{0,16},{8,24},{16,0},{24,8},{1,17},{9,25},{17,1},{25,9},{2,18},{10... | collective-permute-start | bytes 1327112 | tf_op jit(solution)/shard_map/ppermute | solution.py:239
  30.4 1.8 %slice-start.1 = ((s8[7077888]{0:T(1024)(128)(4,1)}), s8[2883584]{0:T(1024)(128)(4,1)S(1)}, s32[]{:S(2)}) async-start(s8[7077888]{0:T(1024)(128)(4,1)} %bitcast.11), calls=%async_computation.1 | async-start | bytes 5767168
  30.4 5.6 %collective-permute-start.10 = (f32[144,256]{1,0:T(8,128)S(1)}, f32[144,256]{1,0:T(8,128)S(1)}, u32[]{:S(2)}, u32[]{:S(2)}) collective-permute-start(f32[144,256]{1,0:T(8,128)S(1)} %get-tuple-element.39), channel_id=1, source_target_pairs={{0,8},{8,0},{16,24},{24,16},{1,9},{9,1},{17,25},{25,17},{2,10},{10... | collective-permute-start | bytes 442376 | tf_op jit(solution)/shard_map/ppermute | solution.py:235
  30.9 5.1 %collective-permute-start.9 = (f32[144,256]{1,0:T(8,128)S(1)}, f32[144,256]{1,0:T(8,128)S(1)}, u32[]{:S(2)}, u32[]{:S(2)}) collective-permute-start(f32[144,256]{1,0:T(8,128)S(1)} %get-tuple-element.37), channel_id=1, source_target_pairs={{0,8},{8,0},{16,24},{24,16},{1,9},{9,1},{17,25},{25,17},{2,10},{10... | collective-permute-start | bytes 442376 | tf_op jit(solution)/shard_map/ppermute | solution.py:235
  32.0 4.1 %collective-permute-start.8 = (f32[144,256]{1,0:T(8,128)S(1)}, f32[144,256]{1,0:T(8,128)S(1)}, u32[]{:S(2)}, u32[]{:S(2)}) collective-permute-start(f32[144,256]{1,0:T(8,128)S(1)} %get-tuple-element.35), channel_id=1, source_target_pairs={{0,8},{8,0},{16,24},{24,16},{1,9},{9,1},{17,25},{25,17},{2,10},{10... | collective-permute-start | bytes 442376 | tf_op jit(solution)/shard_map/ppermute | solution.py:235

commit v3 on v2

--- a/solution.py
+++ b/solution.py
@@ -31,9 +31,8 @@
 MESSAGE_ROWS = LATENT_ROWS + 120
 
 
-def message_kernel(tm, share, lat_ref, grad_ref, *refs):
-    outs, wide_ref = refs[:tm], refs[tm]
-    channels = lat_ref.shape[1]
+def select_kernel(tm, share, lat_ref, wide_ref):
+    channels = lat_ref.shape[2]
     me_dp, me_tm, me_rows = lax.axis_index("dp"), lax.axis_index("tm"), lax.axis_index("rows")
     col = lax.broadcasted_iota(jnp.int32, (1, channels), 1)
     inner = col % share
@@ -46,15 +45,19 @@
     wanted = ((dp * tm + (shift + me_tm) % tm) * 2 + rows) * share + inner
     row = lax.broadcasted_iota(jnp.int32, (channels, channels), 0)
     pick = jnp.where(row == wanted, 1.0, 0.0).astype(jnp.bfloat16)
-    wide_ref[48:64, :] = jnp.zeros((16, channels), jnp.float32)
-    wide_ref[0:60, :] = jnp.dot(lat_ref[...], pick, preferred_element_type=jnp.float32)
+    wide_ref[56:64, :] = jnp.zeros((8, channels), jnp.float32)
+    wide_ref[0:60, :] = jnp.dot(lat_ref[...].reshape(60, channels), pick, preferred_element_type=jnp.float32)
+
+
+def message_kernel(tm, wide_ref, grad_ref, *outs):
+    grads = [grad_ref[f].reshape(120, grad_ref.shape[3]) for f in range(2)]
     for k in range(tm):
         for part in range(4):
-            piece = wide_ref[16 * part : 16 * part + 16, 128 * k : 128 * k + 128]
+            piece = wide_ref[16 * part : 16 * part + 16, 128 * k : 128 * k + 128].astype(jnp.bfloat16)
             lanes = slice(128 * (part % 2), 128 * (part % 2) + 128)
-            outs[k][part // 2, 0:LATENT_ROWS, lanes] = piece.astype(jnp.bfloat16)
+            outs[k][part // 2, 0:LATENT_ROWS, lanes] = piece
         for f in range(2):
-            outs[k][f, LATENT_ROWS:, :] = grad_ref[f]
+            outs[k][f, LATENT_ROWS:, :] = grads[f]
 
 
 def arrange_kernel(tm, share, shifts, *refs):
@@ -83,8 +86,8 @@
         for half, rows in enumerate((me_rows, 1 - me_rows)):
             block = blocks[2 * n + half]
             for part in range(4):
-                lanes = 128 * (part % 2) + group * half
-                piece = block[part // 2, 0:LATENT_ROWS, lanes : lanes + group]
+                lanes = slice(128 * (part % 2) + group * half, 128 * (part % 2) + group * (half + 1))
+                piece = block[part // 2, 0:LATENT_ROWS, lanes]
                 lat_ref[n, rows, 16 * part : 16 * part + 16, :] = piece.astype(jnp.float32)
             for f in range(2):
                 grad_ref[2 * t + f, rows, 112:128, :] = jnp.zeros((16, grad_ref.shape[3]), jnp.bfloat16)
@@ -104,16 +107,35 @@
                     win_ref[2 * t + f + 2, dst : dst + share, :] = wide[src : src + share]
 
 
-def terms_kernel(first, taps, frames, win_ref, grad_ref, send_ref, keep_ref):
-    rows = send_ref.shape[0] // len(taps)
-    for n, a in enumerate(taps):
-        for ref, start in ((send_ref, first), (keep_ref, first + rows)):
-            total = None
-            for f in range(frames):
-                g = grad_ref[f].reshape(256, grad_ref.shape[3])
-                term = jnp.dot(win_ref[f + a, start : start + rows, :], g, preferred_element_type=jnp.float32)
-                total = term if total is None else total + term
-            ref[n * rows : (n + 1) * rows] = total
+def terms_kernel(first, taps, frames, outs, win_ref, grad_ref, *out_refs):
+    each = len(out_refs) // outs
+    rows = out_refs[0].shape[0] * each // len(taps)
+    span = slice(first, first + rows * outs)
+    total = None
+    for f in range(frames):
+        grad = grad_ref[f].reshape(256, grad_ref.shape[3])
+        lhs = jnp.concatenate([win_ref[f + a, span, :] for a in taps], axis=0)
+        term = jnp.dot(lhs, grad, preferred_element_type=jnp.float32)
+        total = term if total is None else total + term
+    for n in range(len(taps)):
+        for m in range(outs):
+            start = (n * outs + m) * rows
+            ref = out_refs[m * each + n % each]
+            place = n // each * rows
+            ref[place : place + rows] = total[start : start + rows]
+
+
+TOP_EXPONENT = 14
+EXPONENT_ROWS = 16
+
+
+def pack_kernel(keep_ref, received_ref, out_ref):
+    rows = keep_ref.shape[0]
+    total = keep_ref[...] + received_ref[...]
+    top = jnp.max(jnp.max(jnp.abs(total), axis=0, keepdims=True), axis=1, keepdims=True)
+    exponent = jnp.floor(jnp.log2(jnp.maximum(top, 2.0**-100))) - TOP_EXPONENT
+    out_ref[0:rows] = total * jnp.exp2(-exponent)
+    out_ref[rows:] = jnp.broadcast_to(exponent, (EXPONENT_ROWS, out_ref.shape[1]))
 
 
 def latents_kernel(tm, own_ref, other_ref, next_ref, next_other_ref, kernel_ref, out_ref, wide_ref, pool_ref, total_ref):
@@ -183,20 +205,26 @@
     factor = float(devices * 240) ** (-0.5)
     swap = [(0, 1), (1, 0)]
 
-    mine = jnp.transpose(grad_out[0], (0, 2, 1, 3)).reshape(2, 120, outputs)
-    lat = jnp.transpose(latents[0, :, 0], (1, 0, 2)).reshape(60, channels)
+    mine = jnp.transpose(grad_out[0], (0, 2, 1, 3))
+    lat = jnp.transpose(latents[0, :, 0], (1, 0, 2))
     message = jax.ShapeDtypeStruct((2, MESSAGE_ROWS, outputs), jnp.bfloat16)
+    selected = pl.pallas_call(
+        functools.partial(select_kernel, tm, share),
+        out_shape=jax.ShapeDtypeStruct((64, channels), jnp.float32),
+        in_specs=whole(1),
+        out_specs=whole(1)[0],
+        compiler_params=params(),
+    )(lat)
     messages = pl.pallas_call(
-        functools.partial(message_kernel, tm, share),
+        functools.partial(message_kernel, tm),
         out_shape=tuple([message] * tm),
         in_specs=whole(2),
         out_specs=tuple(whole(tm)),
-        scratch_shapes=[pltpu.VMEM((64, channels), jnp.float32)],
         compiler_params=params(),
-    )(lat, mine)
+    )(selected, mine)
     order = [0, tm - 1] + list(range(1, tm - 1))
-    shifted = {k: lax.ppermute(messages[k], "tm", cycle(tm, k)) if k else messages[0] for k in order}
-    across = {k: lax.ppermute(shifted[k], "rows", swap) for k in order}
+    shifted = [lax.ppermute(messages[k], "tm", cycle(tm, k)) if k else messages[0] for k in order]
+    across = [lax.ppermute(block, "rows", swap) for block in shifted]
 
     arranged = (
         jax.ShapeDtypeStruct((frames + 2, 36 * share, 256), jnp.bfloat16),
@@ -204,29 +232,31 @@
         jax.ShapeDtypeStruct((128, 18 * 256), jnp.bfloat16),
     )
 
-    def arrange(shifts, earlier):
-        blocks = [block for k in shifts for block in (shifted[k], across[k])]
+    def arrange(first, last, earlier):
+        blocks = [block for n in range(first, last) for block in (shifted[n], across[n])]
         return pl.pallas_call(
-            functools.partial(arrange_kernel, tm, share, tuple(shifts)),
+            functools.partial(arrange_kernel, tm, share, tuple(order[first:last])),
             out_shape=arranged,
             in_specs=whole(len(blocks) + len(earlier)),
             out_specs=tuple(whole(3)),
-            scratch_shapes=[pltpu.VMEM((len(shifts), 2, 64, 4 * share), jnp.float32)],
+            scratch_shapes=[pltpu.VMEM((last - first, 2, 64, 4 * share), jnp.float32)],
             input_output_aliases={len(blocks) + n: n for n in range(len(earlier))},
             compiler_params=params(),
+            cost_estimate=light(),
         )(*blocks, *earlier)
 
-    early = arrange(order[:-1], ())
-    windows, grads, _ = arrange(order[-1:], early)
+    early = arrange(0, tm - 1, ())
+    windows, grads, _ = arrange(tm - 1, tm, early)
 
     rows = 9 * share
 
-    def terms(first, taps, windows):
+    def terms(first, windows, outs, each):
+        out = jax.ShapeDtypeStruct((3 // each * rows, outputs), jnp.float32)
         return pl.pallas_call(
-            functools.partial(terms_kernel, first, taps, frames),
-            out_shape=tuple([jax.ShapeDtypeStruct((len(taps) * rows, outputs), jnp.float32)] * 2),
+            functools.partial(terms_kernel, first, (0, 1, 2), frames, outs),
+            out_shape=tuple([out] * (outs * each)),
             in_specs=whole(2),
-            out_specs=tuple(whole(2)),
+            out_specs=tuple(whole(outs * each)),
             compiler_params=params(),
             cost_estimate=light(),
         )(windows, grads)
@@ -234,9 +264,20 @@
     def other_core(block):
         return lax.ppermute(block, "dp", [(i, i ^ 1) for i in range(4)])
 
-    send, keep = terms(0, (0, 1, 2), windows)
-    chip = keep + other_core(send)
-    crossed = lax.ppermute(chip, "dp", [(i, i ^ 2) for i in range(4)])
+    (send,) = terms(0, windows, 1, 1)
+    after, _ = lax.optimization_barrier((windows, send))
+    (keep,) = terms(rows, after, 1, 1)
+    chip = pl.pallas_call(
+        pack_kernel,
+        out_shape=jax.ShapeDtypeStruct((3 * rows + EXPONENT_ROWS, outputs), jnp.float32),
+        in_specs=whole(2),
+        out_specs=whole(1)[0],
+        compiler_params=params(),
+        cost_estimate=light(),
+    )(keep, other_core(send))
+    chip = chip.astype(jnp.float16)
+    crossed = lax.ppermute(chip, "dp", [(i, i ^ 2) for i in range(4)]).astype(jnp.float32)
+    crossed = crossed[: 3 * rows] * (jnp.exp2(crossed[3 * rows : 3 * rows + 1]) * factor)
     windows, first, *_ = lax.optimization_barrier((windows, shifted[0], chip))
     taps = kernel.reshape(27, channels, outputs)
     grad_latents = pl.pallas_call(
@@ -253,13 +294,11 @@
         ],
         compiler_params=params(),
         cost_estimate=light(),
-    )(first, across[0], shifted[tm - 1], across[tm - 1], taps)
-
-    stay = []
-    for a in range(3):
-        send, keep = terms(2 * rows, (a,), windows)
-        stay.append(keep + other_core(send))
-    total = (jnp.concatenate(stay) + crossed) * factor
+    )(first, across[0], shifted[1], across[1], taps)
+
+    parts = terms(2 * rows, windows, 2, 3)
+    stay = [keep + other_core(send) for send, keep in zip(parts[:3], parts[3:])]
+    total = jnp.concatenate(stay) * factor + crossed
     weight_grad = jnp.transpose(total.reshape(3, 3, 3, share, outputs), (3, 0, 1, 2, 4))
     return (grad_latents.reshape(latents.shape), weight_grad)
 
@@ -350,7 +389,7 @@
 
 def body(latents, grad_out, kernel):
     share = latents.shape[4] // (lax.axis_size("dp") * lax.axis_size("tm") * lax.axis_size("rows"))
-    narrow = lax.axis_size("rows") == 2 and lax.axis_size("dp") == 4 and share == 16
+    narrow = lax.axis_size("rows") == 2 and lax.axis_size("dp") == 4 and lax.axis_size("tm") > 2 and share == 16
     return (narrow_body if narrow else wide_body)(latents, grad_out, kernel)
 
 

time: 41.6 us -> 36.8 us (0.88)
  waiting for transfers between devices: 15.4 us -> 10.8 us
    ppermute x5, waiting for transfers between devices: 7.16 us -> 3.18 us  [the longest x4 2.67 us: narrow_body(): across = [lax.ppermute(block, 'rows', swap) for block in shifted]]
    reshape x2 -> x0, local copies, waits for them, and re-layouts: 1.82 us -> none  [the longest x1 0.96 us: narrow_body(): mine = jnp.transpose(grad_out[0], (0, 2, 1, 3)).reshape(2, 120, outputs)]
    unnamed x5 -> x9, local copies, waits for them, and re-layouts: 0.85 us -> 2.42 us
    mul x1, other arithmetic: 0.82 us -> 0.01 us  [narrow_body(): jnp.exp2(crossed[3 * rows:3 * rows + 1]) * factor]
    add x4, other arithmetic: 0.12 us -> 0.88 us  [the longest x1 0.82 us: narrow_body(): total = jnp.concatenate(stay) * factor + crossed]
    ppermute x4, waiting for transfers between devices: 1.79 us -> 1.16 us  [other_core(): return lax.ppermute(block, 'dp', [(i, i ^ 1) for i in range(4)])]
    pallas_call x7 -> x8, Pallas kernels: 4.01 us -> 4.08 us  [the longest x3 2.32 us: terms(): pl.pallas_call(functools.partial(terms_kernel, first, (0, 1, 2), frames,...]
  transfers between devices with their start and end apart: 12 -> 12, of which waited for: 6 -> 6; matrix products, arithmetic and copies ran while one was open for 2% -> 2% of each run, Pallas kernels for 13% -> 15%
where the time goes in v3:
time: 36.8 us; the launch traced here: 36.6 us
  starting transfers between devices  14.5 us (39%)
  waiting for transfers between devices  10.8 us (29%)
  Pallas kernels  7.19 us (20%)
  local copies, waits for them, and re-layouts  2.42 us (7%)
  other arithmetic  0.95 us (3%)
  between operations  0.81 us (2%)
    ppermute x3, waiting for transfers between devices, narrow_body(): lax.ppermute(messages[k], 'tm', cycle(tm, k))  6.43 us
    ppermute x3, starting transfers between devices, narrow_body(): lax.ppermute(messages[k], 'tm', cycle(tm, k))  6.12 us
    ppermute x4, starting transfers between devices, narrow_body(): across = [lax.ppermute(block, 'rows', swap) for block in shifted]  6.07 us
    pallas_call x1, Pallas kernels, narrow_body(): pl.pallas_call(functools.partial(latents_kernel, tm), grid=(3,), out_shap...  3.11 us
    ppermute x4, waiting for transfers between devices, narrow_body(): across = [lax.ppermute(block, 'rows', swap) for block in shifted]  2.67 us
    unnamed x9, local copies, waits for them, and re-layouts  2.42 us
    pallas_call x3, Pallas kernels, terms(): pl.pallas_call(functools.partial(terms_kernel, first, (0, 1, 2), frames,...  2.32 us
    ppermute x1, starting transfers between devices, narrow_body(): lax.ppermute(chip, 'dp', [(i, i ^ 2) for i in range(4)]).astype(jnp.float32)  1.55 us
  transfers between devices with their start and end apart: 12, of which 6 were waited for; matrix products, arithmetic and copies ran while one was open for 2% of the time, Pallas kernels for 15%

profile of v3, /device:TPU:0, one launch (start us, length us, event | category | flops | bytes accessed | tf_op | source)
XLA Modules:
  0.0 36.6 jit_solution(5817525831710389508)
XLA Ops:
  0.6 0.0 copy-start.1
  0.6 0.8 %copy-done.1 = bf16[1,2,1,30,512]{4,1,3,2,0:T(2,128)(2,1)S(1)} copy-done((bf16[1,2,1,30,512]{4,1,3,2,0:T(2,128)(2,1)S(1)}, bf16[1,2,1,30,512]{4,1,3,2,0:T(2,128)(2,1)}, u32[]{:S(2)}) %copy-start.1) | copy-done | bytes 61464
  1.5 0.2 shard_map.50.wide_ref
  1.7 0.0 copy-start
  1.7 0.9 %copy-done = bf16[1,2,2,60,256]{4,2,3,1,0:T(2,128)(2,1)S(1)} copy-done((bf16[1,2,2,60,256]{4,2,3,1,0:T(2,128)(2,1)S(1)}, bf16[1,2,2,60,256]{4,2,3,1,0:T(2,128)(2,1)}, u32[]{:S(2)}) %copy-start) | copy-done | bytes 122904
  2.6 0.1 shard_map.51
  2.7 5.1 %collective-permute-start.3 = (bf16[2,136,256]{2,1,0:T(8,128)(2,1)S(1)}, bf16[2,136,256]{2,1,0:T(8,128)(2,1)S(1)}, u32[]{:S(2)}, u32[]{:S(2)}) collective-permute-start(bf16[2,136,256]{2,1,0:T(8,128)(2,1)S(1)} %get-tuple-element.22), channel_id=1, source_target_pairs={{0,6},{2,0},{4,2},{6,4},{1,7},{3,1},{5,3},{7,5},{8,14},{10,8},{12,... | collective-permute-start | bytes 417800 | tf_op jit(solution)/shard_map/ppermute | solution.py:226
  7.8 0.0 collective-permute-start.5
  7.8 1.0 %collective-permute-start = (bf16[2,136,256]{2,1,0:T(8,128)(2,1)S(1)}, bf16[2,136,256]{2,1,0:T(8,128)(2,1)S(1)}, u32[]{:S(2)}, u32[]{:S(2)}) collective-permute-start(bf16[2,136,256]{2,1,0:T(8,128)(2,1)S(1)} %get-tuple-element.20), channel_id=1, source_target_pairs={{0,4},{2,6},{4,0},{6,2},{1,5},{3,7},{5,1},{7,3},{8,12},{10,14},{12... | collective-permute-start | bytes 417800 | tf_op jit(solution)/shard_map/ppermute | solution.py:226
  8.8 1.5 %collective-permute-start.2 = (bf16[2,136,256]{2,1,0:T(8,128)(2,1)S(1)}, bf16[2,136,256]{2,1,0:T(8,128)(2,1)S(1)}, u32[]{:S(2)}, u32[]{:S(2)}) collective-permute-start(bf16[2,136,256]{2,1,0:T(8,128)(2,1)S(1)} %get-tuple-element.30.refs_0_.own_ref), channel_id=1, source_target_pairs={{0,1},{1,0},{2,3},{3,2},{4,5},{5,4},{6,7},{7,6},{8,9},{9,8},{10,11... | collective-permute-start | bytes 417800 | tf_op jit(solution)/shard_map/ppermute | solution.py:227
  10.3 1.5 %collective-permute-done.3.refs_2_.next_ref = bf16[2,136,256]{2,1,0:T(8,128)(2,1)S(1)} collective-permute-done((bf16[2,136,256]{2,1,0:T(8,128)(2,1)S(1)}, bf16[2,136,256]{2,1,0:T(8,128)(2,1)S(1)}, u32[]{:S(2)}, u32[]{:S(2)}) %collective-permute-start.3) | collective-permute-done | bytes 139296 | tf_op jit(solution)/shard_map/ppermute | solution.py:226
  11.9 1.5 %collective-permute-start.4 = (bf16[2,136,256]{2,1,0:T(8,128)(2,1)S(1)}, bf16[2,136,256]{2,1,0:T(8,128)(2,1)S(1)}, u32[]{:S(2)}, u32[]{:S(2)}) collective-permute-start(bf16[2,136,256]{2,1,0:T(8,128)(2,1)S(1)} %collective-permute-done.3.refs_2_.next_ref), channel_id=1, source_target_pairs={{0,1},{1,0},{2,3},{3,2},{4,5},{5,4},{6,7},{7,6},{8,9},{9,8},{10,11... | collective-permute-start | bytes 417800 | tf_op jit(solution)/shard_map/ppermute | solution.py:227
  13.4 2.9 %collective-permute-done.5.refs_4_ = bf16[2,136,256]{2,1,0:T(8,128)(2,1)S(1)} collective-permute-done((bf16[2,136,256]{2,1,0:T(8,128)(2,1)S(1)}, bf16[2,136,256]{2,1,0:T(8,128)(2,1)S(1)}, u32[]{:S(2)}, u32[]{:S(2)}) %collective-permute-start.5) | collective-permute-done | bytes 139296 | tf_op jit(solution)/shard_map/ppermute | solution.py:226
  16.2 1.5 %collective-permute-start.6 = (bf16[2,136,256]{2,1,0:T(8,128)(2,1)S(1)}, bf16[2,136,256]{2,1,0:T(8,128)(2,1)S(1)}, u32[]{:S(2)}, u32[]{:S(2)}) collective-permute-start(bf16[2,136,256]{2,1,0:T(8,128)(2,1)S(1)} %collective-permute-done.5.refs_4_), channel_id=1, source_target_pairs={{0,1},{1,0},{2,3},{3,2},{4,5},{5,4},{6,7},{7,6},{8,9},{9,8},{10,11... | collective-permute-start | bytes 417800 | tf_op jit(solution)/shard_map/ppermute | solution.py:227
  17.8 2.0 %collective-permute-done.refs_0_ = bf16[2,136,256]{2,1,0:T(8,128)(2,1)S(1)} collective-permute-done((bf16[2,136,256]{2,1,0:T(8,128)(2,1)S(1)}, bf16[2,136,256]{2,1,0:T(8,128)(2,1)S(1)}, u32[]{:S(2)}, u32[]{:S(2)}) %collective-permute-start) | collective-permute-done | bytes 139296 | tf_op jit(solution)/shard_map/ppermute | solution.py:226
  19.8 1.5 %collective-permute-start.1 = (bf16[2,136,256]{2,1,0:T(8,128)(2,1)S(1)}, bf16[2,136,256]{2,1,0:T(8,128)(2,1)S(1)}, u32[]{:S(2)}, u32[]{:S(2)}) collective-permute-start(bf16[2,136,256]{2,1,0:T(8,128)(2,1)S(1)} %collective-permute-done.refs_0_), channel_id=1, source_target_pairs={{0,1},{1,0},{2,3},{3,2},{4,5},{5,4},{6,7},{7,6},{8,9},{9,8},{10,11... | collective-permute-start | bytes 417800 | tf_op jit(solution)/shard_map/ppermute | solution.py:227
  21.3 0.0 collective-permute-done.2.refs_1_.other_ref
  21.3 0.0 collective-permute-done.4.refs_3_.next_other_ref
  21.3 0.0 collective-permute-done.6.refs_5_
  21.3 0.9 %shard_map.52 = (bf16[10,576,256]{2,1,0:T(8,128)(2,1)S(1)}, bf16[8,2,128,256]{3,2,1,0:T(8,128)(2,1)S(1)}, bf16[128,4608]{1,0:T(8,128)(2,1)S(1)}) custom-call(bf16[2,136,256]{2,1,0:T(8,128)(2,1)S(1)} %get-tuple-element.30.refs_0_.own_ref, bf16[2,136,256]{2,1,0:T(8,128)(2,1)S(1)} %collective-permute-done.2.refs_1_.other_ref, ...), custom_call_target="tpu_custom_call" | custom-call | flops 1 | bytes 1 | tf_op jit(solution)/shard_map/pallas_call | solution.py:237
  22.2 2.7 %collective-permute-done.1.refs_1_ = bf16[2,136,256]{2,1,0:T(8,128)(2,1)S(1)} collective-permute-done((bf16[2,136,256]{2,1,0:T(8,128)(2,1)S(1)}, bf16[2,136,256]{2,1,0:T(8,128)(2,1)S(1)}, u32[]{:S(2)}, u32[]{:S(2)}) %collective-permute-start.1) | collective-permute-done | bytes 139296 | tf_op jit(solution)/shard_map/ppermute | solution.py:227
  24.9 0.4 %shard_map.53 = (bf16[10,576,256]{2,1,0:T(8,128)(2,1)S(1)}, bf16[8,2,128,256]{3,2,1,0:T(8,128)(2,1)S(1)}, bf16[128,4608]{1,0:T(8,128)(2,1)S(1)}) custom-call(bf16[2,136,256]{2,1,0:T(8,128)(2,1)S(1)} %collective-permute-done.refs_0_, ...), custom_call_target="tpu_custom_call", output_to_operand_aliasing={{0}: (2, {}), {1}: (3, {}), {2}: (4, {})} | custom-call | flops 1 | bytes 1 | tf_op jit(solution)/shard_map/pallas_call | solution.py:237
  25.3 0.0 slice-start
  25.3 0.6 %shard_map.54 = f32[432,256]{1,0:T(8,128)S(1)} custom-call(bf16[10,576,256]{2,1,0:T(8,128)(2,1)S(1)} %get-tuple-element.31.win_ref, bf16[8,2,128,256]{3,2,1,0:T(8,128)(2,1)S(1)} %get-tuple-element.28.grad_ref), custom_call_target="tpu_custom_call" | custom-call | flops 1 | bytes 1 | tf_op jit(solution)/shard_map/pallas_call | solution.py:255
  25.9 0.0 slice-start.1
  25.9 0.1 collective-permute-start.7
  26.0 0.6 %shard_map.55.keep_ref = f32[432,256]{1,0:T(8,128)S(1)} custom-call(bf16[10,576,256]{2,1,0:T(8,128)(2,1)S(1)} %get-tuple-element.31.win_ref, bf16[8,2,128,256]{3,2,1,0:T(8,128)(2,1)S(1)} %get-tuple-element.28.grad_ref), custom_call_target="tpu_custom_call" | custom-call | flops 1 | bytes 1 | tf_op jit(solution)/shard_map/pallas_call | solution.py:255
  26.7 1.1 %collective-permute-done.7.received_ref = f32[432,256]{1,0:T(8,128)S(1)} collective-permute-done((f32[432,256]{1,0:T(8,128)S(1)}, f32[432,256]{1,0:T(8,128)S(1)}, u32[]{:S(2)}, u32[]{:S(2)}) %collective-permute-start.7) | collective-permute-done | bytes 442400 | tf_op jit(solution)/shard_map/ppermute | solution.py:265
  27.8 0.2 shard_map.56
  28.0 1.6 %collective-permute-start.11 = (f16[448,256]{1,0:T(8,128)(2,1)S(1)}, f16[448,256]{1,0:T(8,128)(2,1)S(1)}, u32[]{:S(2)}, u32[]{:S(2)}) collective-permute-start(f16[448,256]{1,0:T(8,128)(2,1)S(1)} %convert_element_type.6), channel_id=1, source_target_pairs={{0,16},{8,24},{16,0},{24,8},{1,17},{9,25},{17,1},{25,9},{2,18},{10... | collective-permute-start | bytes 688136 | tf_op jit(solution)/shard_map/ppermute | solution.py:279
  29.6 1.1 %shard_map.58 = (f32[144,256]{1,0:T(8,128)S(1)}, f32[144,256]{1,0:T(8,128)S(1)}, f32[144,256]{1,0:T(8,128)S(1)}, f32[144,256]{1,0:T(8,128)S(1)}, f32[144,256]{1,0:T(8,128)S(1)}, /*index=5*/f32[144,256]{1,0:T(8,128)S(1)}) custom-call(bf16[10,576,256]{2,1,0:T(8,128)(2,1)S(1)} %get-tuple-element.31.win_ref, bf16[8,2,128,256]{3,2,1,0:T(8,128)(2,1)S(1)} %get-tuple-element.28.grad_ref), custom_call_target="tpu_custom_call" | custom-call | flops 1 | bytes 1 | tf_op jit(solution)/shard_map/pallas_call | solution.py:255
  30.7 0.1 collective-permute-start.8
  30.7 0.5 %collective-permute-start.9 = (f32[144,256]{1,0:T(8,128)S(1)}, f32[144,256]{1,0:T(8,128)S(1)}, u32[]{:S(2)}, u32[]{:S(2)}) collective-permute-start(f32[144,256]{1,0:T(8,128)S(1)} %get-tuple-element.35), channel_id=1, source_target_pairs={{0,8},{8,0},{16,24},{24,16},{1,9},{9,1},{17,25},{25,17},{2,10},{10... | collective-permute-start | bytes 442376 | tf_op jit(solution)/shard_map/ppermute | solution.py:265
  31.2 0.1 collective-permute-start.10
  31.3 0.0 slice-done
  31.3 0.0 slice-done.1
  31.3 3.1 %shard_map.57 = bf16[2,30,512]{2,1,0:T(8,128)(2,1)S(1)} custom-call(bf16[2,136,256]{2,1,0:T(8,128)(2,1)S(1)} %get-tuple-element.30.refs_0_.own_ref, bf16[2,136,256]{2,1,0:T(8,128)(2,1)S(1)} %collective-permute-done.2.refs_1_.other_ref, bf16[2,136,256]{2,1,0:T(8,128)(2,1)S(1)} %collective-permute-done.3.refs_2_.next_ref, ...), custom_call_target="tpu_custom_call" | custom-call | flops 1 | bytes 1 | tf_op jit(solution)/shard_map/pallas_call | solution.py:283
  34.4 0.7 %copy.8 = bf16[1,2,1,30,512]{4,1,3,2,0:T(2,128)(2,1)} copy(bf16[1,2,1,30,512]{4,3,1,2,0:T(8,128)(2,1)S(1)} %bitcast.15) | data formatting | bytes 122880
  35.1 0.0 collective-permute-done.8
  35.1 0.0 collective-permute-done.9
  35.2 0.0 collective-permute-done.10
  35.2 0.5 %collective-permute-done.11 = f16[448,256]{1,0:T(8,128)(2,1)S(1)} collective-permute-done((f16[448,256]{1,0:T(8,128)(2,1)S(1)}, f16[448,256]{1,0:T(8,128)(2,1)S(1)}, u32[]{:S(2)}, u32[]{:S(2)}) %collective-permute-start.11) | collective-permute-done | bytes 229408 | tf_op jit(solution)/shard_map/ppermute | solution.py:279
  35.8 0.8 %fusion = f32[432,256]{1,0:T(8,128)} fusion(f32[448,256]{1,0:T(8,128)S(1)} %convert_element_type.7, f32[144,256]{1,0:T(8,128)S(1)} %add.14, f32[144,256]{1,0:T(8,128)S(1)} %add.13, f32[144,256]{1,0:T(8,128)S(1)} %add.12, f32[256]{0:T(256)S(1)} %bitcast.19), kind=kLoop, calls=%fused_computation.1 | loop fusion | flops 552960 | bytes 1328128 | tf_op jit(solution)/shard_map/add | solution.py:301
  (7 shorter events, 0.1 us)
Async XLA Ops:
  0.6 0.8 %copy-start.1 = (bf16[1,2,1,30,512]{4,1,3,2,0:T(2,128)(2,1)S(1)}, bf16[1,2,1,30,512]{4,1,3,2,0:T(2,128)(2,1)}, u32[]{:S(2)}) copy-start(bf16[1,2,1,30,512]{4,1,3,2,0:T(2,128)(2,1)} %param.3) | copy-start | bytes 184324
  1.7 0.9 %copy-start = (bf16[1,2,2,60,256]{4,2,3,1,0:T(2,128)(2,1)S(1)}, bf16[1,2,2,60,256]{4,2,3,1,0:T(2,128)(2,1)}, u32[]{:S(2)}) copy-start(bf16[1,2,2,60,256]{4,2,3,1,0:T(2,128)(2,1)} %param.4) | copy-start | bytes 368644
  2.7 9.2 %collective-permute-start.3 = (bf16[2,136,256]{2,1,0:T(8,128)(2,1)S(1)}, bf16[2,136,256]{2,1,0:T(8,128)(2,1)S(1)}, u32[]{:S(2)}, u32[]{:S(2)}) collective-permute-start(bf16[2,136,256]{2,1,0:T(8,128)(2,1)S(1)} %get-tuple-element.22), channel_id=1, source_target_pairs={{0,6},{2,0},{4,2},{6,4},{1,7},{3,1},{5,3},{7,5},{8,14},{10,8},{12,... | collective-permute-start | bytes 417800 | tf_op jit(solution)/shard_map/ppermute | solution.py:226
  7.8 8.5 %collective-permute-start.5 = (bf16[2,136,256]{2,1,0:T(8,128)(2,1)S(1)}, bf16[2,136,256]{2,1,0:T(8,128)(2,1)S(1)}, u32[]{:S(2)}, u32[]{:S(2)}) collective-permute-start(bf16[2,136,256]{2,1,0:T(8,128)(2,1)S(1)} %get-tuple-element.23), channel_id=1, source_target_pairs={{0,2},{2,4},{4,6},{6,0},{1,3},{3,5},{5,7},{7,1},{8,10},{10,12},{12... | collective-permute-start | bytes 417800 | tf_op jit(solution)/shard_map/ppermute | solution.py:226
  7.8 12.0 %collective-permute-start = (bf16[2,136,256]{2,1,0:T(8,128)(2,1)S(1)}, bf16[2,136,256]{2,1,0:T(8,128)(2,1)S(1)}, u32[]{:S(2)}, u32[]{:S(2)}) collective-permute-start(bf16[2,136,256]{2,1,0:T(8,128)(2,1)S(1)} %get-tuple-element.20), channel_id=1, source_target_pairs={{0,4},{2,6},{4,0},{6,2},{1,5},{3,7},{5,1},{7,3},{8,12},{10,14},{12... | collective-permute-start | bytes 417800 | tf_op jit(solution)/shard_map/ppermute | solution.py:226
  8.8 12.5 %collective-permute-start.2 = (bf16[2,136,256]{2,1,0:T(8,128)(2,1)S(1)}, bf16[2,136,256]{2,1,0:T(8,128)(2,1)S(1)}, u32[]{:S(2)}, u32[]{:S(2)}) collective-permute-start(bf16[2,136,256]{2,1,0:T(8,128)(2,1)S(1)} %get-tuple-element.30.refs_0_.own_ref), channel_id=1, source_target_pairs={{0,1},{1,0},{2,3},{3,2},{4,5},{5,4},{6,7},{7,6},{8,9},{9,8},{10,11... | collective-permute-start | bytes 417800 | tf_op jit(solution)/shard_map/ppermute | solution.py:227
  11.9 9.5 %collective-permute-start.4 = (bf16[2,136,256]{2,1,0:T(8,128)(2,1)S(1)}, bf16[2,136,256]{2,1,0:T(8,128)(2,1)S(1)}, u32[]{:S(2)}, u32[]{:S(2)}) collective-permute-start(bf16[2,136,256]{2,1,0:T(8,128)(2,1)S(1)} %collective-permute-done.3.refs_2_.next_ref), channel_id=1, source_target_pairs={{0,1},{1,0},{2,3},{3,2},{4,5},{5,4},{6,7},{7,6},{8,9},{9,8},{10,11... | collective-permute-start | bytes 417800 | tf_op jit(solution)/shard_map/ppermute | solution.py:227
  16.2 5.1 %collective-permute-start.6 = (bf16[2,136,256]{2,1,0:T(8,128)(2,1)S(1)}, bf16[2,136,256]{2,1,0:T(8,128)(2,1)S(1)}, u32[]{:S(2)}, u32[]{:S(2)}) collective-permute-start(bf16[2,136,256]{2,1,0:T(8,128)(2,1)S(1)} %collective-permute-done.5.refs_4_), channel_id=1, source_target_pairs={{0,1},{1,0},{2,3},{3,2},{4,5},{5,4},{6,7},{7,6},{8,9},{9,8},{10,11... | collective-permute-start | bytes 417800 | tf_op jit(solution)/shard_map/ppermute | solution.py:227
  19.8 5.1 %collective-permute-start.1 = (bf16[2,136,256]{2,1,0:T(8,128)(2,1)S(1)}, bf16[2,136,256]{2,1,0:T(8,128)(2,1)S(1)}, u32[]{:S(2)}, u32[]{:S(2)}) collective-permute-start(bf16[2,136,256]{2,1,0:T(8,128)(2,1)S(1)} %collective-permute-done.refs_0_), channel_id=1, source_target_pairs={{0,1},{1,0},{2,3},{3,2},{4,5},{5,4},{6,7},{7,6},{8,9},{9,8},{10,11... | collective-permute-start | bytes 417800 | tf_op jit(solution)/shard_map/ppermute | solution.py:227
  25.3 6.0 %slice-start = ((s8[7077888]{0:T(1024)(128)(4,1)}), s8[4194304]{0:T(1024)(128)(4,1)S(1)}, s32[]{:S(2)}) async-start(s8[7077888]{0:T(1024)(128)(4,1)} %bitcast.12), calls=%async_computation | async-start | bytes 8388608
  25.9 5.4 %slice-start.1 = ((s8[7077888]{0:T(1024)(128)(4,1)}), s8[2883584]{0:T(1024)(128)(4,1)S(1)}, s32[]{:S(2)}) async-start(s8[7077888]{0:T(1024)(128)(4,1)} %bitcast.12), calls=%async_computation.1 | async-start | bytes 5767168
  25.9 1.9 %collective-permute-start.7 = (f32[432,256]{1,0:T(8,128)S(1)}, f32[432,256]{1,0:T(8,128)S(1)}, u32[]{:S(2)}, u32[]{:S(2)}) collective-permute-start(f32[432,256]{1,0:T(8,128)S(1)} %shard_map.54), channel_id=1, source_target_pairs={{0,8},{8,0},{16,24},{24,16},{1,9},{9,1},{17,25},{25,17},{2,10},{10... | collective-permute-start | bytes 1327112 | tf_op jit(solution)/shard_map/ppermute | solution.py:265
  28.0 7.7 %collective-permute-start.11 = (f16[448,256]{1,0:T(8,128)(2,1)S(1)}, f16[448,256]{1,0:T(8,128)(2,1)S(1)}, u32[]{:S(2)}, u32[]{:S(2)}) collective-permute-start(f16[448,256]{1,0:T(8,128)(2,1)S(1)} %convert_element_type.6), channel_id=1, source_target_pairs={{0,16},{8,24},{16,0},{24,8},{1,17},{9,25},{17,1},{25,9},{2,18},{10... | collective-permute-start | bytes 688136 | tf_op jit(solution)/shard_map/ppermute | solution.py:279
  30.7 4.5 %collective-permute-start.8 = (f32[144,256]{1,0:T(8,128)S(1)}, f32[144,256]{1,0:T(8,128)S(1)}, u32[]{:S(2)}, u32[]{:S(2)}) collective-permute-start(f32[144,256]{1,0:T(8,128)S(1)} %get-tuple-element.33), channel_id=1, source_target_pairs={{0,8},{8,0},{16,24},{24,16},{1,9},{9,1},{17,25},{25,17},{2,10},{10... | collective-permute-start | bytes 442376 | tf_op jit(solution)/shard_map/ppermute | solution.py:265
  30.7 4.4 %collective-permute-start.9 = (f32[144,256]{1,0:T(8,128)S(1)}, f32[144,256]{1,0:T(8,128)S(1)}, u32[]{:S(2)}, u32[]{:S(2)}) collective-permute-start(f32[144,256]{1,0:T(8,128)S(1)} %get-tuple-element.35), channel_id=1, source_target_pairs={{0,8},{8,0},{16,24},{24,16},{1,9},{9,1},{17,25},{25,17},{2,10},{10... | collective-permute-start | bytes 442376 | tf_op jit(solution)/shard_map/ppermute | solution.py:265
  31.2 4.0 %collective-permute-start.10 = (f32[144,256]{1,0:T(8,128)S(1)}, f32[144,256]{1,0:T(8,128)S(1)}, u32[]{:S(2)}, u32[]{:S(2)}) collective-permute-start(f32[144,256]{1,0:T(8,128)S(1)} %get-tuple-element.37), channel_id=1, source_target_pairs={{0,8},{8,0},{16,24},{24,16},{1,9},{9,1},{17,25},{25,17},{2,10},{10... | collective-permute-start | bytes 442376 | tf_op jit(solution)/shard_map/ppermute | solution.py:265

commit v4 on v3

--- a/solution.py
+++ b/solution.py
@@ -60,7 +60,7 @@
             outs[k][f, LATENT_ROWS:, :] = grads[f]
 
 
-def arrange_kernel(tm, share, shifts, *refs):
+def arrange_kernel(tm, share, shifts, late, *refs):
     blocks = refs[: 2 * len(shifts)]
     win_ref, grad_ref, pick_ref, lat_ref = refs[-4:]
     group = 4 * share
@@ -81,6 +81,9 @@
                     base = (f * 9 + ij) * 256 + s * 128
                     pick_ref[:, base : base + 128] = pick
         win_ref[0:2] = jnp.zeros((2,) + win_ref.shape[1:], jnp.bfloat16)
+        t = lax.rem(me_tm + tm - late, tm)
+        win_ref[pl.ds(2 * t + 2, 2)] = jnp.zeros((2,) + win_ref.shape[1:], jnp.bfloat16)
+        grad_ref[pl.ds(2 * t, 2)] = jnp.zeros((2,) + grad_ref.shape[1:], jnp.bfloat16)
     where = [lax.rem(me_tm + tm - k, tm) for k in shifts]
     for n, t in enumerate(where):
         for half, rows in enumerate((me_rows, 1 - me_rows)):
@@ -123,6 +126,37 @@
             ref = out_refs[m * each + n % each]
             place = n // each * rows
             ref[place : place + rows] = total[start : start + rows]
+
+
+def late_terms(tm, late, first, win_ref, grad_ref, part_ref, out_ref):
+    rows = part_ref.shape[0] // 3
+    frames = grad_ref.shape[0]
+    block = lax.rem(lax.axis_index("tm") + tm - late, tm)
+    total = [part_ref[a * rows : (a + 1) * rows] for a in range(3)]
+    for step, taps in enumerate(((0, 1, 2), (0, 1, 2), (0, 1), (0,))):
+        frame = 2 * block + step
+        if step > 1:
+            inside = jnp.where(frame < frames, 1.0, 0.0).astype(jnp.bfloat16)
+            frame = jnp.minimum(frame, frames - 1)
+        grad = grad_ref[frame].reshape(256, grad_ref.shape[3])
+        if step > 1:
+            grad = grad * inside
+        lhs = jnp.concatenate([win_ref[frame + a, first : first + rows, :] for a in taps], axis=0)
+        term = jnp.dot(lhs, grad, preferred_element_type=jnp.float32)
+        for n, a in enumerate(taps):
+            total[a] = total[a] + term[n * rows : (n + 1) * rows]
+    for a in range(3):
+        out_ref[a * rows : (a + 1) * rows] = total[a]
+
+
+def arrange_late_kernel(tm, share, late, own_ref, other_ref, w_ref, g_ref, p_ref, part_ref, *refs):
+    win_ref, grad_ref, pick_ref, out_ref, lat_ref = refs
+    arrange_kernel(tm, share, (late,), late, own_ref, other_ref, win_ref, grad_ref, pick_ref, lat_ref)
+    late_terms(tm, late, 0, win_ref, grad_ref, part_ref, out_ref)
+
+
+def keep_late_kernel(tm, late, win_ref, grad_ref, part_ref, out_ref):
+    late_terms(tm, late, part_ref.shape[0] // 3, win_ref, grad_ref, part_ref, out_ref)
 
 
 TOP_EXPONENT = 14
@@ -214,6 +248,7 @@
         in_specs=whole(1),
         out_specs=whole(1)[0],
         compiler_params=params(),
+        cost_estimate=pl.CostEstimate(flops=2**31, bytes_accessed=2**24, transcendentals=0),
     )(lat)
     messages = pl.pallas_call(
         functools.partial(message_kernel, tm),
@@ -232,25 +267,21 @@
         jax.ShapeDtypeStruct((128, 18 * 256), jnp.bfloat16),
     )
 
-    def arrange(first, last, earlier):
-        blocks = [block for n in range(first, last) for block in (shifted[n], across[n])]
-        return pl.pallas_call(
-            functools.partial(arrange_kernel, tm, share, tuple(order[first:last])),
-            out_shape=arranged,
-            in_specs=whole(len(blocks) + len(earlier)),
-            out_specs=tuple(whole(3)),
-            scratch_shapes=[pltpu.VMEM((last - first, 2, 64, 4 * share), jnp.float32)],
-            input_output_aliases={len(blocks) + n: n for n in range(len(earlier))},
-            compiler_params=params(),
-            cost_estimate=light(),
-        )(*blocks, *earlier)
-
-    early = arrange(0, tm - 1, ())
-    windows, grads, _ = arrange(tm - 1, tm, early)
+    late = order[-1]
+    early = [block for pair in zip(shifted[:-1], across[:-1]) for block in pair]
+    early = pl.pallas_call(
+        functools.partial(arrange_kernel, tm, share, tuple(order[:-1]), late),
+        out_shape=arranged,
+        in_specs=whole(len(early)),
+        out_specs=tuple(whole(3)),
+        scratch_shapes=[pltpu.VMEM((tm - 1, 2, 64, 4 * share), jnp.float32)],
+        compiler_params=params(),
+        cost_estimate=light(),
+    )(*early)
 
     rows = 9 * share
 
-    def terms(first, windows, outs, each):
+    def terms(first, windows, grads, outs, each):
         out = jax.ShapeDtypeStruct((3 // each * rows, outputs), jnp.float32)
         return pl.pallas_call(
             functools.partial(terms_kernel, first, (0, 1, 2), frames, outs),
@@ -264,9 +295,25 @@
     def other_core(block):
         return lax.ppermute(block, "dp", [(i, i ^ 1) for i in range(4)])
 
-    (send,) = terms(0, windows, 1, 1)
-    after, _ = lax.optimization_barrier((windows, send))
-    (keep,) = terms(rows, after, 1, 1)
+    send, keep = terms(0, early[0], early[1], 2, 1)
+    windows, grads, _, send = pl.pallas_call(
+        functools.partial(arrange_late_kernel, tm, share, late),
+        out_shape=arranged + (jax.ShapeDtypeStruct(send.shape, jnp.float32),),
+        in_specs=whole(6),
+        out_specs=tuple(whole(4)),
+        scratch_shapes=[pltpu.VMEM((1, 2, 64, 4 * share), jnp.float32)],
+        input_output_aliases={2: 0, 3: 1, 4: 2},
+        compiler_params=params(),
+        cost_estimate=light(),
+    )(shifted[-1], across[-1], *early, send)
+    keep = pl.pallas_call(
+        functools.partial(keep_late_kernel, tm, late),
+        out_shape=jax.ShapeDtypeStruct(keep.shape, jnp.float32),
+        in_specs=whole(3),
+        out_specs=whole(1)[0],
+        compiler_params=params(),
+        cost_estimate=light(),
+    )(windows, grads, keep)
     chip = pl.pallas_call(
         pack_kernel,
         out_shape=jax.ShapeDtypeStruct((3 * rows + EXPONENT_ROWS, outputs), jnp.float32),
@@ -296,7 +343,7 @@
         cost_estimate=light(),
     )(first, across[0], shifted[1], across[1], taps)
 
-    parts = terms(2 * rows, windows, 2, 3)
+    parts = terms(2 * rows, windows, grads, 2, 3)
     stay = [keep + other_core(send) for send, keep in zip(parts[:3], parts[3:])]
     total = jnp.concatenate(stay) * factor + crossed
     weight_grad = jnp.transpose(total.reshape(3, 3, 3, share, outputs), (3, 0, 1, 2, 4))

time: 36.8 us -> 36.1 us (0.981)
  waiting for transfers between devices: 10.8 us -> 9.9 us
  Pallas kernels: 7.19 us -> 7.67 us
    ppermute x4, waiting for transfers between devices: 2.67 us -> 1.53 us  [narrow_body(): across = [lax.ppermute(block, 'rows', swap) for block in shifted]]
    pallas_call x2 -> x3, Pallas kernels: 1.28 us -> 1.95 us  [the longest x1 0.91 us: narrow_body(): pl.pallas_call(functools.partial(arrange_kernel, tm, share, tuple(order[:...]
    pallas_call x3 -> x2, Pallas kernels: 2.32 us -> 2.15 us  [terms(): pl.pallas_call(functools.partial(terms_kernel, first, (0, 1, 2), frames,...]
  transfers between devices with their start and end apart: 12 -> 12, of which waited for: 6 -> 6; matrix products, arithmetic and copies ran while one was open for 2% -> 2% of each run, Pallas kernels for 15% -> 18%
where the time goes in v4:
time: 36.1 us; the launch traced here: 35.9 us
  starting transfers between devices  14.5 us (40%)
  waiting for transfers between devices  9.9 us (27%)
  Pallas kernels  7.67 us (21%)
  local copies, waits for them, and re-layouts  2.17 us (6%)
  other arithmetic  0.95 us (3%)
  between operations  0.79 us (2%)
    ppermute x3, waiting for transfers between devices, narrow_body(): lax.ppermute(messages[k], 'tm', cycle(tm, k))  6.43 us
    ppermute x3, starting transfers between devices, narrow_body(): lax.ppermute(messages[k], 'tm', cycle(tm, k))  6.11 us
    ppermute x4, starting transfers between devices, narrow_body(): across = [lax.ppermute(block, 'rows', swap) for block in shifted]  6.08 us
    pallas_call x1, Pallas kernels, narrow_body(): pl.pallas_call(functools.partial(latents_kernel, tm), grid=(3,), out_shap...  3.09 us
    unnamed x9, local copies, waits for them, and re-layouts  2.17 us
    pallas_call x2, Pallas kernels, terms(): pl.pallas_call(functools.partial(terms_kernel, first, (0, 1, 2), frames,...  2.15 us
    ppermute x1, starting transfers between devices, narrow_body(): lax.ppermute(chip, 'dp', [(i, i ^ 2) for i in range(4)]).astype(jnp.float32)  1.56 us
    ppermute x4, waiting for transfers between devices, narrow_body(): across = [lax.ppermute(block, 'rows', swap) for block in shifted]  1.53 us
  transfers between devices with their start and end apart: 12, of which 6 were waited for; matrix products, arithmetic and copies ran while one was open for 2% of the time, Pallas kernels for 18%

profile of v4, /device:TPU:0, one launch (start us, length us, event | category | flops | bytes accessed | tf_op | source)
XLA Modules:
  0.0 35.9 jit_solution(1604145106631556382)
XLA Ops:
  0.6 0.0 copy-start.1
  0.6 0.8 %copy-done.1 = bf16[1,2,1,30,512]{4,1,3,2,0:T(2,128)(2,1)S(1)} copy-done((bf16[1,2,1,30,512]{4,1,3,2,0:T(2,128)(2,1)S(1)}, bf16[1,2,1,30,512]{4,1,3,2,0:T(2,128)(2,1)}, u32[]{:S(2)}) %copy-start.1) | copy-done | bytes 61464
  1.5 0.0 copy-start
  1.5 0.2 shard_map.50.wide_ref
  1.7 0.7 %copy-done = bf16[1,2,2,60,256]{4,2,3,1,0:T(2,128)(2,1)S(1)} copy-done((bf16[1,2,2,60,256]{4,2,3,1,0:T(2,128)(2,1)S(1)}, bf16[1,2,2,60,256]{4,2,3,1,0:T(2,128)(2,1)}, u32[]{:S(2)}) %copy-start) | copy-done | bytes 122904
  2.4 0.1 shard_map.51
  2.4 5.1 %collective-permute-start.3 = (bf16[2,136,256]{2,1,0:T(8,128)(2,1)S(1)}, bf16[2,136,256]{2,1,0:T(8,128)(2,1)S(1)}, u32[]{:S(2)}, u32[]{:S(2)}) collective-permute-start(bf16[2,136,256]{2,1,0:T(8,128)(2,1)S(1)} %get-tuple-element.24), channel_id=1, source_target_pairs={{0,6},{2,0},{4,2},{6,4},{1,7},{3,1},{5,3},{7,5},{8,14},{10,8},{12,... | collective-permute-start | bytes 417800 | tf_op jit(solution)/shard_map/ppermute | solution.py:261
  7.5 0.0 collective-permute-start.5
  7.5 1.0 %collective-permute-start = (bf16[2,136,256]{2,1,0:T(8,128)(2,1)S(1)}, bf16[2,136,256]{2,1,0:T(8,128)(2,1)S(1)}, u32[]{:S(2)}, u32[]{:S(2)}) collective-permute-start(bf16[2,136,256]{2,1,0:T(8,128)(2,1)S(1)} %get-tuple-element.22), channel_id=1, source_target_pairs={{0,4},{2,6},{4,0},{6,2},{1,5},{3,7},{5,1},{7,3},{8,12},{10,14},{12... | collective-permute-start | bytes 417800 | tf_op jit(solution)/shard_map/ppermute | solution.py:261
  8.5 1.5 %collective-permute-start.2 = (bf16[2,136,256]{2,1,0:T(8,128)(2,1)S(1)}, bf16[2,136,256]{2,1,0:T(8,128)(2,1)S(1)}, u32[]{:S(2)}, u32[]{:S(2)}) collective-permute-start(bf16[2,136,256]{2,1,0:T(8,128)(2,1)S(1)} %get-tuple-element.34.refs_0_.own_ref), channel_id=1, source_target_pairs={{0,1},{1,0},{2,3},{3,2},{4,5},{5,4},{6,7},{7,6},{8,9},{9,8},{10,11... | collective-permute-start | bytes 417800 | tf_op jit(solution)/shard_map/ppermute | solution.py:262
  10.1 1.5 %collective-permute-done.3.refs_2_.next_ref = bf16[2,136,256]{2,1,0:T(8,128)(2,1)S(1)} collective-permute-done((bf16[2,136,256]{2,1,0:T(8,128)(2,1)S(1)}, bf16[2,136,256]{2,1,0:T(8,128)(2,1)S(1)}, u32[]{:S(2)}, u32[]{:S(2)}) %collective-permute-start.3) | collective-permute-done | bytes 139296 | tf_op jit(solution)/shard_map/ppermute | solution.py:261
  11.6 1.5 %collective-permute-start.4 = (bf16[2,136,256]{2,1,0:T(8,128)(2,1)S(1)}, bf16[2,136,256]{2,1,0:T(8,128)(2,1)S(1)}, u32[]{:S(2)}, u32[]{:S(2)}) collective-permute-start(bf16[2,136,256]{2,1,0:T(8,128)(2,1)S(1)} %collective-permute-done.3.refs_2_.next_ref), channel_id=1, source_target_pairs={{0,1},{1,0},{2,3},{3,2},{4,5},{5,4},{6,7},{7,6},{8,9},{9,8},{10,11... | collective-permute-start | bytes 417800 | tf_op jit(solution)/shard_map/ppermute | solution.py:262
  13.1 2.9 %collective-permute-done.5.refs_4_ = bf16[2,136,256]{2,1,0:T(8,128)(2,1)S(1)} collective-permute-done((bf16[2,136,256]{2,1,0:T(8,128)(2,1)S(1)}, bf16[2,136,256]{2,1,0:T(8,128)(2,1)S(1)}, u32[]{:S(2)}, u32[]{:S(2)}) %collective-permute-start.5) | collective-permute-done | bytes 139296 | tf_op jit(solution)/shard_map/ppermute | solution.py:261
  16.0 1.5 %collective-permute-start.6 = (bf16[2,136,256]{2,1,0:T(8,128)(2,1)S(1)}, bf16[2,136,256]{2,1,0:T(8,128)(2,1)S(1)}, u32[]{:S(2)}, u32[]{:S(2)}) collective-permute-start(bf16[2,136,256]{2,1,0:T(8,128)(2,1)S(1)} %collective-permute-done.5.refs_4_), channel_id=1, source_target_pairs={{0,1},{1,0},{2,3},{3,2},{4,5},{5,4},{6,7},{7,6},{8,9},{9,8},{10,11... | collective-permute-start | bytes 417800 | tf_op jit(solution)/shard_map/ppermute | solution.py:262
  17.5 2.0 %collective-permute-done.own_ref = bf16[2,136,256]{2,1,0:T(8,128)(2,1)S(1)} collective-permute-done((bf16[2,136,256]{2,1,0:T(8,128)(2,1)S(1)}, bf16[2,136,256]{2,1,0:T(8,128)(2,1)S(1)}, u32[]{:S(2)}, u32[]{:S(2)}) %collective-permute-start) | collective-permute-done | bytes 139296 | tf_op jit(solution)/shard_map/ppermute | solution.py:261
  19.5 1.5 %collective-permute-start.1 = (bf16[2,136,256]{2,1,0:T(8,128)(2,1)S(1)}, bf16[2,136,256]{2,1,0:T(8,128)(2,1)S(1)}, u32[]{:S(2)}, u32[]{:S(2)}) collective-permute-start(bf16[2,136,256]{2,1,0:T(8,128)(2,1)S(1)} %collective-permute-done.own_ref), channel_id=1, source_target_pairs={{0,1},{1,0},{2,3},{3,2},{4,5},{5,4},{6,7},{7,6},{8,9},{9,8},{10,11... | collective-permute-start | bytes 417800 | tf_op jit(solution)/shard_map/ppermute | solution.py:262
  21.1 0.0 collective-permute-done.2.refs_1_.other_ref
  21.1 0.0 collective-permute-done.4.refs_3_.next_other_ref
  21.1 0.0 collective-permute-done.6.refs_5_
  21.1 0.9 %shard_map.52 = (bf16[10,576,256]{2,1,0:T(8,128)(2,1)S(1)}, bf16[8,2,128,256]{3,2,1,0:T(8,128)(2,1)S(1)}, bf16[128,4608]{1,0:T(8,128)(2,1)S(1)}) custom-call(bf16[2,136,256]{2,1,0:T(8,128)(2,1)S(1)} %get-tuple-element.34.refs_0_.own_ref, bf16[2,136,256]{2,1,0:T(8,128)(2,1)S(1)} %collective-permute-done.2.refs_1_.other_ref, ...), custom_call_target="tpu_custom_call" | custom-call | flops 1 | bytes 1 | tf_op jit(solution)/shard_map/pallas_call | solution.py:272
  22.0 1.1 %shard_map.53 = (f32[432,256]{1,0:T(8,128)S(1)}, f32[432,256]{1,0:T(8,128)S(1)}) custom-call(bf16[10,576,256]{2,1,0:T(8,128)(2,1)S(1)} %get-tuple-element.26.win_ref.w_ref, bf16[8,2,128,256]{3,2,1,0:T(8,128)(2,1)S(1)} %get-tuple-element.27.grad_ref.g_ref), custom_call_target="tpu_custom_call" | custom-call | flops 1 | bytes 1 | tf_op jit(solution)/shard_map/pallas_call | solution.py:286
  23.1 1.5 %collective-permute-done.1.other_ref = bf16[2,136,256]{2,1,0:T(8,128)(2,1)S(1)} collective-permute-done((bf16[2,136,256]{2,1,0:T(8,128)(2,1)S(1)}, bf16[2,136,256]{2,1,0:T(8,128)(2,1)S(1)}, u32[]{:S(2)}, u32[]{:S(2)}) %collective-permute-start.1) | collective-permute-done | bytes 139296 | tf_op jit(solution)/shard_map/ppermute | solution.py:262
  24.6 0.0 slice-start
  24.6 0.7 %shard_map.54 = (bf16[10,576,256]{2,1,0:T(8,128)(2,1)S(1)}, bf16[8,2,128,256]{3,2,1,0:T(8,128)(2,1)S(1)}, bf16[128,4608]{1,0:T(8,128)(2,1)S(1)}, f32[432,256]{1,0:T(8,128)S(1)}) custom-call(bf16[2,136,256]{2,1,0:T(8,128)(2,1)S(1)} %collective-permute-done.own_ref, ...), custom_call_target="tpu_custom_call", output_to_operand_aliasing={{0}: (2, {}), {1}: (3, {}), {2}: (4, {})} | custom-call | flops 1 | bytes 1 | tf_op jit(solution)/shard_map/pallas_call | solution.py:299
  25.3 0.1 collective-permute-start.7
  25.4 0.0 slice-start.1
  25.4 0.4 shard_map.55.keep_ref
  25.7 1.4 %collective-permute-done.7.received_ref = f32[432,256]{1,0:T(8,128)S(1)} collective-permute-done((f32[432,256]{1,0:T(8,128)S(1)}, f32[432,256]{1,0:T(8,128)S(1)}, u32[]{:S(2)}, u32[]{:S(2)}) %collective-permute-start.7) | collective-permute-done | bytes 442400 | tf_op jit(solution)/shard_map/ppermute | solution.py:296
  27.1 0.2 shard_map.56
  27.4 1.6 %collective-permute-start.11 = (f16[448,256]{1,0:T(8,128)(2,1)S(1)}, f16[448,256]{1,0:T(8,128)(2,1)S(1)}, u32[]{:S(2)}, u32[]{:S(2)}) collective-permute-start(f16[448,256]{1,0:T(8,128)(2,1)S(1)} %convert_element_type.6), channel_id=1, source_target_pairs={{0,16},{8,24},{16,0},{24,8},{1,17},{9,25},{17,1},{25,9},{2,18},{10... | collective-permute-start | bytes 688136 | tf_op jit(solution)/shard_map/ppermute | solution.py:326
  28.9 1.1 %shard_map.58 = (f32[144,256]{1,0:T(8,128)S(1)}, f32[144,256]{1,0:T(8,128)S(1)}, f32[144,256]{1,0:T(8,128)S(1)}, f32[144,256]{1,0:T(8,128)S(1)}, f32[144,256]{1,0:T(8,128)S(1)}, /*index=5*/f32[144,256]{1,0:T(8,128)S(1)}) custom-call(bf16[10,576,256]{2,1,0:T(8,128)(2,1)S(1)} %get-tuple-element.35.win_ref, bf16[8,2,128,256]{3,2,1,0:T(8,128)(2,1)S(1)} %get-tuple-element.31.grad_ref), custom_call_target="tpu_custom_call" | custom-call | flops 1 | bytes 1 | tf_op jit(solution)/shard_map/pallas_call | solution.py:286
  30.0 0.1 collective-permute-start.8
  30.1 0.5 %collective-permute-start.9 = (f32[144,256]{1,0:T(8,128)S(1)}, f32[144,256]{1,0:T(8,128)S(1)}, u32[]{:S(2)}, u32[]{:S(2)}) collective-permute-start(f32[144,256]{1,0:T(8,128)S(1)} %get-tuple-element.39), channel_id=1, source_target_pairs={{0,8},{8,0},{16,24},{24,16},{1,9},{9,1},{17,25},{25,17},{2,10},{10... | collective-permute-start | bytes 442376 | tf_op jit(solution)/shard_map/ppermute | solution.py:296
  30.6 0.1 collective-permute-start.10
  30.7 0.0 slice-done
  30.7 0.0 slice-done.1
  30.7 3.1 %shard_map.57 = bf16[2,30,512]{2,1,0:T(8,128)(2,1)S(1)} custom-call(bf16[2,136,256]{2,1,0:T(8,128)(2,1)S(1)} %get-tuple-element.34.refs_0_.own_ref, bf16[2,136,256]{2,1,0:T(8,128)(2,1)S(1)} %collective-permute-done.2.refs_1_.other_ref, bf16[2,136,256]{2,1,0:T(8,128)(2,1)S(1)} %collective-permute-done.3.refs_2_.next_ref, ...), custom_call_target="tpu_custom_call" | custom-call | flops 1 | bytes 1 | tf_op jit(solution)/shard_map/pallas_call | solution.py:330
  33.8 0.7 %copy.8 = bf16[1,2,1,30,512]{4,1,3,2,0:T(2,128)(2,1)} copy(bf16[1,2,1,30,512]{4,3,1,2,0:T(8,128)(2,1)S(1)} %bitcast.15) | data formatting | bytes 122880
  34.4 0.0 collective-permute-done.8
  34.5 0.0 collective-permute-done.9
  34.5 0.0 collective-permute-done.10
  34.5 0.5 %collective-permute-done.11 = f16[448,256]{1,0:T(8,128)(2,1)S(1)} collective-permute-done((f16[448,256]{1,0:T(8,128)(2,1)S(1)}, f16[448,256]{1,0:T(8,128)(2,1)S(1)}, u32[]{:S(2)}, u32[]{:S(2)}) %collective-permute-start.11) | collective-permute-done | bytes 229408 | tf_op jit(solution)/shard_map/ppermute | solution.py:326
  35.1 0.8 %fusion = f32[432,256]{1,0:T(8,128)} fusion(f32[448,256]{1,0:T(8,128)S(1)} %convert_element_type.7, f32[144,256]{1,0:T(8,128)S(1)} %add.14, f32[144,256]{1,0:T(8,128)S(1)} %add.13, f32[144,256]{1,0:T(8,128)S(1)} %add.12, f32[256]{0:T(256)S(1)} %bitcast.19), kind=kLoop, calls=%fused_computation.1 | loop fusion | flops 552960 | bytes 1328128 | tf_op jit(solution)/shard_map/add | solution.py:348
  (7 shorter events, 0.1 us)
Async XLA Ops:
  0.6 0.8 %copy-start.1 = (bf16[1,2,1,30,512]{4,1,3,2,0:T(2,128)(2,1)S(1)}, bf16[1,2,1,30,512]{4,1,3,2,0:T(2,128)(2,1)}, u32[]{:S(2)}) copy-start(bf16[1,2,1,30,512]{4,1,3,2,0:T(2,128)(2,1)} %param.3) | copy-start | bytes 184324
  1.5 0.9 %copy-start = (bf16[1,2,2,60,256]{4,2,3,1,0:T(2,128)(2,1)S(1)}, bf16[1,2,2,60,256]{4,2,3,1,0:T(2,128)(2,1)}, u32[]{:S(2)}) copy-start(bf16[1,2,2,60,256]{4,2,3,1,0:T(2,128)(2,1)} %param.4) | copy-start | bytes 368644
  2.4 9.2 %collective-permute-start.3 = (bf16[2,136,256]{2,1,0:T(8,128)(2,1)S(1)}, bf16[2,136,256]{2,1,0:T(8,128)(2,1)S(1)}, u32[]{:S(2)}, u32[]{:S(2)}) collective-permute-start(bf16[2,136,256]{2,1,0:T(8,128)(2,1)S(1)} %get-tuple-element.24), channel_id=1, source_target_pairs={{0,6},{2,0},{4,2},{6,4},{1,7},{3,1},{5,3},{7,5},{8,14},{10,8},{12,... | collective-permute-start | bytes 417800 | tf_op jit(solution)/shard_map/ppermute | solution.py:261
  7.5 8.5 %collective-permute-start.5 = (bf16[2,136,256]{2,1,0:T(8,128)(2,1)S(1)}, bf16[2,136,256]{2,1,0:T(8,128)(2,1)S(1)}, u32[]{:S(2)}, u32[]{:S(2)}) collective-permute-start(bf16[2,136,256]{2,1,0:T(8,128)(2,1)S(1)} %get-tuple-element.25), channel_id=1, source_target_pairs={{0,2},{2,4},{4,6},{6,0},{1,3},{3,5},{5,7},{7,1},{8,10},{10,12},{12... | collective-permute-start | bytes 417800 | tf_op jit(solution)/shard_map/ppermute | solution.py:261
  7.5 12.0 %collective-permute-start = (bf16[2,136,256]{2,1,0:T(8,128)(2,1)S(1)}, bf16[2,136,256]{2,1,0:T(8,128)(2,1)S(1)}, u32[]{:S(2)}, u32[]{:S(2)}) collective-permute-start(bf16[2,136,256]{2,1,0:T(8,128)(2,1)S(1)} %get-tuple-element.22), channel_id=1, source_target_pairs={{0,4},{2,6},{4,0},{6,2},{1,5},{3,7},{5,1},{7,3},{8,12},{10,14},{12... | collective-permute-start | bytes 417800 | tf_op jit(solution)/shard_map/ppermute | solution.py:261
  8.5 12.5 %collective-permute-start.2 = (bf16[2,136,256]{2,1,0:T(8,128)(2,1)S(1)}, bf16[2,136,256]{2,1,0:T(8,128)(2,1)S(1)}, u32[]{:S(2)}, u32[]{:S(2)}) collective-permute-start(bf16[2,136,256]{2,1,0:T(8,128)(2,1)S(1)} %get-tuple-element.34.refs_0_.own_ref), channel_id=1, source_target_pairs={{0,1},{1,0},{2,3},{3,2},{4,5},{5,4},{6,7},{7,6},{8,9},{9,8},{10,11... | collective-permute-start | bytes 417800 | tf_op jit(solution)/shard_map/ppermute | solution.py:262
  11.6 9.4 %collective-permute-start.4 = (bf16[2,136,256]{2,1,0:T(8,128)(2,1)S(1)}, bf16[2,136,256]{2,1,0:T(8,128)(2,1)S(1)}, u32[]{:S(2)}, u32[]{:S(2)}) collective-permute-start(bf16[2,136,256]{2,1,0:T(8,128)(2,1)S(1)} %collective-permute-done.3.refs_2_.next_ref), channel_id=1, source_target_pairs={{0,1},{1,0},{2,3},{3,2},{4,5},{5,4},{6,7},{7,6},{8,9},{9,8},{10,11... | collective-permute-start | bytes 417800 | tf_op jit(solution)/shard_map/ppermute | solution.py:262
  16.0 5.1 %collective-permute-start.6 = (bf16[2,136,256]{2,1,0:T(8,128)(2,1)S(1)}, bf16[2,136,256]{2,1,0:T(8,128)(2,1)S(1)}, u32[]{:S(2)}, u32[]{:S(2)}) collective-permute-start(bf16[2,136,256]{2,1,0:T(8,128)(2,1)S(1)} %collective-permute-done.5.refs_4_), channel_id=1, source_target_pairs={{0,1},{1,0},{2,3},{3,2},{4,5},{5,4},{6,7},{7,6},{8,9},{9,8},{10,11... | collective-permute-start | bytes 417800 | tf_op jit(solution)/shard_map/ppermute | solution.py:262
  19.5 5.1 %collective-permute-start.1 = (bf16[2,136,256]{2,1,0:T(8,128)(2,1)S(1)}, bf16[2,136,256]{2,1,0:T(8,128)(2,1)S(1)}, u32[]{:S(2)}, u32[]{:S(2)}) collective-permute-start(bf16[2,136,256]{2,1,0:T(8,128)(2,1)S(1)} %collective-permute-done.own_ref), channel_id=1, source_target_pairs={{0,1},{1,0},{2,3},{3,2},{4,5},{5,4},{6,7},{7,6},{8,9},{9,8},{10,11... | collective-permute-start | bytes 417800 | tf_op jit(solution)/shard_map/ppermute | solution.py:262
  24.6 6.1 %slice-start = ((s8[7077888]{0:T(1024)(128)(4,1)}), s8[4194304]{0:T(1024)(128)(4,1)S(1)}, s32[]{:S(2)}) async-start(s8[7077888]{0:T(1024)(128)(4,1)} %bitcast.12), calls=%async_computation | async-start | bytes 8388608
  25.3 1.9 %collective-permute-start.7 = (f32[432,256]{1,0:T(8,128)S(1)}, f32[432,256]{1,0:T(8,128)S(1)}, u32[]{:S(2)}, u32[]{:S(2)}) collective-permute-start(f32[432,256]{1,0:T(8,128)S(1)} %get-tuple-element.33), channel_id=1, source_target_pairs={{0,8},{8,0},{16,24},{24,16},{1,9},{9,1},{17,25},{25,17},{2,10},{10... | collective-permute-start | bytes 1327112 | tf_op jit(solution)/shard_map/ppermute | solution.py:296
  25.4 5.3 %slice-start.1 = ((s8[7077888]{0:T(1024)(128)(4,1)}), s8[2883584]{0:T(1024)(128)(4,1)S(1)}, s32[]{:S(2)}) async-start(s8[7077888]{0:T(1024)(128)(4,1)} %bitcast.12), calls=%async_computation.1 | async-start | bytes 5767168
  27.4 7.7 %collective-permute-start.11 = (f16[448,256]{1,0:T(8,128)(2,1)S(1)}, f16[448,256]{1,0:T(8,128)(2,1)S(1)}, u32[]{:S(2)}, u32[]{:S(2)}) collective-permute-start(f16[448,256]{1,0:T(8,128)(2,1)S(1)} %convert_element_type.6), channel_id=1, source_target_pairs={{0,16},{8,24},{16,0},{24,8},{1,17},{9,25},{17,1},{25,9},{2,18},{10... | collective-permute-start | bytes 688136 | tf_op jit(solution)/shard_map/ppermute | solution.py:326
  30.0 4.4 %collective-permute-start.8 = (f32[144,256]{1,0:T(8,128)S(1)}, f32[144,256]{1,0:T(8,128)S(1)}, u32[]{:S(2)}, u32[]{:S(2)}) collective-permute-start(f32[144,256]{1,0:T(8,128)S(1)} %get-tuple-element.37), channel_id=1, source_target_pairs={{0,8},{8,0},{16,24},{24,16},{1,9},{9,1},{17,25},{25,17},{2,10},{10... | collective-permute-start | bytes 442376 | tf_op jit(solution)/shard_map/ppermute | solution.py:296
  30.1 4.4 %collective-permute-start.9 = (f32[144,256]{1,0:T(8,128)S(1)}, f32[144,256]{1,0:T(8,128)S(1)}, u32[]{:S(2)}, u32[]{:S(2)}) collective-permute-start(f32[144,256]{1,0:T(8,128)S(1)} %get-tuple-element.39), channel_id=1, source_target_pairs={{0,8},{8,0},{16,24},{24,16},{1,9},{9,1},{17,25},{25,17},{2,10},{10... | collective-permute-start | bytes 442376 | tf_op jit(solution)/shard_map/ppermute | solution.py:296
  30.6 3.9 %collective-permute-start.10 = (f32[144,256]{1,0:T(8,128)S(1)}, f32[144,256]{1,0:T(8,128)S(1)}, u32[]{:S(2)}, u32[]{:S(2)}) collective-permute-start(f32[144,256]{1,0:T(8,128)S(1)} %get-tuple-element.41), channel_id=1, source_target_pairs={{0,8},{8,0},{16,24},{24,16},{1,9},{9,1},{17,25},{25,17},{2,10},{10... | collective-permute-start | bytes 442376 | tf_op jit(solution)/shard_map/ppermute | solution.py:296

commit v5 on v4

--- a/solution.py
+++ b/solution.py
@@ -31,8 +31,8 @@
 MESSAGE_ROWS = LATENT_ROWS + 120
 
 
-def select_kernel(tm, share, lat_ref, wide_ref):
-    channels = lat_ref.shape[2]
+def pick_kernel(tm, share, pick_ref):
+    channels = pick_ref.shape[0]
     me_dp, me_tm, me_rows = lax.axis_index("dp"), lax.axis_index("tm"), lax.axis_index("rows")
     col = lax.broadcasted_iota(jnp.int32, (1, channels), 1)
     inner = col % share
@@ -44,12 +44,15 @@
     rows = jnp.bitwise_xor(crossing, me_rows)
     wanted = ((dp * tm + (shift + me_tm) % tm) * 2 + rows) * share + inner
     row = lax.broadcasted_iota(jnp.int32, (channels, channels), 0)
-    pick = jnp.where(row == wanted, 1.0, 0.0).astype(jnp.bfloat16)
+    pick_ref[...] = jnp.where(row == wanted, 1.0, 0.0).astype(jnp.bfloat16)
+
+
+def message_kernel(tm, pick_ref, lat_ref, grad_ref, *refs):
+    outs, wide_ref = refs[:tm], refs[tm]
+    channels = pick_ref.shape[0]
+    lat = lat_ref[...].reshape(60, channels)
     wide_ref[56:64, :] = jnp.zeros((8, channels), jnp.float32)
-    wide_ref[0:60, :] = jnp.dot(lat_ref[...].reshape(60, channels), pick, preferred_element_type=jnp.float32)
-
-
-def message_kernel(tm, wide_ref, grad_ref, *outs):
+    wide_ref[0:60, :] = jnp.dot(lat, pick_ref[...], preferred_element_type=jnp.float32)
     grads = [grad_ref[f].reshape(120, grad_ref.shape[3]) for f in range(2)]
     for k in range(tm):
         for part in range(4):
@@ -242,21 +245,22 @@
     mine = jnp.transpose(grad_out[0], (0, 2, 1, 3))
     lat = jnp.transpose(latents[0, :, 0], (1, 0, 2))
     message = jax.ShapeDtypeStruct((2, MESSAGE_ROWS, outputs), jnp.bfloat16)
-    selected = pl.pallas_call(
-        functools.partial(select_kernel, tm, share),
-        out_shape=jax.ShapeDtypeStruct((64, channels), jnp.float32),
-        in_specs=whole(1),
+    pick = pl.pallas_call(
+        functools.partial(pick_kernel, tm, share),
+        out_shape=jax.ShapeDtypeStruct((channels, channels), jnp.bfloat16),
+        in_specs=[],
         out_specs=whole(1)[0],
         compiler_params=params(),
-        cost_estimate=pl.CostEstimate(flops=2**31, bytes_accessed=2**24, transcendentals=0),
-    )(lat)
+        cost_estimate=pl.CostEstimate(flops=2**33, bytes_accessed=2**24, transcendentals=0),
+    )()
     messages = pl.pallas_call(
         functools.partial(message_kernel, tm),
         out_shape=tuple([message] * tm),
-        in_specs=whole(2),
+        in_specs=whole(3),
         out_specs=tuple(whole(tm)),
-        compiler_params=params(),
-    )(selected, mine)
+        scratch_shapes=[pltpu.VMEM((64, channels), jnp.float32)],
+        compiler_params=params(),
+    )(pick, lat, mine)
     order = [0, tm - 1] + list(range(1, tm - 1))
     shifted = [lax.ppermute(messages[k], "tm", cycle(tm, k)) if k else messages[0] for k in order]
     across = [lax.ppermute(block, "rows", swap) for block in shifted]

time: 36.1 us -> 35.4 us (0.981)
  local copies, waits for them, and re-layouts: 2.17 us -> 1.46 us
    unnamed x9, local copies, waits for them, and re-layouts: 2.17 us -> 1.46 us
where the time goes in v5:
time: 35.4 us; the launch traced here: 35.3 us
  starting transfers between devices  14.5 us (41%)
  waiting for transfers between devices  9.87 us (28%)
  Pallas kernels  7.71 us (22%)
  local copies, waits for them, and re-layouts  1.46 us (4%)
  other arithmetic  0.95 us (3%)
  between operations  0.8 us (2%)
    ppermute x3, waiting for transfers between devices, narrow_body(): lax.ppermute(messages[k], 'tm', cycle(tm, k))  6.43 us
    ppermute x3, starting transfers between devices, narrow_body(): lax.ppermute(messages[k], 'tm', cycle(tm, k))  6.11 us
    ppermute x4, starting transfers between devices, narrow_body(): across = [lax.ppermute(block, 'rows', swap) for block in shifted]  6.08 us
    pallas_call x1, Pallas kernels, narrow_body(): pl.pallas_call(functools.partial(latents_kernel, tm), grid=(3,), out_shap...  3.11 us
    pallas_call x2, Pallas kernels, terms(): pl.pallas_call(functools.partial(terms_kernel, first, (0, 1, 2), frames,...  2.15 us
    ppermute x1, starting transfers between devices, narrow_body(): lax.ppermute(chip, 'dp', [(i, i ^ 2) for i in range(4)]).astype(jnp.float32)  1.56 us
    ppermute x4, waiting for transfers between devices, narrow_body(): across = [lax.ppermute(block, 'rows', swap) for block in shifted]  1.53 us
    unnamed x9, local copies, waits for them, and re-layouts  1.46 us
  transfers between devices with their start and end apart: 12, of which 6 were waited for; matrix products, arithmetic and copies ran while one was open for 2% of the time, Pallas kernels for 18%

profile of v5, /device:TPU:0, one launch (start us, length us, event | category | flops | bytes accessed | tf_op | source)
XLA Modules:
  0.0 35.3 jit_solution(18348258885421249798)
XLA Ops:
  0.6 0.0 copy-start
  0.6 0.0 copy-start.1
  0.6 0.1 shard_map.50.pick_ref
  0.8 0.8 %copy-done = bf16[1,2,2,60,256]{4,2,3,1,0:T(2,128)(2,1)S(1)} copy-done((bf16[1,2,2,60,256]{4,2,3,1,0:T(2,128)(2,1)S(1)}, bf16[1,2,2,60,256]{4,2,3,1,0:T(2,128)(2,1)}, u32[]{:S(2)}) %copy-start) | copy-done | bytes 122904
  1.5 0.0 copy-done.1
  1.5 0.2 shard_map.51
  1.7 5.1 %collective-permute-start.3 = (bf16[2,136,256]{2,1,0:T(8,128)(2,1)S(1)}, bf16[2,136,256]{2,1,0:T(8,128)(2,1)S(1)}, u32[]{:S(2)}, u32[]{:S(2)}) collective-permute-start(bf16[2,136,256]{2,1,0:T(8,128)(2,1)S(1)} %get-tuple-element.24), channel_id=1, source_target_pairs={{0,6},{2,0},{4,2},{6,4},{1,7},{3,1},{5,3},{7,5},{8,14},{10,8},{12,... | collective-permute-start | bytes 417800 | tf_op jit(solution)/shard_map/ppermute | solution.py:265
  6.9 0.0 collective-permute-start.5
  6.9 1.0 %collective-permute-start = (bf16[2,136,256]{2,1,0:T(8,128)(2,1)S(1)}, bf16[2,136,256]{2,1,0:T(8,128)(2,1)S(1)}, u32[]{:S(2)}, u32[]{:S(2)}) collective-permute-start(bf16[2,136,256]{2,1,0:T(8,128)(2,1)S(1)} %get-tuple-element.22), channel_id=1, source_target_pairs={{0,4},{2,6},{4,0},{6,2},{1,5},{3,7},{5,1},{7,3},{8,12},{10,14},{12... | collective-permute-start | bytes 417800 | tf_op jit(solution)/shard_map/ppermute | solution.py:265
  7.9 1.5 %collective-permute-start.2 = (bf16[2,136,256]{2,1,0:T(8,128)(2,1)S(1)}, bf16[2,136,256]{2,1,0:T(8,128)(2,1)S(1)}, u32[]{:S(2)}, u32[]{:S(2)}) collective-permute-start(bf16[2,136,256]{2,1,0:T(8,128)(2,1)S(1)} %get-tuple-element.34.refs_0_.own_ref), channel_id=1, source_target_pairs={{0,1},{1,0},{2,3},{3,2},{4,5},{5,4},{6,7},{7,6},{8,9},{9,8},{10,11... | collective-permute-start | bytes 417800 | tf_op jit(solution)/shard_map/ppermute | solution.py:266
  9.4 1.5 %collective-permute-done.3.refs_2_.next_ref = bf16[2,136,256]{2,1,0:T(8,128)(2,1)S(1)} collective-permute-done((bf16[2,136,256]{2,1,0:T(8,128)(2,1)S(1)}, bf16[2,136,256]{2,1,0:T(8,128)(2,1)S(1)}, u32[]{:S(2)}, u32[]{:S(2)}) %collective-permute-start.3) | collective-permute-done | bytes 139296 | tf_op jit(solution)/shard_map/ppermute | solution.py:265
  10.9 1.5 %collective-permute-start.4 = (bf16[2,136,256]{2,1,0:T(8,128)(2,1)S(1)}, bf16[2,136,256]{2,1,0:T(8,128)(2,1)S(1)}, u32[]{:S(2)}, u32[]{:S(2)}) collective-permute-start(bf16[2,136,256]{2,1,0:T(8,128)(2,1)S(1)} %collective-permute-done.3.refs_2_.next_ref), channel_id=1, source_target_pairs={{0,1},{1,0},{2,3},{3,2},{4,5},{5,4},{6,7},{7,6},{8,9},{9,8},{10,11... | collective-permute-start | bytes 417800 | tf_op jit(solution)/shard_map/ppermute | solution.py:266
  12.5 2.9 %collective-permute-done.5.refs_4_ = bf16[2,136,256]{2,1,0:T(8,128)(2,1)S(1)} collective-permute-done((bf16[2,136,256]{2,1,0:T(8,128)(2,1)S(1)}, bf16[2,136,256]{2,1,0:T(8,128)(2,1)S(1)}, u32[]{:S(2)}, u32[]{:S(2)}) %collective-permute-start.5) | collective-permute-done | bytes 139296 | tf_op jit(solution)/shard_map/ppermute | solution.py:265
  15.3 1.5 %collective-permute-start.6 = (bf16[2,136,256]{2,1,0:T(8,128)(2,1)S(1)}, bf16[2,136,256]{2,1,0:T(8,128)(2,1)S(1)}, u32[]{:S(2)}, u32[]{:S(2)}) collective-permute-start(bf16[2,136,256]{2,1,0:T(8,128)(2,1)S(1)} %collective-permute-done.5.refs_4_), channel_id=1, source_target_pairs={{0,1},{1,0},{2,3},{3,2},{4,5},{5,4},{6,7},{7,6},{8,9},{9,8},{10,11... | collective-permute-start | bytes 417800 | tf_op jit(solution)/shard_map/ppermute | solution.py:266
  16.8 2.0 %collective-permute-done.own_ref = bf16[2,136,256]{2,1,0:T(8,128)(2,1)S(1)} collective-permute-done((bf16[2,136,256]{2,1,0:T(8,128)(2,1)S(1)}, bf16[2,136,256]{2,1,0:T(8,128)(2,1)S(1)}, u32[]{:S(2)}, u32[]{:S(2)}) %collective-permute-start) | collective-permute-done | bytes 139296 | tf_op jit(solution)/shard_map/ppermute | solution.py:265
  18.9 1.5 %collective-permute-start.1 = (bf16[2,136,256]{2,1,0:T(8,128)(2,1)S(1)}, bf16[2,136,256]{2,1,0:T(8,128)(2,1)S(1)}, u32[]{:S(2)}, u32[]{:S(2)}) collective-permute-start(bf16[2,136,256]{2,1,0:T(8,128)(2,1)S(1)} %collective-permute-done.own_ref), channel_id=1, source_target_pairs={{0,1},{1,0},{2,3},{3,2},{4,5},{5,4},{6,7},{7,6},{8,9},{9,8},{10,11... | collective-permute-start | bytes 417800 | tf_op jit(solution)/shard_map/ppermute | solution.py:266
  20.4 0.0 collective-permute-done.2.refs_1_.other_ref
  20.4 0.0 collective-permute-done.4.refs_3_.next_other_ref
  20.4 0.0 collective-permute-done.6.refs_5_
  20.4 0.9 %shard_map.52 = (bf16[10,576,256]{2,1,0:T(8,128)(2,1)S(1)}, bf16[8,2,128,256]{3,2,1,0:T(8,128)(2,1)S(1)}, bf16[128,4608]{1,0:T(8,128)(2,1)S(1)}) custom-call(bf16[2,136,256]{2,1,0:T(8,128)(2,1)S(1)} %get-tuple-element.34.refs_0_.own_ref, bf16[2,136,256]{2,1,0:T(8,128)(2,1)S(1)} %collective-permute-done.2.refs_1_.other_ref, ...), custom_call_target="tpu_custom_call" | custom-call | flops 1 | bytes 1 | tf_op jit(solution)/shard_map/pallas_call | solution.py:276
  21.3 1.1 %shard_map.53 = (f32[432,256]{1,0:T(8,128)S(1)}, f32[432,256]{1,0:T(8,128)S(1)}) custom-call(bf16[10,576,256]{2,1,0:T(8,128)(2,1)S(1)} %get-tuple-element.26.win_ref.w_ref, bf16[8,2,128,256]{3,2,1,0:T(8,128)(2,1)S(1)} %get-tuple-element.27.grad_ref.g_ref), custom_call_target="tpu_custom_call" | custom-call | flops 1 | bytes 1 | tf_op jit(solution)/shard_map/pallas_call | solution.py:290
  22.4 1.5 %collective-permute-done.1.other_ref = bf16[2,136,256]{2,1,0:T(8,128)(2,1)S(1)} collective-permute-done((bf16[2,136,256]{2,1,0:T(8,128)(2,1)S(1)}, bf16[2,136,256]{2,1,0:T(8,128)(2,1)S(1)}, u32[]{:S(2)}, u32[]{:S(2)}) %collective-permute-start.1) | collective-permute-done | bytes 139296 | tf_op jit(solution)/shard_map/ppermute | solution.py:266
  23.9 0.0 slice-start
  23.9 0.7 %shard_map.54 = (bf16[10,576,256]{2,1,0:T(8,128)(2,1)S(1)}, bf16[8,2,128,256]{3,2,1,0:T(8,128)(2,1)S(1)}, bf16[128,4608]{1,0:T(8,128)(2,1)S(1)}, f32[432,256]{1,0:T(8,128)S(1)}) custom-call(bf16[2,136,256]{2,1,0:T(8,128)(2,1)S(1)} %collective-permute-done.own_ref, ...), custom_call_target="tpu_custom_call", output_to_operand_aliasing={{0}: (2, {}), {1}: (3, {}), {2}: (4, {})} | custom-call | flops 1 | bytes 1 | tf_op jit(solution)/shard_map/pallas_call | solution.py:303
  24.6 0.1 collective-permute-start.7
  24.7 0.0 slice-start.1
  24.7 0.4 %shard_map.55.keep_ref = f32[432,256]{1,0:T(8,128)S(1)} custom-call(bf16[10,576,256]{2,1,0:T(8,128)(2,1)S(1)} %get-tuple-element.35.win_ref, bf16[8,2,128,256]{3,2,1,0:T(8,128)(2,1)S(1)} %get-tuple-element.31.grad_ref, f32[432,256]{1,0:T(8,128)S(1)} %get-tuple-element.32.part_ref), custom_call_target="tpu_custom_call" | custom-call | flops 1 | bytes 1 | tf_op jit(solution)/shard_map/pallas_call | solution.py:313
  25.1 1.4 %collective-permute-done.7.received_ref = f32[432,256]{1,0:T(8,128)S(1)} collective-permute-done((f32[432,256]{1,0:T(8,128)S(1)}, f32[432,256]{1,0:T(8,128)S(1)}, u32[]{:S(2)}, u32[]{:S(2)}) %collective-permute-start.7) | collective-permute-done | bytes 442400 | tf_op jit(solution)/shard_map/ppermute | solution.py:300
  26.5 0.2 shard_map.56
  26.7 1.6 %collective-permute-start.11 = (f16[448,256]{1,0:T(8,128)(2,1)S(1)}, f16[448,256]{1,0:T(8,128)(2,1)S(1)}, u32[]{:S(2)}, u32[]{:S(2)}) collective-permute-start(f16[448,256]{1,0:T(8,128)(2,1)S(1)} %convert_element_type.6), channel_id=1, source_target_pairs={{0,16},{8,24},{16,0},{24,8},{1,17},{9,25},{17,1},{25,9},{2,18},{10... | collective-permute-start | bytes 688136 | tf_op jit(solution)/shard_map/ppermute | solution.py:330
  28.2 1.1 %shard_map.58 = (f32[144,256]{1,0:T(8,128)S(1)}, f32[144,256]{1,0:T(8,128)S(1)}, f32[144,256]{1,0:T(8,128)S(1)}, f32[144,256]{1,0:T(8,128)S(1)}, f32[144,256]{1,0:T(8,128)S(1)}, /*index=5*/f32[144,256]{1,0:T(8,128)S(1)}) custom-call(bf16[10,576,256]{2,1,0:T(8,128)(2,1)S(1)} %get-tuple-element.35.win_ref, bf16[8,2,128,256]{3,2,1,0:T(8,128)(2,1)S(1)} %get-tuple-element.31.grad_ref), custom_call_target="tpu_custom_call" | custom-call | flops 1 | bytes 1 | tf_op jit(solution)/shard_map/pallas_call | solution.py:290
  29.3 0.1 collective-permute-start.8
  29.4 0.5 %collective-permute-start.9 = (f32[144,256]{1,0:T(8,128)S(1)}, f32[144,256]{1,0:T(8,128)S(1)}, u32[]{:S(2)}, u32[]{:S(2)}) collective-permute-start(f32[144,256]{1,0:T(8,128)S(1)} %get-tuple-element.39), channel_id=1, source_target_pairs={{0,8},{8,0},{16,24},{24,16},{1,9},{9,1},{17,25},{25,17},{2,10},{10... | collective-permute-start | bytes 442376 | tf_op jit(solution)/shard_map/ppermute | solution.py:300
  29.9 0.1 collective-permute-start.10
  30.0 0.0 slice-done
  30.0 0.0 slice-done.1
  30.0 3.1 %shard_map.57 = bf16[2,30,512]{2,1,0:T(8,128)(2,1)S(1)} custom-call(bf16[2,136,256]{2,1,0:T(8,128)(2,1)S(1)} %get-tuple-element.34.refs_0_.own_ref, bf16[2,136,256]{2,1,0:T(8,128)(2,1)S(1)} %collective-permute-done.2.refs_1_.other_ref, bf16[2,136,256]{2,1,0:T(8,128)(2,1)S(1)} %collective-permute-done.3.refs_2_.next_ref, ...), custom_call_target="tpu_custom_call" | custom-call | flops 1 | bytes 1 | tf_op jit(solution)/shard_map/pallas_call | solution.py:334
  33.1 0.7 %copy.8 = bf16[1,2,1,30,512]{4,1,3,2,0:T(2,128)(2,1)} copy(bf16[1,2,1,30,512]{4,3,1,2,0:T(8,128)(2,1)S(1)} %bitcast.15) | data formatting | bytes 122880
  33.8 0.0 collective-permute-done.8
  33.8 0.0 collective-permute-done.9
  33.8 0.0 collective-permute-done.10
  33.9 0.5 %collective-permute-done.11 = f16[448,256]{1,0:T(8,128)(2,1)S(1)} collective-permute-done((f16[448,256]{1,0:T(8,128)(2,1)S(1)}, f16[448,256]{1,0:T(8,128)(2,1)S(1)}, u32[]{:S(2)}, u32[]{:S(2)}) %collective-permute-start.11) | collective-permute-done | bytes 229408 | tf_op jit(solution)/shard_map/ppermute | solution.py:330
  34.4 0.8 %fusion = f32[432,256]{1,0:T(8,128)} fusion(f32[448,256]{1,0:T(8,128)S(1)} %convert_element_type.7, f32[144,256]{1,0:T(8,128)S(1)} %add.14, f32[144,256]{1,0:T(8,128)S(1)} %add.13, f32[144,256]{1,0:T(8,128)S(1)} %add.12, f32[256]{0:T(256)S(1)} %bitcast.19), kind=kLoop, calls=%fused_computation.1 | loop fusion | flops 552960 | bytes 1328128 | tf_op jit(solution)/shard_map/add | solution.py:352
  (7 shorter events, 0.1 us)
Async XLA Ops:
  0.6 0.9 %copy-start = (bf16[1,2,2,60,256]{4,2,3,1,0:T(2,128)(2,1)S(1)}, bf16[1,2,2,60,256]{4,2,3,1,0:T(2,128)(2,1)}, u32[]{:S(2)}) copy-start(bf16[1,2,2,60,256]{4,2,3,1,0:T(2,128)(2,1)} %param.4) | copy-start | bytes 368644
  0.6 0.9 %copy-start.1 = (bf16[1,2,1,30,512]{4,1,3,2,0:T(2,128)(2,1)S(1)}, bf16[1,2,1,30,512]{4,1,3,2,0:T(2,128)(2,1)}, u32[]{:S(2)}) copy-start(bf16[1,2,1,30,512]{4,1,3,2,0:T(2,128)(2,1)} %param.3) | copy-start | bytes 184324
  1.7 9.2 %collective-permute-start.3 = (bf16[2,136,256]{2,1,0:T(8,128)(2,1)S(1)}, bf16[2,136,256]{2,1,0:T(8,128)(2,1)S(1)}, u32[]{:S(2)}, u32[]{:S(2)}) collective-permute-start(bf16[2,136,256]{2,1,0:T(8,128)(2,1)S(1)} %get-tuple-element.24), channel_id=1, source_target_pairs={{0,6},{2,0},{4,2},{6,4},{1,7},{3,1},{5,3},{7,5},{8,14},{10,8},{12,... | collective-permute-start | bytes 417800 | tf_op jit(solution)/shard_map/ppermute | solution.py:265
  6.9 8.5 %collective-permute-start.5 = (bf16[2,136,256]{2,1,0:T(8,128)(2,1)S(1)}, bf16[2,136,256]{2,1,0:T(8,128)(2,1)S(1)}, u32[]{:S(2)}, u32[]{:S(2)}) collective-permute-start(bf16[2,136,256]{2,1,0:T(8,128)(2,1)S(1)} %get-tuple-element.25), channel_id=1, source_target_pairs={{0,2},{2,4},{4,6},{6,0},{1,3},{3,5},{5,7},{7,1},{8,10},{10,12},{12... | collective-permute-start | bytes 417800 | tf_op jit(solution)/shard_map/ppermute | solution.py:265
  6.9 12.0 %collective-permute-start = (bf16[2,136,256]{2,1,0:T(8,128)(2,1)S(1)}, bf16[2,136,256]{2,1,0:T(8,128)(2,1)S(1)}, u32[]{:S(2)}, u32[]{:S(2)}) collective-permute-start(bf16[2,136,256]{2,1,0:T(8,128)(2,1)S(1)} %get-tuple-element.22), channel_id=1, source_target_pairs={{0,4},{2,6},{4,0},{6,2},{1,5},{3,7},{5,1},{7,3},{8,12},{10,14},{12... | collective-permute-start | bytes 417800 | tf_op jit(solution)/shard_map/ppermute | solution.py:265
  7.9 12.5 %collective-permute-start.2 = (bf16[2,136,256]{2,1,0:T(8,128)(2,1)S(1)}, bf16[2,136,256]{2,1,0:T(8,128)(2,1)S(1)}, u32[]{:S(2)}, u32[]{:S(2)}) collective-permute-start(bf16[2,136,256]{2,1,0:T(8,128)(2,1)S(1)} %get-tuple-element.34.refs_0_.own_ref), channel_id=1, source_target_pairs={{0,1},{1,0},{2,3},{3,2},{4,5},{5,4},{6,7},{7,6},{8,9},{9,8},{10,11... | collective-permute-start | bytes 417800 | tf_op jit(solution)/shard_map/ppermute | solution.py:266
  10.9 9.4 %collective-permute-start.4 = (bf16[2,136,256]{2,1,0:T(8,128)(2,1)S(1)}, bf16[2,136,256]{2,1,0:T(8,128)(2,1)S(1)}, u32[]{:S(2)}, u32[]{:S(2)}) collective-permute-start(bf16[2,136,256]{2,1,0:T(8,128)(2,1)S(1)} %collective-permute-done.3.refs_2_.next_ref), channel_id=1, source_target_pairs={{0,1},{1,0},{2,3},{3,2},{4,5},{5,4},{6,7},{7,6},{8,9},{9,8},{10,11... | collective-permute-start | bytes 417800 | tf_op jit(solution)/shard_map/ppermute | solution.py:266
  15.3 5.1 %collective-permute-start.6 = (bf16[2,136,256]{2,1,0:T(8,128)(2,1)S(1)}, bf16[2,136,256]{2,1,0:T(8,128)(2,1)S(1)}, u32[]{:S(2)}, u32[]{:S(2)}) collective-permute-start(bf16[2,136,256]{2,1,0:T(8,128)(2,1)S(1)} %collective-permute-done.5.refs_4_), channel_id=1, source_target_pairs={{0,1},{1,0},{2,3},{3,2},{4,5},{5,4},{6,7},{7,6},{8,9},{9,8},{10,11... | collective-permute-start | bytes 417800 | tf_op jit(solution)/shard_map/ppermute | solution.py:266
  18.9 5.1 %collective-permute-start.1 = (bf16[2,136,256]{2,1,0:T(8,128)(2,1)S(1)}, bf16[2,136,256]{2,1,0:T(8,128)(2,1)S(1)}, u32[]{:S(2)}, u32[]{:S(2)}) collective-permute-start(bf16[2,136,256]{2,1,0:T(8,128)(2,1)S(1)} %collective-permute-done.own_ref), channel_id=1, source_target_pairs={{0,1},{1,0},{2,3},{3,2},{4,5},{5,4},{6,7},{7,6},{8,9},{9,8},{10,11... | collective-permute-start | bytes 417800 | tf_op jit(solution)/shard_map/ppermute | solution.py:266
  23.9 6.1 %slice-start = ((s8[7077888]{0:T(1024)(128)(4,1)}), s8[4194304]{0:T(1024)(128)(4,1)S(1)}, s32[]{:S(2)}) async-start(s8[7077888]{0:T(1024)(128)(4,1)} %bitcast.12), calls=%async_computation | async-start | bytes 8388608
  24.6 1.9 %collective-permute-start.7 = (f32[432,256]{1,0:T(8,128)S(1)}, f32[432,256]{1,0:T(8,128)S(1)}, u32[]{:S(2)}, u32[]{:S(2)}) collective-permute-start(f32[432,256]{1,0:T(8,128)S(1)} %get-tuple-element.33), channel_id=1, source_target_pairs={{0,8},{8,0},{16,24},{24,16},{1,9},{9,1},{17,25},{25,17},{2,10},{10... | collective-permute-start | bytes 1327112 | tf_op jit(solution)/shard_map/ppermute | solution.py:300
  24.7 5.3 %slice-start.1 = ((s8[7077888]{0:T(1024)(128)(4,1)}), s8[2883584]{0:T(1024)(128)(4,1)S(1)}, s32[]{:S(2)}) async-start(s8[7077888]{0:T(1024)(128)(4,1)} %bitcast.12), calls=%async_computation.1 | async-start | bytes 5767168
  26.7 7.7 %collective-permute-start.11 = (f16[448,256]{1,0:T(8,128)(2,1)S(1)}, f16[448,256]{1,0:T(8,128)(2,1)S(1)}, u32[]{:S(2)}, u32[]{:S(2)}) collective-permute-start(f16[448,256]{1,0:T(8,128)(2,1)S(1)} %convert_element_type.6), channel_id=1, source_target_pairs={{0,16},{8,24},{16,0},{24,8},{1,17},{9,25},{17,1},{25,9},{2,18},{10... | collective-permute-start | bytes 688136 | tf_op jit(solution)/shard_map/ppermute | solution.py:330
  29.3 4.5 %collective-permute-start.8 = (f32[144,256]{1,0:T(8,128)S(1)}, f32[144,256]{1,0:T(8,128)S(1)}, u32[]{:S(2)}, u32[]{:S(2)}) collective-permute-start(f32[144,256]{1,0:T(8,128)S(1)} %get-tuple-element.37), channel_id=1, source_target_pairs={{0,8},{8,0},{16,24},{24,16},{1,9},{9,1},{17,25},{25,17},{2,10},{10... | collective-permute-start | bytes 442376 | tf_op jit(solution)/shard_map/ppermute | solution.py:300
  29.4 4.4 %collective-permute-start.9 = (f32[144,256]{1,0:T(8,128)S(1)}, f32[144,256]{1,0:T(8,128)S(1)}, u32[]{:S(2)}, u32[]{:S(2)}) collective-permute-start(f32[144,256]{1,0:T(8,128)S(1)} %get-tuple-element.39), channel_id=1, source_target_pairs={{0,8},{8,0},{16,24},{24,16},{1,9},{9,1},{17,25},{25,17},{2,10},{10... | collective-permute-start | bytes 442376 | tf_op jit(solution)/shard_map/ppermute | solution.py:300
  29.9 4.0 %collective-permute-start.10 = (f32[144,256]{1,0:T(8,128)S(1)}, f32[144,256]{1,0:T(8,128)S(1)}, u32[]{:S(2)}, u32[]{:S(2)}) collective-permute-start(f32[144,256]{1,0:T(8,128)S(1)} %get-tuple-element.41), channel_id=1, source_target_pairs={{0,8},{8,0},{16,24},{24,16},{1,9},{9,1},{17,25},{25,17},{2,10},{10... | collective-permute-start | bytes 442376 | tf_op jit(solution)/shard_map/ppermute | solution.py:300

commit v6 on v5

--- a/solution.py
+++ b/solution.py
@@ -163,7 +163,7 @@
 
 
 TOP_EXPONENT = 14
-EXPONENT_ROWS = 16
+EXPONENT_ROWS = 8
 
 
 def pack_kernel(keep_ref, received_ref, out_ref):

time: 35.4 us -> 35.3 us (level)
  transfers between devices with their start and end apart: 12 -> 12, of which waited for: 6 -> 6; matrix products, arithmetic and copies ran while one was open for 2% -> 2% of each run, Pallas kernels for 18% -> 19%
where the time goes in v6:
time: 35.3 us; the launch traced here: 35.2 us
  starting transfers between devices  14.5 us (41%)
  waiting for transfers between devices  9.77 us (28%)
  Pallas kernels  7.73 us (22%)
  local copies, waits for them, and re-layouts  1.46 us (4%)
  other arithmetic  0.98 us (3%)
  between operations  0.78 us (2%)
    ppermute x3, waiting for transfers between devices, narrow_body(): lax.ppermute(messages[k], 'tm', cycle(tm, k))  6.43 us
    ppermute x3, starting transfers between devices, narrow_body(): lax.ppermute(messages[k], 'tm', cycle(tm, k))  6.11 us
    ppermute x4, starting transfers between devices, narrow_body(): across = [lax.ppermute(block, 'rows', swap) for block in shifted]  6.08 us
    pallas_call x1, Pallas kernels, narrow_body(): pl.pallas_call(functools.partial(latents_kernel, tm), grid=(3,), out_shap...  3.1 us
    pallas_call x2, Pallas kernels, terms(): pl.pallas_call(functools.partial(terms_kernel, first, (0, 1, 2), frames,...  2.16 us
    ppermute x1, starting transfers between devices, narrow_body(): lax.ppermute(chip, 'dp', [(i, i ^ 2) for i in range(4)]).astype(jnp.float32)  1.56 us
    ppermute x4, waiting for transfers between devices, narrow_body(): across = [lax.ppermute(block, 'rows', swap) for block in shifted]  1.52 us
    unnamed x9, local copies, waits for them, and re-layouts  1.46 us
  transfers between devices with their start and end apart: 12, of which 6 were waited for; matrix products, arithmetic and copies ran while one was open for 2% of the time, Pallas kernels for 19%

profile of v6, /device:TPU:0, one launch (start us, length us, event | category | flops | bytes accessed | tf_op | source)
XLA Modules:
  0.0 35.2 jit_solution(17062911988459625660)
XLA Ops:
  0.6 0.0 copy-start
  0.6 0.0 copy-start.1
  0.6 0.1 shard_map.50.pick_ref
  0.8 0.8 %copy-done = bf16[1,2,2,60,256]{4,2,3,1,0:T(2,128)(2,1)S(1)} copy-done((bf16[1,2,2,60,256]{4,2,3,1,0:T(2,128)(2,1)S(1)}, bf16[1,2,2,60,256]{4,2,3,1,0:T(2,128)(2,1)}, u32[]{:S(2)}) %copy-start) | copy-done | bytes 122904
  1.5 0.0 copy-done.1
  1.5 0.2 shard_map.51
  1.7 5.1 %collective-permute-start.3 = (bf16[2,136,256]{2,1,0:T(8,128)(2,1)S(1)}, bf16[2,136,256]{2,1,0:T(8,128)(2,1)S(1)}, u32[]{:S(2)}, u32[]{:S(2)}) collective-permute-start(bf16[2,136,256]{2,1,0:T(8,128)(2,1)S(1)} %get-tuple-element.24), channel_id=1, source_target_pairs={{0,6},{2,0},{4,2},{6,4},{1,7},{3,1},{5,3},{7,5},{8,14},{10,8},{12,... | collective-permute-start | bytes 417800 | tf_op jit(solution)/shard_map/ppermute | solution.py:265
  6.9 0.0 collective-permute-start.5
  6.9 1.0 %collective-permute-start = (bf16[2,136,256]{2,1,0:T(8,128)(2,1)S(1)}, bf16[2,136,256]{2,1,0:T(8,128)(2,1)S(1)}, u32[]{:S(2)}, u32[]{:S(2)}) collective-permute-start(bf16[2,136,256]{2,1,0:T(8,128)(2,1)S(1)} %get-tuple-element.22), channel_id=1, source_target_pairs={{0,4},{2,6},{4,0},{6,2},{1,5},{3,7},{5,1},{7,3},{8,12},{10,14},{12... | collective-permute-start | bytes 417800 | tf_op jit(solution)/shard_map/ppermute | solution.py:265
  7.9 1.5 %collective-permute-start.2 = (bf16[2,136,256]{2,1,0:T(8,128)(2,1)S(1)}, bf16[2,136,256]{2,1,0:T(8,128)(2,1)S(1)}, u32[]{:S(2)}, u32[]{:S(2)}) collective-permute-start(bf16[2,136,256]{2,1,0:T(8,128)(2,1)S(1)} %get-tuple-element.34.refs_0_.own_ref), channel_id=1, source_target_pairs={{0,1},{1,0},{2,3},{3,2},{4,5},{5,4},{6,7},{7,6},{8,9},{9,8},{10,11... | collective-permute-start | bytes 417800 | tf_op jit(solution)/shard_map/ppermute | solution.py:266
  9.4 1.5 %collective-permute-done.3.refs_2_.next_ref = bf16[2,136,256]{2,1,0:T(8,128)(2,1)S(1)} collective-permute-done((bf16[2,136,256]{2,1,0:T(8,128)(2,1)S(1)}, bf16[2,136,256]{2,1,0:T(8,128)(2,1)S(1)}, u32[]{:S(2)}, u32[]{:S(2)}) %collective-permute-start.3) | collective-permute-done | bytes 139296 | tf_op jit(solution)/shard_map/ppermute | solution.py:265
  10.9 1.5 %collective-permute-start.4 = (bf16[2,136,256]{2,1,0:T(8,128)(2,1)S(1)}, bf16[2,136,256]{2,1,0:T(8,128)(2,1)S(1)}, u32[]{:S(2)}, u32[]{:S(2)}) collective-permute-start(bf16[2,136,256]{2,1,0:T(8,128)(2,1)S(1)} %collective-permute-done.3.refs_2_.next_ref), channel_id=1, source_target_pairs={{0,1},{1,0},{2,3},{3,2},{4,5},{5,4},{6,7},{7,6},{8,9},{9,8},{10,11... | collective-permute-start | bytes 417800 | tf_op jit(solution)/shard_map/ppermute | solution.py:266
  12.5 2.9 %collective-permute-done.5.refs_4_ = bf16[2,136,256]{2,1,0:T(8,128)(2,1)S(1)} collective-permute-done((bf16[2,136,256]{2,1,0:T(8,128)(2,1)S(1)}, bf16[2,136,256]{2,1,0:T(8,128)(2,1)S(1)}, u32[]{:S(2)}, u32[]{:S(2)}) %collective-permute-start.5) | collective-permute-done | bytes 139296 | tf_op jit(solution)/shard_map/ppermute | solution.py:265
  15.3 1.5 %collective-permute-start.6 = (bf16[2,136,256]{2,1,0:T(8,128)(2,1)S(1)}, bf16[2,136,256]{2,1,0:T(8,128)(2,1)S(1)}, u32[]{:S(2)}, u32[]{:S(2)}) collective-permute-start(bf16[2,136,256]{2,1,0:T(8,128)(2,1)S(1)} %collective-permute-done.5.refs_4_), channel_id=1, source_target_pairs={{0,1},{1,0},{2,3},{3,2},{4,5},{5,4},{6,7},{7,6},{8,9},{9,8},{10,11... | collective-permute-start | bytes 417800 | tf_op jit(solution)/shard_map/ppermute | solution.py:266
  16.8 2.0 %collective-permute-done.own_ref = bf16[2,136,256]{2,1,0:T(8,128)(2,1)S(1)} collective-permute-done((bf16[2,136,256]{2,1,0:T(8,128)(2,1)S(1)}, bf16[2,136,256]{2,1,0:T(8,128)(2,1)S(1)}, u32[]{:S(2)}, u32[]{:S(2)}) %collective-permute-start) | collective-permute-done | bytes 139296 | tf_op jit(solution)/shard_map/ppermute | solution.py:265
  18.9 1.5 %collective-permute-start.1 = (bf16[2,136,256]{2,1,0:T(8,128)(2,1)S(1)}, bf16[2,136,256]{2,1,0:T(8,128)(2,1)S(1)}, u32[]{:S(2)}, u32[]{:S(2)}) collective-permute-start(bf16[2,136,256]{2,1,0:T(8,128)(2,1)S(1)} %collective-permute-done.own_ref), channel_id=1, source_target_pairs={{0,1},{1,0},{2,3},{3,2},{4,5},{5,4},{6,7},{7,6},{8,9},{9,8},{10,11... | collective-permute-start | bytes 417800 | tf_op jit(solution)/shard_map/ppermute | solution.py:266
  20.4 0.0 collective-permute-done.2.refs_1_.other_ref
  20.4 0.0 collective-permute-done.4.refs_3_.next_other_ref
  20.4 0.0 collective-permute-done.6.refs_5_
  20.4 0.9 %shard_map.52 = (bf16[10,576,256]{2,1,0:T(8,128)(2,1)S(1)}, bf16[8,2,128,256]{3,2,1,0:T(8,128)(2,1)S(1)}, bf16[128,4608]{1,0:T(8,128)(2,1)S(1)}) custom-call(bf16[2,136,256]{2,1,0:T(8,128)(2,1)S(1)} %get-tuple-element.34.refs_0_.own_ref, bf16[2,136,256]{2,1,0:T(8,128)(2,1)S(1)} %collective-permute-done.2.refs_1_.other_ref, ...), custom_call_target="tpu_custom_call" | custom-call | flops 1 | bytes 1 | tf_op jit(solution)/shard_map/pallas_call | solution.py:276
  21.3 1.1 %shard_map.53 = (f32[432,256]{1,0:T(8,128)S(1)}, f32[432,256]{1,0:T(8,128)S(1)}) custom-call(bf16[10,576,256]{2,1,0:T(8,128)(2,1)S(1)} %get-tuple-element.26.win_ref.w_ref, bf16[8,2,128,256]{3,2,1,0:T(8,128)(2,1)S(1)} %get-tuple-element.27.grad_ref.g_ref), custom_call_target="tpu_custom_call" | custom-call | flops 1 | bytes 1 | tf_op jit(solution)/shard_map/pallas_call | solution.py:290
  22.4 1.5 %collective-permute-done.1.other_ref = bf16[2,136,256]{2,1,0:T(8,128)(2,1)S(1)} collective-permute-done((bf16[2,136,256]{2,1,0:T(8,128)(2,1)S(1)}, bf16[2,136,256]{2,1,0:T(8,128)(2,1)S(1)}, u32[]{:S(2)}, u32[]{:S(2)}) %collective-permute-start.1) | collective-permute-done | bytes 139296 | tf_op jit(solution)/shard_map/ppermute | solution.py:266
  23.9 0.0 slice-start
  23.9 0.7 %shard_map.54 = (bf16[10,576,256]{2,1,0:T(8,128)(2,1)S(1)}, bf16[8,2,128,256]{3,2,1,0:T(8,128)(2,1)S(1)}, bf16[128,4608]{1,0:T(8,128)(2,1)S(1)}, f32[432,256]{1,0:T(8,128)S(1)}) custom-call(bf16[2,136,256]{2,1,0:T(8,128)(2,1)S(1)} %collective-permute-done.own_ref, ...), custom_call_target="tpu_custom_call", output_to_operand_aliasing={{0}: (2, {}), {1}: (3, {}), {2}: (4, {})} | custom-call | flops 1 | bytes 1 | tf_op jit(solution)/shard_map/pallas_call | solution.py:303
  24.6 0.1 collective-permute-start.7
  24.7 0.0 slice-start.1
  24.7 0.4 %shard_map.55.keep_ref = f32[432,256]{1,0:T(8,128)S(1)} custom-call(bf16[10,576,256]{2,1,0:T(8,128)(2,1)S(1)} %get-tuple-element.35.win_ref, bf16[8,2,128,256]{3,2,1,0:T(8,128)(2,1)S(1)} %get-tuple-element.31.grad_ref, f32[432,256]{1,0:T(8,128)S(1)} %get-tuple-element.32.part_ref), custom_call_target="tpu_custom_call" | custom-call | flops 1 | bytes 1 | tf_op jit(solution)/shard_map/pallas_call | solution.py:313
  25.1 1.4 %collective-permute-done.7.received_ref = f32[432,256]{1,0:T(8,128)S(1)} collective-permute-done((f32[432,256]{1,0:T(8,128)S(1)}, f32[432,256]{1,0:T(8,128)S(1)}, u32[]{:S(2)}, u32[]{:S(2)}) %collective-permute-start.7) | collective-permute-done | bytes 442400 | tf_op jit(solution)/shard_map/ppermute | solution.py:300
  26.5 0.2 shard_map.56
  26.7 1.6 %collective-permute-start.11 = (f16[440,256]{1,0:T(8,128)(2,1)S(1)}, f16[440,256]{1,0:T(8,128)(2,1)S(1)}, u32[]{:S(2)}, u32[]{:S(2)}) collective-permute-start(f16[440,256]{1,0:T(8,128)(2,1)S(1)} %convert_element_type.6), channel_id=1, source_target_pairs={{0,16},{8,24},{16,0},{24,8},{1,17},{9,25},{17,1},{25,9},{2,18},{10... | collective-permute-start | bytes 675848 | tf_op jit(solution)/shard_map/ppermute | solution.py:330
  28.2 1.1 %shard_map.58 = (f32[144,256]{1,0:T(8,128)S(1)}, f32[144,256]{1,0:T(8,128)S(1)}, f32[144,256]{1,0:T(8,128)S(1)}, f32[144,256]{1,0:T(8,128)S(1)}, f32[144,256]{1,0:T(8,128)S(1)}, /*index=5*/f32[144,256]{1,0:T(8,128)S(1)}) custom-call(bf16[10,576,256]{2,1,0:T(8,128)(2,1)S(1)} %get-tuple-element.35.win_ref, bf16[8,2,128,256]{3,2,1,0:T(8,128)(2,1)S(1)} %get-tuple-element.31.grad_ref), custom_call_target="tpu_custom_call" | custom-call | flops 1 | bytes 1 | tf_op jit(solution)/shard_map/pallas_call | solution.py:290
  29.3 0.1 collective-permute-start.8
  29.4 0.5 %collective-permute-start.9 = (f32[144,256]{1,0:T(8,128)S(1)}, f32[144,256]{1,0:T(8,128)S(1)}, u32[]{:S(2)}, u32[]{:S(2)}) collective-permute-start(f32[144,256]{1,0:T(8,128)S(1)} %get-tuple-element.39), channel_id=1, source_target_pairs={{0,8},{8,0},{16,24},{24,16},{1,9},{9,1},{17,25},{25,17},{2,10},{10... | collective-permute-start | bytes 442376 | tf_op jit(solution)/shard_map/ppermute | solution.py:300
  29.9 0.1 collective-permute-start.10
  30.0 0.0 slice-done
  30.0 0.0 slice-done.1
  30.0 3.1 %shard_map.57 = bf16[2,30,512]{2,1,0:T(8,128)(2,1)S(1)} custom-call(bf16[2,136,256]{2,1,0:T(8,128)(2,1)S(1)} %get-tuple-element.34.refs_0_.own_ref, bf16[2,136,256]{2,1,0:T(8,128)(2,1)S(1)} %collective-permute-done.2.refs_1_.other_ref, bf16[2,136,256]{2,1,0:T(8,128)(2,1)S(1)} %collective-permute-done.3.refs_2_.next_ref, ...), custom_call_target="tpu_custom_call" | custom-call | flops 1 | bytes 1 | tf_op jit(solution)/shard_map/pallas_call | solution.py:334
  33.1 0.7 %copy.8 = bf16[1,2,1,30,512]{4,1,3,2,0:T(2,128)(2,1)} copy(bf16[1,2,1,30,512]{4,3,1,2,0:T(8,128)(2,1)S(1)} %bitcast.15) | data formatting | bytes 122880
  33.8 0.0 collective-permute-done.8
  33.8 0.0 collective-permute-done.9
  33.9 0.0 collective-permute-done.10
  33.9 0.4 %collective-permute-done.11 = f16[440,256]{1,0:T(8,128)(2,1)S(1)} collective-permute-done((f16[440,256]{1,0:T(8,128)(2,1)S(1)}, f16[440,256]{1,0:T(8,128)(2,1)S(1)}, u32[]{:S(2)}, u32[]{:S(2)}) %collective-permute-start.11) | collective-permute-done | bytes 225312 | tf_op jit(solution)/shard_map/ppermute | solution.py:330
  34.4 0.8 %fusion = f32[432,256]{1,0:T(8,128)} fusion(f32[440,256]{1,0:T(8,128)S(1)} %convert_element_type.7, f32[144,256]{1,0:T(8,128)S(1)} %add.14, f32[144,256]{1,0:T(8,128)S(1)} %add.13, f32[144,256]{1,0:T(8,128)S(1)} %add.12, f32[256]{0:T(256)S(1)} %bitcast.19), kind=kLoop, calls=%fused_computation.1 | loop fusion | flops 552960 | bytes 1328128 | tf_op jit(solution)/shard_map/add | solution.py:352
  (7 shorter events, 0.1 us)
Async XLA Ops:
  0.6 0.9 %copy-start = (bf16[1,2,2,60,256]{4,2,3,1,0:T(2,128)(2,1)S(1)}, bf16[1,2,2,60,256]{4,2,3,1,0:T(2,128)(2,1)}, u32[]{:S(2)}) copy-start(bf16[1,2,2,60,256]{4,2,3,1,0:T(2,128)(2,1)} %param.4) | copy-start | bytes 368644
  0.6 0.9 %copy-start.1 = (bf16[1,2,1,30,512]{4,1,3,2,0:T(2,128)(2,1)S(1)}, bf16[1,2,1,30,512]{4,1,3,2,0:T(2,128)(2,1)}, u32[]{:S(2)}) copy-start(bf16[1,2,1,30,512]{4,1,3,2,0:T(2,128)(2,1)} %param.3) | copy-start | bytes 184324
  1.7 9.2 %collective-permute-start.3 = (bf16[2,136,256]{2,1,0:T(8,128)(2,1)S(1)}, bf16[2,136,256]{2,1,0:T(8,128)(2,1)S(1)}, u32[]{:S(2)}, u32[]{:S(2)}) collective-permute-start(bf16[2,136,256]{2,1,0:T(8,128)(2,1)S(1)} %get-tuple-element.24), channel_id=1, source_target_pairs={{0,6},{2,0},{4,2},{6,4},{1,7},{3,1},{5,3},{7,5},{8,14},{10,8},{12,... | collective-permute-start | bytes 417800 | tf_op jit(solution)/shard_map/ppermute | solution.py:265
  6.9 8.5 %collective-permute-start.5 = (bf16[2,136,256]{2,1,0:T(8,128)(2,1)S(1)}, bf16[2,136,256]{2,1,0:T(8,128)(2,1)S(1)}, u32[]{:S(2)}, u32[]{:S(2)}) collective-permute-start(bf16[2,136,256]{2,1,0:T(8,128)(2,1)S(1)} %get-tuple-element.25), channel_id=1, source_target_pairs={{0,2},{2,4},{4,6},{6,0},{1,3},{3,5},{5,7},{7,1},{8,10},{10,12},{12... | collective-permute-start | bytes 417800 | tf_op jit(solution)/shard_map/ppermute | solution.py:265
  6.9 12.0 %collective-permute-start = (bf16[2,136,256]{2,1,0:T(8,128)(2,1)S(1)}, bf16[2,136,256]{2,1,0:T(8,128)(2,1)S(1)}, u32[]{:S(2)}, u32[]{:S(2)}) collective-permute-start(bf16[2,136,256]{2,1,0:T(8,128)(2,1)S(1)} %get-tuple-element.22), channel_id=1, source_target_pairs={{0,4},{2,6},{4,0},{6,2},{1,5},{3,7},{5,1},{7,3},{8,12},{10,14},{12... | collective-permute-start | bytes 417800 | tf_op jit(solution)/shard_map/ppermute | solution.py:265
  7.9 12.5 %collective-permute-start.2 = (bf16[2,136,256]{2,1,0:T(8,128)(2,1)S(1)}, bf16[2,136,256]{2,1,0:T(8,128)(2,1)S(1)}, u32[]{:S(2)}, u32[]{:S(2)}) collective-permute-start(bf16[2,136,256]{2,1,0:T(8,128)(2,1)S(1)} %get-tuple-element.34.refs_0_.own_ref), channel_id=1, source_target_pairs={{0,1},{1,0},{2,3},{3,2},{4,5},{5,4},{6,7},{7,6},{8,9},{9,8},{10,11... | collective-permute-start | bytes 417800 | tf_op jit(solution)/shard_map/ppermute | solution.py:266
  10.9 9.4 %collective-permute-start.4 = (bf16[2,136,256]{2,1,0:T(8,128)(2,1)S(1)}, bf16[2,136,256]{2,1,0:T(8,128)(2,1)S(1)}, u32[]{:S(2)}, u32[]{:S(2)}) collective-permute-start(bf16[2,136,256]{2,1,0:T(8,128)(2,1)S(1)} %collective-permute-done.3.refs_2_.next_ref), channel_id=1, source_target_pairs={{0,1},{1,0},{2,3},{3,2},{4,5},{5,4},{6,7},{7,6},{8,9},{9,8},{10,11... | collective-permute-start | bytes 417800 | tf_op jit(solution)/shard_map/ppermute | solution.py:266
  15.3 5.1 %collective-permute-start.6 = (bf16[2,136,256]{2,1,0:T(8,128)(2,1)S(1)}, bf16[2,136,256]{2,1,0:T(8,128)(2,1)S(1)}, u32[]{:S(2)}, u32[]{:S(2)}) collective-permute-start(bf16[2,136,256]{2,1,0:T(8,128)(2,1)S(1)} %collective-permute-done.5.refs_4_), channel_id=1, source_target_pairs={{0,1},{1,0},{2,3},{3,2},{4,5},{5,4},{6,7},{7,6},{8,9},{9,8},{10,11... | collective-permute-start | bytes 417800 | tf_op jit(solution)/shard_map/ppermute | solution.py:266
  18.9 5.1 %collective-permute-start.1 = (bf16[2,136,256]{2,1,0:T(8,128)(2,1)S(1)}, bf16[2,136,256]{2,1,0:T(8,128)(2,1)S(1)}, u32[]{:S(2)}, u32[]{:S(2)}) collective-permute-start(bf16[2,136,256]{2,1,0:T(8,128)(2,1)S(1)} %collective-permute-done.own_ref), channel_id=1, source_target_pairs={{0,1},{1,0},{2,3},{3,2},{4,5},{5,4},{6,7},{7,6},{8,9},{9,8},{10,11... | collective-permute-start | bytes 417800 | tf_op jit(solution)/shard_map/ppermute | solution.py:266
  23.9 6.1 %slice-start = ((s8[7077888]{0:T(1024)(128)(4,1)}), s8[4194304]{0:T(1024)(128)(4,1)S(1)}, s32[]{:S(2)}) async-start(s8[7077888]{0:T(1024)(128)(4,1)} %bitcast.12), calls=%async_computation | async-start | bytes 8388608
  24.6 1.9 %collective-permute-start.7 = (f32[432,256]{1,0:T(8,128)S(1)}, f32[432,256]{1,0:T(8,128)S(1)}, u32[]{:S(2)}, u32[]{:S(2)}) collective-permute-start(f32[432,256]{1,0:T(8,128)S(1)} %get-tuple-element.33), channel_id=1, source_target_pairs={{0,8},{8,0},{16,24},{24,16},{1,9},{9,1},{17,25},{25,17},{2,10},{10... | collective-permute-start | bytes 1327112 | tf_op jit(solution)/shard_map/ppermute | solution.py:300
  24.7 5.3 %slice-start.1 = ((s8[7077888]{0:T(1024)(128)(4,1)}), s8[2883584]{0:T(1024)(128)(4,1)S(1)}, s32[]{:S(2)}) async-start(s8[7077888]{0:T(1024)(128)(4,1)} %bitcast.12), calls=%async_computation.1 | async-start | bytes 5767168
  26.7 7.6 %collective-permute-start.11 = (f16[440,256]{1,0:T(8,128)(2,1)S(1)}, f16[440,256]{1,0:T(8,128)(2,1)S(1)}, u32[]{:S(2)}, u32[]{:S(2)}) collective-permute-start(f16[440,256]{1,0:T(8,128)(2,1)S(1)} %convert_element_type.6), channel_id=1, source_target_pairs={{0,16},{8,24},{16,0},{24,8},{1,17},{9,25},{17,1},{25,9},{2,18},{10... | collective-permute-start | bytes 675848 | tf_op jit(solution)/shard_map/ppermute | solution.py:330
  29.3 4.5 %collective-permute-start.8 = (f32[144,256]{1,0:T(8,128)S(1)}, f32[144,256]{1,0:T(8,128)S(1)}, u32[]{:S(2)}, u32[]{:S(2)}) collective-permute-start(f32[144,256]{1,0:T(8,128)S(1)} %get-tuple-element.37), channel_id=1, source_target_pairs={{0,8},{8,0},{16,24},{24,16},{1,9},{9,1},{17,25},{25,17},{2,10},{10... | collective-permute-start | bytes 442376 | tf_op jit(solution)/shard_map/ppermute | solution.py:300
  29.4 4.4 %collective-permute-start.9 = (f32[144,256]{1,0:T(8,128)S(1)}, f32[144,256]{1,0:T(8,128)S(1)}, u32[]{:S(2)}, u32[]{:S(2)}) collective-permute-start(f32[144,256]{1,0:T(8,128)S(1)} %get-tuple-element.39), channel_id=1, source_target_pairs={{0,8},{8,0},{16,24},{24,16},{1,9},{9,1},{17,25},{25,17},{2,10},{10... | collective-permute-start | bytes 442376 | tf_op jit(solution)/shard_map/ppermute | solution.py:300
  29.9 3.9 %collective-permute-start.10 = (f32[144,256]{1,0:T(8,128)S(1)}, f32[144,256]{1,0:T(8,128)S(1)}, u32[]{:S(2)}, u32[]{:S(2)}) collective-permute-start(f32[144,256]{1,0:T(8,128)S(1)} %get-tuple-element.41), channel_id=1, source_target_pairs={{0,8},{8,0},{16,24},{24,16},{1,9},{9,1},{17,25},{25,17},{2,10},{10... | collective-permute-start | bytes 442376 | tf_op jit(solution)/shard_map/ppermute | solution.py:300
